TPU v7x, 32 devices: a whole 2x2x4 slice. The times are simulated.
32 devices in a mesh: dp: 16 (over z, y, core), tensor: 2 (over x).
Axes of the slice: x: 2, y: 2, z: 4, core: 2. Of those that a mesh axis runs over, the one named last changes fastest.
Arguments:
- tokens: bfloat16 [64, 576, 1024], P('dp', 'tensor'), may hold values from -6 to 6
- image_mask: int32 [64], P('dp'), may hold values 0 or 1
- out_grad: bfloat16 [64, 576, 1024], P('dp', 'tensor'), may hold values from -6 to 6
- norm1_gain: bfloat16 [1024], replicated, may hold values from 0.5 to 1.5
- norm1_shift: bfloat16 [1024], replicated, may hold values from -3 to 3
- qkv_weight: bfloat16 [1024, 3, 1024], P('dp', None, 'tensor'), may hold values from -0.1875 to 0.1875
- qv_bias: bfloat16 [2, 1024], P(None, 'tensor'), may hold values from -3 to 3
- out_weight: bfloat16 [1024, 1024], P('dp', 'tensor'), may hold values from -1.5 to 1.5
- out_bias: bfloat16 [1024], replicated, may hold values from -3 to 3
- norm2_gain: bfloat16 [1024], replicated, may hold values from 0.5 to 1.5
- norm2_shift: bfloat16 [1024], replicated, may hold values from -3 to 3
- up_weight: bfloat16 [1024, 4096], P('dp', 'tensor'), may hold values from -0.1875 to 0.1875
- up_bias: bfloat16 [4096], P('tensor'), may hold values from -3 to 3
- down_weight: bfloat16 [1024, 4096], P('dp', 'tensor'), may hold values from -0.09375 to 0.09375
- down_bias: bfloat16 [1024], replicated, may hold values from -3 to 3
Outputs:
- block_out: bfloat16 [64, 576, 1024], P('dp', 'tensor')
- tokens_grad: bfloat16 [64, 576, 1024], P('dp', 'tensor')
- norm1_gain_grad: float32 [1024], replicated
- norm1_shift_grad: float32 [1024], replicated
- qkv_weight_grad: float32 [1024, 3, 1024], P('dp', None, 'tensor')
- qv_bias_grad: float32 [2, 1024], P(None, 'tensor')
- out_weight_grad: float32 [1024, 1024], P('dp', 'tensor')
- out_bias_grad: float32 [1024], replicated
- norm2_gain_grad: float32 [1024], replicated
- norm2_shift_grad: float32 [1024], replicated
- up_weight_grad: float32 [1024, 4096], P('dp', 'tensor')
- up_bias_grad: float32 [4096], P('tensor')
- down_weight_grad: float32 [1024, 4096], P('dp', 'tensor')
- down_bias_grad: float32 [1024], replicated
Inputs may be any that keep to these rules, and one draw needn't show every extreme that they name: `image_mask`: 1 marks a real image, 0 a padding image.
All inputs are finite; a program needn't handle non-finite values. No bound on the sum of `image_mask` on one device may be relied on, other than what follows from the above.
Results may differ from a plain program's by a relative error of at most 0.015.
Values may be sent and summed in bfloat16 or wider, within the bound.
No kernel may reach another device: no remote copies, remote signals or barrier semaphores. Data moves between devices by JAX's collectives and lax.ppermute only.
A program may use at most 320 MiB of HBM per device.

v0:
```python
import jax
import jax.numpy as jnp
from jax import lax
from jax.sharding import PartitionSpec as P

HDIM = 64
MICRO = 2


def mixed(form, left, right):
    return jnp.einsum(form, left, right, preferred_element_type=jnp.float32)


def normalize(values, gain, shift):
    mean_val = jnp.mean(values, axis=-1, keepdims=True)
    centered = values - mean_val
    inv_std = lax.rsqrt(jnp.mean(centered * centered, axis=-1, keepdims=True) + 1e-05)
    unit_val = centered * inv_std
    return (unit_val * gain + shift, unit_val, inv_std)


def normalize_back(grad_in, unit_val, inv_std, gain):
    scaled = grad_in * gain
    return inv_std * (
        scaled
        - jnp.mean(scaled, axis=-1, keepdims=True)
        - unit_val * jnp.mean(scaled * unit_val, axis=-1, keepdims=True)
    )


def token_sum(values):
    return jnp.sum(values, axis=(0, 1))


def shards(
    tokens,
    image_mask,
    out_grad,
    norm1_gain,
    norm1_shift,
    qkv_weight,
    qv_bias,
    out_weight,
    out_bias,
    norm2_gain,
    norm2_shift,
    up_weight,
    up_bias,
    down_weight,
    down_bias,
):
    images_here = tokens.shape[0] // MICRO
    full_width = norm1_gain.shape[0]
    local_width = qkv_weight.shape[2]
    local_hidden = up_weight.shape[1]
    local_heads = local_width // HDIM
    score_scale = HDIM ** (-0.5)
    gain_one = norm1_gain.astype(jnp.float32)
    shift_one = norm1_shift.astype(jnp.float32)
    gain_two = norm2_gain.astype(jnp.float32)
    shift_two = norm2_shift.astype(jnp.float32)
    bias_pair = qv_bias.astype(jnp.float32)
    grad_qkv = jnp.zeros((full_width, 3, local_width), jnp.float32)
    grad_out = jnp.zeros((full_width, local_width), jnp.float32)
    grad_up = jnp.zeros((full_width, local_hidden), jnp.float32)
    grad_down = jnp.zeros((full_width, local_hidden), jnp.float32)
    grad_gain_one = jnp.zeros((full_width,), jnp.float32)
    grad_shift_one = jnp.zeros((full_width,), jnp.float32)
    grad_gain_two = jnp.zeros((full_width,), jnp.float32)
    grad_shift_two = jnp.zeros((full_width,), jnp.float32)
    grad_out_bias = jnp.zeros((full_width,), jnp.float32)
    grad_down_bias = jnp.zeros((full_width,), jnp.float32)
    grad_pair = jnp.zeros((2, local_width), jnp.float32)
    grad_up_bias = jnp.zeros((local_hidden,), jnp.float32)
    outputs = []
    input_grads = []
    for micro_index in range(MICRO):
        first_image = micro_index * images_here
        block_rows = tokens[first_image : first_image + images_here].astype(jnp.float32)
        keep_mask = image_mask[first_image : first_image + images_here].astype(jnp.float32)[
            :, None, None
        ]
        fwd_weights = (
            lax.all_gather(qkv_weight, "dp", axis=0, tiled=True),
            lax.all_gather(out_weight, "dp", axis=0, tiled=True),
            lax.all_gather(up_weight, "dp", axis=0, tiled=True),
            lax.all_gather(down_weight, "dp", axis=0, tiled=True),
        )
        qkv_full, out_full, up_full, down_full = fwd_weights
        normed, unit_one, inv_one = normalize(block_rows, gain_one, shift_one)
        normed_full = lax.all_gather(normed.astype(jnp.bfloat16), "tensor", axis=1, tiled=True)
        seq_len = normed_full.shape[1]
        head_shape = (images_here, seq_len, local_heads, HDIM)
        projected = mixed("isd,dcf->iscf", normed_full, qkv_full)
        queries = (projected[:, :, 0] + bias_pair[0]).astype(jnp.bfloat16).reshape(head_shape)
        key_rows = projected[:, :, 1].astype(jnp.bfloat16).reshape(head_shape)
        value_rows = (projected[:, :, 2] + bias_pair[1]).astype(jnp.bfloat16).reshape(head_shape)
        scores = mixed("iqhe,ikhe->ihqk", queries, key_rows) * score_scale
        row_top = jnp.max(scores, axis=-1, keepdims=True)
        raw_weights = jnp.exp(scores - row_top)
        row_total = jnp.sum(raw_weights, axis=-1, keepdims=True)
        log_total = row_top + jnp.log(row_total)
        probs = (raw_weights / row_total).astype(jnp.bfloat16)
        context = mixed("ihqk,ikhe->iqhe", probs, value_rows).astype(jnp.bfloat16)
        context = context.reshape(images_here, seq_len, local_width)
        attn_terms = mixed("isf,of->iso", context, out_full)
        branch = lax.psum_scatter(
            attn_terms, "tensor", scatter_dimension=1, tiled=True
        ) + out_bias.astype(jnp.float32)
        middle = block_rows + branch
        second, unit_two, inv_two = normalize(middle, gain_two, shift_two)
        second_full = lax.all_gather(second.astype(jnp.bfloat16), "tensor", axis=1, tiled=True)
        hidden = mixed("isd,df->isf", second_full, up_full) + up_bias.astype(jnp.float32)
        gate_sig = jax.nn.sigmoid(1.702 * hidden)
        active = (hidden * gate_sig).astype(jnp.bfloat16)
        feed_terms = mixed("isf,of->iso", active, down_full)
        feed_out = lax.psum_scatter(
            feed_terms.astype(jnp.bfloat16), "tensor", scatter_dimension=1, tiled=True
        ).astype(jnp.float32) + down_bias.astype(jnp.float32)
        outputs.append(((middle + feed_out) * keep_mask).astype(jnp.bfloat16))
        back_weights = (
            lax.all_gather(qkv_weight, "dp", axis=0, tiled=True),
            lax.all_gather(out_weight, "dp", axis=0, tiled=True),
            lax.all_gather(up_weight, "dp", axis=0, tiled=True),
            lax.all_gather(down_weight, "dp", axis=0, tiled=True),
        )
        qkv_back, out_back, up_back, down_back = back_weights
        grad_final = (
            out_grad[first_image : first_image + images_here].astype(jnp.float32) * keep_mask
        )
        grad_down_bias = grad_down_bias + token_sum(grad_final)
        final_full = lax.all_gather(grad_final.astype(jnp.bfloat16), "tensor", axis=1, tiled=True)
        grad_down = grad_down + mixed("iso,isf->of", final_full, active)
        grad_active = mixed("iso,of->isf", final_full, down_back)
        grad_hidden = (
            grad_active * (gate_sig + 1.702 * hidden * gate_sig * (1.0 - gate_sig))
        ).astype(jnp.bfloat16)
        grad_up_bias = grad_up_bias + token_sum(grad_hidden.astype(jnp.float32))
        grad_up = grad_up + mixed("isd,isf->df", second_full, grad_hidden)
        second_terms = mixed("isf,df->isd", grad_hidden, up_back)
        grad_second = lax.psum_scatter(second_terms, "tensor", scatter_dimension=1, tiled=True)
        grad_gain_two = grad_gain_two + token_sum(grad_second * unit_two)
        grad_shift_two = grad_shift_two + token_sum(grad_second)
        grad_middle = grad_final + normalize_back(grad_second, unit_two, inv_two, gain_two)
        grad_branch = grad_middle.astype(jnp.bfloat16)
        grad_out_bias = grad_out_bias + token_sum(grad_branch.astype(jnp.float32))
        branch_full = lax.all_gather(grad_branch, "tensor", axis=1, tiled=True)
        grad_out = grad_out + mixed("iso,isf->of", branch_full, context)
        grad_context = (
            mixed("iso,of->isf", branch_full, out_back).astype(jnp.bfloat16).reshape(head_shape)
        )
        again = mixed("iqhe,ikhe->ihqk", queries, key_rows) * score_scale
        soft_again = jnp.exp(again - log_total)
        probs_again = soft_again.astype(jnp.bfloat16)
        grad_values = mixed("ihqk,iqhe->ikhe", probs_again, grad_context)
        grad_soft = mixed("iqhe,ikhe->ihqk", grad_context, value_rows)
        grad_scores = (
            soft_again * (grad_soft - jnp.sum(grad_soft * soft_again, axis=-1, keepdims=True))
        ).astype(jnp.bfloat16)
        grad_queries = mixed("ihqk,ikhe->iqhe", grad_scores, key_rows) * score_scale
        grad_keys = mixed("ihqk,iqhe->ikhe", grad_scores, queries) * score_scale
        flat_shape = (images_here, seq_len, local_width)
        grad_projected = jnp.stack(
            (
                grad_queries.reshape(flat_shape),
                grad_keys.reshape(flat_shape),
                grad_values.reshape(flat_shape),
            ),
            axis=2,
        ).astype(jnp.bfloat16)
        pair_terms = grad_projected.astype(jnp.float32)
        grad_pair = grad_pair + jnp.stack(
            (token_sum(pair_terms[:, :, 0]), token_sum(pair_terms[:, :, 2])), axis=0
        )
        grad_qkv = grad_qkv + mixed("isd,iscf->dcf", normed_full, grad_projected)
        normed_terms = mixed("iscf,dcf->isd", grad_projected, qkv_back)
        grad_normed = lax.psum_scatter(
            normed_terms.astype(jnp.bfloat16), "tensor", scatter_dimension=1, tiled=True
        ).astype(jnp.float32)
        grad_gain_one = grad_gain_one + token_sum(grad_normed * unit_one)
        grad_shift_one = grad_shift_one + token_sum(grad_normed)
        grad_tokens = grad_middle + normalize_back(grad_normed, unit_one, inv_one, gain_one)
        input_grads.append(grad_tokens.astype(jnp.bfloat16))
    grad_qkv, grad_out, grad_up, grad_down = (
        lax.psum_scatter(
            grad_qkv.astype(jnp.bfloat16), "dp", scatter_dimension=0, tiled=True
        ).astype(jnp.float32),
        lax.psum_scatter(
            grad_out.astype(jnp.bfloat16), "dp", scatter_dimension=0, tiled=True
        ).astype(jnp.float32),
        lax.psum_scatter(
            grad_up.astype(jnp.bfloat16), "dp", scatter_dimension=0, tiled=True
        ).astype(jnp.float32),
        lax.psum_scatter(
            grad_down.astype(jnp.bfloat16), "dp", scatter_dimension=0, tiled=True
        ).astype(jnp.float32),
    )
    grad_gain_one, grad_shift_one, grad_gain_two, grad_shift_two, grad_out_bias, grad_down_bias = (
        lax.psum(
            (
                grad_gain_one,
                grad_shift_one,
                grad_gain_two,
                grad_shift_two,
                grad_out_bias,
                grad_down_bias,
            ),
            ("dp", "tensor"),
        )
    )
    grad_pair, grad_up_bias = lax.psum((grad_pair, grad_up_bias), "dp")
    block_out = jnp.concatenate(outputs, axis=0)
    tokens_grad = jnp.concatenate(input_grads, axis=0)
    return (
        block_out,
        tokens_grad,
        grad_gain_one,
        grad_shift_one,
        grad_qkv,
        grad_pair,
        grad_out,
        grad_out_bias,
        grad_gain_two,
        grad_shift_two,
        grad_up,
        grad_up_bias,
        grad_down,
        grad_down_bias,
    )


def solution(mesh):
    in_specs = (
        P("dp", "tensor", None),
        P("dp"),
        P("dp", "tensor", None),
        P(),
        P(),
        P("dp", None, "tensor"),
        P(None, "tensor"),
        P("dp", "tensor"),
        P(),
        P(),
        P(),
        P("dp", "tensor"),
        P("tensor"),
        P("dp", "tensor"),
        P(),
    )
    out_specs = (
        P("dp", "tensor", None),
        P("dp", "tensor", None),
        P(),
        P(),
        P("dp", None, "tensor"),
        P(None, "tensor"),
        P("dp", "tensor"),
        P(),
        P(),
        P(),
        P("dp", "tensor"),
        P("tensor"),
        P("dp", "tensor"),
        P(),
    )
    return jax.shard_map(shards, mesh=mesh, in_specs=in_specs, out_specs=out_specs, check_vma=False)
```

profile of v0, /device:TPU:0, one launch (start us, length us, event | category | flops | bytes accessed | tf_op | source)
XLA Modules:
  0.0 1199.9 jit_solution(9553132368857087687)
XLA Ops:
  16.1 36.6 %all-gather.13.cloned.1.call-done = bf16[2,576,1024]{2,1,0:T(8,128)(2,1)} async-done(((bf16[2,288,1024]{2,1,0:T(8,128)(2,1)}), bf16[2,576,1024]{2,1,0:T(8,128)(2,1)}) %all-gather.13.cloned.1.call-update) | async-done | bytes 2359312 | tf_op jit(solution)/shard_map/all_gather | solution.py:91
  52.7 47.4 %all-gather.15.cloned.1.call-done = bf16[1024,3,512]{2,0,1:T(8,128)(2,1)} async-done(((bf16[64,3,512]{2,0,1:T(8,128)(2,1)}), bf16[1024,3,512]{2,0,1:T(8,128)(2,1)}) %all-gather.15.cloned.1.call-update) | async-done | bytes 3145744 | tf_op jit(solution)/shard_map/all_gather | solution.py:84
  117.5 13.4 %multiply_reduce_fusion.3 = (f32[2,8,576]{2,1,0:T(8,128)S(1)}, f32[2,8,576,576]{2,3,1,0:T(8,128)}) fusion(bf16[2,576,8,64]{1,3,2,0:T(8,128)(2,1)} %bitcast.180, f32[2,576,8,64]{1,3,2,0:T(8,128)} %bitcast.174, f32[8,64]{1,0:T(8,128)S(1)} %add.272), kind=kOutput, calls=%fused_computation.13 | convolution fusion | flops 691264512 | bytes 24811520 | tf_op jit(solution)/shard_map/iqhe,ikhe->ihqk/dot_general | solution.py:11
  159.4 16.1 %all-gather.25.cloned.1.call-done = bf16[2,576,1024]{2,1,0:T(8,128)(2,1)} async-done(((bf16[2,288,1024]{2,1,0:T(8,128)(2,1)}), bf16[2,576,1024]{2,1,0:T(8,128)(2,1)}) %all-gather.25.cloned.1.call-update) | async-done | bytes 2359312 | tf_op jit(solution)/shard_map/all_gather | solution.py:91
  198.6 14.0 %multiply_reduce_fusion.2 = (f32[2,8,576]{2,1,0:T(8,128)S(1)}, f32[2,8,576,576]{2,3,1,0:T(8,128)}) fusion(bf16[2,576,8,64]{1,3,2,0:T(8,128)(2,1)} %bitcast.178, f32[2,576,8,64]{1,3,2,0:T(8,128)} %bitcast.176, f32[8,64]{1,0:T(8,128)S(1)} %add.272), kind=kOutput, calls=%fused_computation.12 | convolution fusion | flops 691264512 | bytes 24811520 | tf_op jit(solution)/shard_map/iqhe,ikhe->ihqk/dot_general | solution.py:11
  239.7 60.2 %reduce-scatter.17.cloned.1.call-done = f32[2,288,1024]{2,1,0:T(8,128)} async-done(((f32[2,576,1024]{2,1,0:T(8,128)}), f32[2,288,1024]{2,1,0:T(8,128)}) %reduce-scatter.17.cloned.1.call-update) | async-done | bytes 2359312 | tf_op jit(solution)/shard_map/reduce_scatter | solution.py:107
  312.0 40.8 %all-gather.21.cloned.1.call-done = bf16[1024,2048]{1,0:T(8,128)(2,1)} async-done(((bf16[64,2048]{1,0:T(8,128)(2,1)}), bf16[1024,2048]{1,0:T(8,128)(2,1)}) %all-gather.21.cloned.1.call-update) | async-done | bytes 4194320 | tf_op jit(solution)/shard_map/all_gather | solution.py:86
  352.7 36.1 %all-gather.27.cloned.1.call-done = bf16[2,576,1024]{2,1,0:T(8,128)(2,1)} async-done(((bf16[2,288,1024]{2,1,0:T(8,128)(2,1)}), bf16[2,576,1024]{2,1,0:T(8,128)(2,1)}) %all-gather.27.cloned.1.call-update) | async-done | bytes 2359312 | tf_op jit(solution)/shard_map/all_gather | solution.py:112
  398.5 28.0 %all-gather.33.cloned.1.call-done = bf16[2,576,1024]{2,1,0:T(8,128)(2,1)} async-done(((bf16[2,288,1024]{2,1,0:T(8,128)(2,1)}), bf16[2,576,1024]{2,1,0:T(8,128)(2,1)}) %all-gather.33.cloned.1.call-update) | async-done | bytes 2359312 | tf_op jit(solution)/shard_map/all_gather | solution.py:132
  426.5 52.6 %all-gather.23.cloned.1.call-done = bf16[1024,2048]{1,0:T(8,128)(2,1)} async-done(((bf16[64,2048]{1,0:T(8,128)(2,1)}), bf16[1024,2048]{1,0:T(8,128)(2,1)}) %all-gather.23.cloned.1.call-update) | async-done | bytes 4194320 | tf_op jit(solution)/shard_map/all_gather | solution.py:87
  500.8 14.5 %all-gather.19.cloned.1.call-done = bf16[2,576,1024]{2,1,0:T(8,128)(2,1)} async-done(((bf16[2,288,1024]{2,1,0:T(8,128)(2,1)}), bf16[2,576,1024]{2,1,0:T(8,128)(2,1)}) %all-gather.19.cloned.1.call-update) | async-done | bytes 2359312 | tf_op jit(solution)/shard_map/all_gather | solution.py:112
  526.9 25.9 %all-gather.29.cloned.1.call-done = bf16[2,576,1024]{2,1,0:T(8,128)(2,1)} async-done(((bf16[2,288,1024]{2,1,0:T(8,128)(2,1)}), bf16[2,576,1024]{2,1,0:T(8,128)(2,1)}) %all-gather.29.cloned.1.call-update) | async-done | bytes 2359312 | tf_op jit(solution)/shard_map/all_gather | solution.py:132
  574.2 40.9 %reduce-scatter.25.cloned.1.call-done = f32[2,288,1024]{2,1,0:T(8,128)} async-done(((f32[2,576,1024]{2,1,0:T(8,128)}), f32[2,288,1024]{2,1,0:T(8,128)}) %reduce-scatter.25.cloned.1.call-update) | async-done | bytes 2359312 | tf_op jit(solution)/shard_map/reduce_scatter | solution.py:141
  615.1 62.3 %reduce-scatter.21.cloned.1.call-done = f32[2,288,1024]{2,1,0:T(8,128)} async-done(((f32[2,576,1024]{2,1,0:T(8,128)}), f32[2,288,1024]{2,1,0:T(8,128)}) %reduce-scatter.21.cloned.1.call-update) | async-done | bytes 2359312 | tf_op jit(solution)/shard_map/reduce_scatter | solution.py:141
  731.9 29.2 %all-gather.35.cloned.1.call-done = bf16[2,576,1024]{2,1,0:T(8,128)(2,1)} async-done(((bf16[2,288,1024]{2,1,0:T(8,128)(2,1)}), bf16[2,576,1024]{2,1,0:T(8,128)(2,1)}) %all-gather.35.cloned.1.call-update) | async-done | bytes 2359312 | tf_op jit(solution)/shard_map/all_gather | solution.py:147
  779.4 16.6 %multiply_reduce_fusion.1 = (f32[2,8,576]{2,1,0:T(8,128)S(1)}, f32[2,8,576,576]{2,3,1,0:T(8,128)}) fusion(f32[2,8,576,576]{2,3,1,0:T(8,128)} %get-tuple-element.87, f32[2,8,576]{2,1,0:T(8,128)S(1)} %copy-done.45, bf16[2,576,8,64]{1,3,2,0:T(8,128)(2,1)S(1)} %bitcast.185, f32[2,576,8,64]{1,3,2,0:T(8,128)} %bitcast.188, f32[8,64]{1,0:T(8,128)S(1)} %copy-done.63), kind=kOutput, calls=%fused_computation.4 | convolution fusion | flops 701881344 | bytes 46082048 | tf_op jit(solution)/shard_map/iqhe,ikhe->ihqk/dot_general | solution.py:11
  796.0 16.0 %multiply_convert_fusion.1 = bf16[2,8,576,576]{2,3,1,0:T(8,128)(2,1)S(1)} fusion(f32[2,8,576,576]{2,3,1,0:T(8,128)} %get-tuple-element.93, f32[2,8,576,576]{2,3,1,0:T(8,128)} %get-tuple-element.87, f32[2,8,576]{2,1,0:T(8,128)S(1)} %get-tuple-element.92, f32[2,8,576]{2,1,0:T(8,128)S(1)} %copy-done.45), kind=kLoop, calls=%fused_computation.3 | loop fusion | flops 26542080 | bytes 53157888 | tf_op jit(solution)/shard_map/convert_element_type | solution.py:159
  843.9 18.5 %multiply_reduce_fusion = (f32[2,8,576]{2,1,0:T(8,128)S(1)}, f32[2,8,576,576]{2,3,1,0:T(8,128)}) fusion(f32[2,8,576,576]{2,3,1,0:T(8,128)} %get-tuple-element.89, f32[2,8,576]{2,1,0:T(8,128)S(1)} %copy-done.43, bf16[2,576,8,64]{1,3,2,0:T(8,128)(2,1)S(1)} %bitcast.182, f32[2,576,8,64]{1,3,2,0:T(8,128)} %bitcast.186, f32[8,64]{1,0:T(8,128)S(1)} %copy-done.63), kind=kOutput, calls=%fused_computation.1 | convolution fusion | flops 701881344 | bytes 46082048 | tf_op jit(solution)/shard_map/iqhe,ikhe->ihqk/dot_general | solution.py:11
  875.7 16.0 %multiply_convert_fusion = bf16[2,8,576,576]{2,3,1,0:T(8,128)(2,1)S(1)} fusion(f32[2,8,576,576]{2,3,1,0:T(8,128)} %get-tuple-element.91, f32[2,8,576,576]{2,3,1,0:T(8,128)} %get-tuple-element.89, f32[2,8,576]{2,1,0:T(8,128)S(1)} %get-tuple-element.90, f32[2,8,576]{2,1,0:T(8,128)S(1)} %copy-done.44), kind=kLoop, calls=%fused_computation | loop fusion | flops 26542080 | bytes 53157888 | tf_op jit(solution)/shard_map/convert_element_type | solution.py:159
  965.7 62.0 %all-reduce.1 = (f32[2,512]{1,0:T(2,128)}, f32[2048]{0:T(1024)}) all-reduce(f32[2,512]{1,0:T(2,128)S(1)} %maximum_add_fusion, f32[2048]{0:T(1024)S(1)} %copy-done.76), channel_id=1, replica_groups=mesh['dp'=16,'tensor'=2] {'dp'}, use_global_device_ids=true, to_apply=%region_41.0 | all-reduce | flops 3072 | bytes 24576 | tf_op jit(solution)/shard_map/psum | solution.py:211
  1029.3 16.7 %reduce-scatter.27.cloned.1.call-done = bf16[2,288,1024]{2,1,0:T(8,128)(2,1)} async-done(((bf16[2,576,1024]{2,1,0:T(8,128)(2,1)}), bf16[2,288,1024]{2,1,0:T(8,128)(2,1)}) %reduce-scatter.27.cloned.1.call-update) | async-done | bytes 1179664 | tf_op jit(solution)/shard_map/reduce_scatter | solution.py:177
  1049.8 40.5 %all-reduce = (f32[1024]{0:T(1024)}, f32[1024]{0:T(1024)}, f32[1024]{0:T(1024)}, f32[1024]{0:T(1024)}, f32[1024]{0:T(1024)}, /*index=5*/f32[1024]{0:T(1024)}) all-reduce(f32[1024]{0:T(1024)S(1)} %add.307, f32[1024]{0:T(1024)S(1)} %add.308, f32[1024]{0:T(1024)S(1)} %copy-done.87, ...), channel_id=1, replica_groups=mesh['dp'=16,'tensor'=2] {'dp','tensor'}, use_global_device_ids=true, to_apply=%region_32.0 | all-reduce | flops 6144 | bytes 49152 | tf_op jit(solution)/shard_map/psum | solution.py:199
  1098.2 22.6 %reduce-scatter.15.cloned.1.call-done = bf16[2,288,1024]{2,1,0:T(8,128)(2,1)} async-done(((bf16[2,576,1024]{2,1,0:T(8,128)(2,1)}), bf16[2,288,1024]{2,1,0:T(8,128)(2,1)}) %reduce-scatter.15.cloned.1.call-update) | async-done | bytes 1179664 | tf_op jit(solution)/shard_map/reduce_scatter | solution.py:117
  1128.3 62.7 %reduce-scatter.29.cloned.1.call-done = bf16[64,3,512]{2,0,1:T(8,128)(2,1)} async-done(((bf16[1024,3,512]{2,0,1:T(8,128)(2,1)}), bf16[64,3,512]{2,0,1:T(8,128)(2,1)}) %reduce-scatter.29.cloned.1.call-update) | async-done | bytes 196624 | tf_op jit(solution)/shard_map/reduce_scatter | solution.py:185
  (380 shorter events, 394.3 us)
Async XLA Ops:
  7.2 45.5 %all-gather.13.cloned.1.call-start = ((), (), s32[]{:S(2)}) async-start(), calls=%async_computation.12 | async-start | bytes 3538944 | tf_op jit(solution)/shard_map/all_gather | solution.py:91
  13.8 86.4 %all-gather.15.cloned.1.call-start = ((), (), s32[]{:S(2)}) async-start(), calls=%async_computation.13 | async-start | bytes 3342336 | tf_op jit(solution)/shard_map/all_gather | solution.py:84
  14.5 139.3 %all-gather.17.cloned.1.call-start = ((), (), s32[]{:S(2)}) async-start(), calls=%async_computation.14 | async-start | bytes 1114112 | tf_op jit(solution)/shard_map/all_gather | solution.py:85
  15.2 160.2 %all-gather.25.cloned.1.call-start = ((), (), s32[]{:S(2)}) async-start(), calls=%async_computation.20 | async-start | bytes 3538944 | tf_op jit(solution)/shard_map/all_gather | solution.py:91
  15.8 223.9 %reduce-scatter.13.cloned.1.call-start = ((), (), s32[]{:S(2)}) async-start(), calls=%async_computation.15 | async-start | bytes 7077888 | tf_op jit(solution)/shard_map/reduce_scatter | solution.py:107
  159.3 140.6 %reduce-scatter.17.cloned.1.call-start = ((), (), s32[]{:S(2)}) async-start(), calls=%async_computation.21 | async-start | bytes 7077888 | tf_op jit(solution)/shard_map/reduce_scatter | solution.py:107
  238.7 114.1 %all-gather.21.cloned.1.call-start = ((), (), s32[]{:S(2)}) async-start(), calls=%async_computation.17 | async-start | bytes 4456448 | tf_op jit(solution)/shard_map/all_gather | solution.py:86
  239.4 149.5 %all-gather.27.cloned.1.call-start = ((), (), s32[]{:S(2)}) async-start(), calls=%async_computation.22 | async-start | bytes 3538944 | tf_op jit(solution)/shard_map/all_gather | solution.py:112
  307.5 119.0 %all-gather.33.cloned.1.call-start = ((), (), s32[]{:S(2)}) async-start(), calls=%async_computation.28 | async-start | bytes 3538944 | tf_op jit(solution)/shard_map/all_gather | solution.py:132
  310.0 169.1 %all-gather.23.cloned.1.call-start = ((), (), s32[]{:S(2)}) async-start(), calls=%async_computation.18 | async-start | bytes 4456448 | tf_op jit(solution)/shard_map/all_gather | solution.py:87
  310.6 204.7 %all-gather.19.cloned.1.call-start = ((), (), s32[]{:S(2)}) async-start(), calls=%async_computation.16 | async-start | bytes 3538944 | tf_op jit(solution)/shard_map/all_gather | solution.py:112
  311.3 241.5 %all-gather.29.cloned.1.call-start = ((), (), s32[]{:S(2)}) async-start(), calls=%async_computation.24 | async-start | bytes 3538944 | tf_op jit(solution)/shard_map/all_gather | solution.py:132
  311.9 303.2 %reduce-scatter.25.cloned.1.call-start = ((), (), s32[]{:S(2)}) async-start(), calls=%async_computation.29 | async-start | bytes 7077888 | tf_op jit(solution)/shard_map/reduce_scatter | solution.py:141
  500.5 176.9 %reduce-scatter.21.cloned.1.call-start = ((), (), s32[]{:S(2)}) async-start(), calls=%async_computation.25 | async-start | bytes 7077888 | tf_op jit(solution)/shard_map/reduce_scatter | solution.py:141
  574.2 152.7 %all-gather.31.cloned.1.call-start = ((), (), s32[]{:S(2)}) async-start(), calls=%async_computation.26 | async-start | bytes 3538944 | tf_op jit(solution)/shard_map/all_gather | solution.py:147
  687.4 73.7 %all-gather.35.cloned.1.call-start = ((), (), s32[]{:S(2)}) async-start(), calls=%async_computation.30 | async-start | bytes 3538944 | tf_op jit(solution)/shard_map/all_gather | solution.py:147
  688.0 266.6 %reduce-scatter.33.cloned.1.call-start = ((), (), s32[]{:S(2)}) async-start(), calls=%async_computation.34 | async-start | bytes 4456448 | tf_op jit(solution)/shard_map/reduce_scatter | solution.py:191
  707.1 249.2 %reduce-scatter.35.cloned.1.call-start = ((), (), s32[]{:S(2)}) async-start(), calls=%async_computation.35 | async-start | bytes 4456448 | tf_op jit(solution)/shard_map/reduce_scatter | solution.py:194
  726.8 301.0 %reduce-scatter.31.cloned.1.call-start = ((), (), s32[]{:S(2)}) async-start(), calls=%async_computation.33 | async-start | bytes 1114112 | tf_op jit(solution)/shard_map/reduce_scatter | solution.py:188
  824.0 205.3 %reduce-scatter.23.cloned.1.call-start = ((), (), s32[]{:S(2)}) async-start(), calls=%async_computation.27 | async-start | bytes 3538944 | tf_op jit(solution)/shard_map/reduce_scatter | solution.py:177
  842.6 203.4 %reduce-scatter.27.cloned.1.call-start = ((), (), s32[]{:S(2)}) async-start(), calls=%async_computation.31 | async-start | bytes 3538944 | tf_op jit(solution)/shard_map/reduce_scatter | solution.py:177
  918.1 174.6 %reduce-scatter.19.cloned.1.call-start = ((), (), s32[]{:S(2)}) async-start(), calls=%async_computation.23 | async-start | bytes 3538944 | tf_op jit(solution)/shard_map/reduce_scatter | solution.py:117
  928.3 192.5 %reduce-scatter.15.cloned.1.call-start = ((), (), s32[]{:S(2)}) async-start(), calls=%async_computation.19 | async-start | bytes 3538944 | tf_op jit(solution)/shard_map/reduce_scatter | solution.py:117
  937.9 253.1 %reduce-scatter.29.cloned.1.call-start = ((), (), s32[]{:S(2)}) async-start(), calls=%async_computation.32 | async-start | bytes 3342336 | tf_op jit(solution)/shard_map/reduce_scatter | solution.py:185
  (106 other events, 4349.8 us)
Sparse Core Ops, SparseCore 0:
  13.9 38.7 all-gather.12
  54.9 45.2 all-gather.14
  102.3 36.7 all-gather.16
  140.5 34.9 all-gather.24
  177.6 59.9 reduce-scatter.12
  239.9 59.9 reduce-scatter.16
  302.1 50.5 all-gather.20
  354.3 34.5 all-gather.26
  390.4 36.0 all-gather.32
  428.5 50.5 all-gather.22
  480.7 34.5 all-gather.18
  516.7 36.0 all-gather.28
  555.1 59.9 reduce-scatter.24
  617.4 59.9 reduce-scatter.20
  687.5 36.0 all-gather.30
  725.0 36.0 all-gather.34
  764.8 72.4 reduce-scatter.32
  841.5 71.3 reduce-scatter.34
  916.6 56.4 reduce-scatter.30
  975.2 33.7 reduce-scatter.22
  1011.3 34.7 reduce-scatter.26
  1048.4 35.4 reduce-scatter.18
  1086.2 34.5 reduce-scatter.14
  1124.9 66.1 reduce-scatter.28
where the time goes:
time: 1210 us; the launch traced here: 1200 us
  waiting for transfers between devices  598 us (49%)
  matrix products  310 us (26%)
  other arithmetic  112 us (9%)
  blocking collectives  103 us (9%)
  local copies, waits for them, and re-layouts  59 us (5%)
  between operations  15.9 us (1%)
    dot_general x36, matrix products, mixed(): return jnp.einsum(form, left, right, preferred_element_type=jnp.float32)  310 us
    reduce_scatter x2, waiting for transfers between devices, shards(): lax.psum_scatter(second_terms, 'tensor', scatter_dimension=1, tiled=True)  103 us
    reduce_scatter x1, waiting for transfers between devices, shards(): lax.psum_scatter(grad_qkv.astype(jnp.bfloat16), 'dp', scatter_dimension=0...  62.7 us
    psum x1, blocking collectives, shards(): grad_pair, grad_up_bias = lax.psum((grad_pair, grad_up_bias), 'dp')  62 us
    reduce_scatter x2, waiting for transfers between devices, shards(): lax.psum_scatter(attn_terms, 'tensor', scatter_dimension=1, tiled=True)  60.3 us
    all_gather x2, waiting for transfers between devices, shards(): lax.all_gather(grad_final.astype(jnp.bfloat16), 'tensor', axis=1, tiled=T...  53.9 us
    all_gather x2, waiting for transfers between devices, shards(): lax.all_gather(normed.astype(jnp.bfloat16), 'tensor', axis=1, tiled=True)  52.7 us
    all_gather x1, waiting for transfers between devices, shards(): lax.all_gather(down_weight, 'dp', axis=0, tiled=True)  52.6 us
  transfers between devices with their start and end apart: 24, of which 16 were waited for; matrix products, arithmetic and copies ran while one was open for 37% of the time, Pallas kernels for 0%

commit v1 on v0

--- a/solution.py
+++ b/solution.py
@@ -32,7 +32,7 @@
     return jnp.sum(values, axis=(0, 1))
 
 
-def shards(
+def general_shards(
     tokens,
     image_mask,
     out_grad,
@@ -229,6 +229,293 @@
     )
 
 
+ROWS = 64
+
+
+def swap(values, axis_name, flip):
+    count = lax.axis_size(axis_name)
+    return lax.ppermute(values, axis_name, [(place, place ^ flip) for place in range(count)])
+
+
+def over_core(values):
+    return swap(values, "dp", 1)
+
+
+def over_y(values):
+    return swap(values, "dp", 2)
+
+
+def over_z(values, step):
+    return swap(values, "dp", 4 * step)
+
+
+def over_x(values):
+    return swap(values, "tensor", 1)
+
+
+def gather_pieces(own, x_first):
+    base = jnp.concatenate([own] + [over_z(own, step) for step in (1, 2, 3)], axis=0)
+    if x_first:
+        side = over_x(base)
+        near = ((base, side), (over_y(base), over_y(side)))
+    else:
+        side = over_y(base)
+        near = ((base, over_x(base)), (side, over_x(side)))
+    far = tuple(tuple(over_core(piece) for piece in pair) for pair in near)
+    return (near, far)
+
+
+def scatter_pieces(pieces, x_first):
+    def join(mine, other):
+        return (mine.astype(jnp.float32) + other.astype(jnp.float32)).astype(jnp.bfloat16)
+
+    near = [
+        [join(pieces[0][y_at][x_at], over_core(pieces[1][y_at][x_at])) for x_at in range(2)]
+        for y_at in range(2)
+    ]
+    if x_first:
+        pair = [join(near[y_at][0], over_x(near[y_at][1])) for y_at in range(2)]
+        whole = join(pair[0], over_y(pair[1]))
+    else:
+        pair = [join(near[0][x_at], over_y(near[1][x_at])) for x_at in range(2)]
+        whole = join(pair[0], over_x(pair[1]))
+    rows = whole.shape[0] // 4
+    parts = [whole[:rows]] + [
+        over_z(whole[step * rows : (step + 1) * rows], step) for step in (1, 2, 3)
+    ]
+    parts = [part.astype(jnp.float32) for part in parts]
+    return (parts[0] + parts[1]) + (parts[2] + parts[3])
+
+
+def join_pieces(pieces):
+    return jnp.concatenate(
+        [jnp.concatenate(pair, axis=1) for half in pieces for pair in half], axis=0
+    )
+
+
+def cut_pieces(values):
+    values = values.astype(jnp.bfloat16)
+    rows, columns = values.shape[0] // 4, values.shape[1] // 2
+    return [
+        [
+            [
+                values[(2 * core + y_at) * rows :][:rows, x_at * columns :][:, :columns]
+                for x_at in range(2)
+            ]
+            for y_at in range(2)
+        ]
+        for core in range(2)
+    ]
+
+
+def fast_shards(
+    tokens,
+    image_mask,
+    out_grad,
+    norm1_gain,
+    norm1_shift,
+    qkv_weight,
+    qv_bias,
+    out_weight,
+    out_bias,
+    norm2_gain,
+    norm2_shift,
+    up_weight,
+    up_bias,
+    down_weight,
+    down_bias,
+):
+    f32, bf16 = jnp.float32, jnp.bfloat16
+    images, half_len, width = tokens.shape
+    mine = images // 2
+    half_width = qkv_weight.shape[2]
+    half_hidden = up_weight.shape[1]
+    heads = width // HDIM
+    score_scale = HDIM ** (-0.5)
+    me = lax.axis_index("dp")
+    side = lax.axis_index("tensor")
+    block = jnp.arange(width) // ROWS
+    core_rel, y_rel, z_rel = block // 8, (block // 4) % 2, block % 4
+    source = ((z_rel * 4 + y_rel * 2 + core_rel) ^ me) * ROWS + jnp.arange(width) % ROWS
+    order = (jnp.arange(width)[:, None] == source[None, :]).astype(bf16)
+
+    def arrange(values):
+        return jnp.matmul(values, order, preferred_element_type=f32).astype(bf16)
+
+    def restore(values):
+        return jnp.einsum("...d,od->...o", values, order, preferred_element_type=f32).astype(bf16)
+
+    def exchange(values):
+        keep_part = lax.dynamic_slice_in_dim(values, side * mine, mine, 0)
+        send_part = lax.dynamic_slice_in_dim(values, (1 - side) * mine, mine, 0)
+        return jnp.stack([keep_part, over_x(send_part)])
+
+    def give_back(values):
+        own, other = values[0], over_x(values[1])
+        low_part = jnp.where(side == 0, own, other)
+        high_part = jnp.where(side == 0, other, own)
+        return jnp.concatenate([low_part, high_part], axis=0)
+
+    rows_here = 2 * mine * half_len
+    first = jnp.concatenate([qkv_weight.reshape(ROWS, 3 * half_width), out_weight], axis=1)
+    first_pieces = gather_pieces(first, True)
+    block_rows = arrange(exchange(tokens)).astype(f32).reshape(rows_here, width)
+    up_pieces = gather_pieces(up_weight, False)
+    down_pieces = gather_pieces(down_weight, True)
+    biases = jnp.concatenate([qv_bias.reshape(-1), up_bias])
+    biases = jnp.stack([biases, over_x(biases)]).astype(f32)
+    bias_q = biases[:, :half_width].reshape(-1)
+    bias_v = biases[:, half_width : 2 * half_width].reshape(-1)
+    bias_up = biases[:, 2 * half_width :].reshape(-1)
+    vectors = jnp.stack([norm1_gain, norm1_shift, norm2_gain, norm2_shift, out_bias, down_bias])
+    gain_one, shift_one, gain_two, shift_two, bias_out, bias_down = arrange(vectors).astype(f32)
+    keep = image_mask.astype(f32)
+    keep = lax.dynamic_slice_in_dim(keep, side * mine, mine, 0)
+    keep_rows = jnp.broadcast_to(keep[None, :, None], (2, mine, half_len)).reshape(rows_here, 1)
+
+    first_full = join_pieces(first_pieces)
+    first_split = first_full.reshape(width, 2, 2 * width // 1)
+    qkv_full = first_split[:, :, : 3 * half_width].reshape(width, 2, 3, half_width)
+    out_full = first_split[:, :, 3 * half_width :].reshape(width, width)
+    normed, unit_one, inv_one = normalize(block_rows, gain_one, shift_one)
+    normed = normed.astype(bf16)
+    projected = jnp.einsum("rd,dxcf->rcxf", normed, qkv_full, preferred_element_type=f32)
+    projected = projected.reshape(rows_here, 3, width)
+
+    def to_heads(values):
+        return (
+            values.astype(bf16)
+            .reshape(2, mine, half_len, heads, HDIM)
+            .transpose(1, 3, 0, 2, 4)
+            .reshape(mine, heads, 2 * half_len, HDIM)
+        )
+
+    def from_heads(values):
+        return (
+            values.astype(bf16)
+            .reshape(mine, heads, 2, half_len, HDIM)
+            .transpose(2, 0, 3, 1, 4)
+            .reshape(rows_here, width)
+        )
+
+    queries = to_heads(projected[:, 0] + bias_q)
+    key_rows = to_heads(projected[:, 1])
+    value_rows = to_heads(projected[:, 2] + bias_v)
+    scores = mixed("ihqe,ihke->ihqk", queries, key_rows) * score_scale
+    row_top = jnp.max(scores, axis=-1, keepdims=True)
+    raw_weights = jnp.exp(scores - row_top)
+    row_total = jnp.sum(raw_weights, axis=-1, keepdims=True)
+    log_total = row_top + jnp.log(row_total)
+    probs = (raw_weights / row_total).astype(bf16)
+    context = from_heads(mixed("ihqk,ihke->ihqe", probs, value_rows))
+    middle = block_rows + mixed("rf,of->ro", context, out_full) + bias_out
+    second, unit_two, inv_two = normalize(middle, gain_two, shift_two)
+    second = second.astype(bf16)
+    up_full = join_pieces(up_pieces)
+    hidden = mixed("rd,df->rf", second, up_full) + bias_up
+    gate_sig = jax.nn.sigmoid(1.702 * hidden)
+    active = (hidden * gate_sig).astype(bf16)
+    slope = gate_sig + 1.702 * hidden * gate_sig * (1.0 - gate_sig)
+    down_full = join_pieces(down_pieces)
+    feed_out = mixed("rf,of->ro", active, down_full) + bias_down
+    block_out = ((middle + feed_out) * keep_rows).astype(bf16)
+    block_out = give_back(restore(block_out).reshape(2, mine, half_len, width))
+
+    grad_final = arrange(exchange(out_grad)).reshape(rows_here, width).astype(f32) * keep_rows
+    final_low = grad_final.astype(bf16)
+    grad_down = scatter_pieces(cut_pieces(mixed("ro,rf->of", final_low, active)), True)
+    grad_hidden = (mixed("ro,of->rf", final_low, down_full) * slope).astype(bf16)
+    grad_up = scatter_pieces(cut_pieces(mixed("rd,rf->df", second, grad_hidden)), False)
+    grad_second = mixed("rf,df->rd", grad_hidden, up_full)
+    grad_middle = grad_final + normalize_back(grad_second, unit_two, inv_two, gain_two)
+    grad_branch = grad_middle.astype(bf16)
+    grad_out = mixed("ro,rf->of", grad_branch, context)
+    grad_context = to_heads(mixed("ro,of->rf", grad_branch, out_full))
+    again = mixed("ihqe,ihke->ihqk", queries, key_rows) * score_scale
+    soft_again = jnp.exp(again - log_total)
+    probs_again = soft_again.astype(bf16)
+    grad_values = mixed("ihqk,ihqe->ihke", probs_again, grad_context)
+    grad_soft = mixed("ihqe,ihke->ihqk", grad_context, value_rows)
+    grad_scores = (
+        soft_again * (grad_soft - jnp.sum(grad_soft * soft_again, axis=-1, keepdims=True))
+    ).astype(bf16)
+    grad_queries = mixed("ihqk,ihke->ihqe", grad_scores, key_rows) * score_scale
+    grad_keys = mixed("ihqk,ihqe->ihke", grad_scores, queries) * score_scale
+    grad_projected = jnp.stack(
+        [from_heads(grad_queries), from_heads(grad_keys), from_heads(grad_values)], axis=1
+    )
+    grad_qkv = jnp.einsum(
+        "rd,rcxf->dxcf",
+        normed,
+        grad_projected.reshape(rows_here, 3, 2, half_width),
+        preferred_element_type=f32,
+    )
+    grad_first = jnp.concatenate(
+        [
+            grad_qkv.reshape(width, 2, 3 * half_width),
+            grad_out.reshape(width, 2, half_width),
+        ],
+        axis=2,
+    ).reshape(width, 4 * width)
+    grad_first = scatter_pieces(cut_pieces(grad_first), False)
+    grad_normed = jnp.einsum(
+        "rcxf,dxcf->rd",
+        grad_projected.reshape(rows_here, 3, 2, half_width),
+        qkv_full,
+        preferred_element_type=f32,
+    )
+    grad_tokens = grad_middle + normalize_back(grad_normed, unit_one, inv_one, gain_one)
+    tokens_grad = give_back(
+        restore(grad_tokens.astype(bf16)).reshape(2, mine, half_len, width)
+    )
+
+    sums = jnp.stack(
+        [
+            jnp.sum(grad_normed * unit_one, axis=0),
+            jnp.sum(grad_normed, axis=0),
+            jnp.sum(grad_branch.astype(f32), axis=0),
+            jnp.sum(grad_second * unit_two, axis=0),
+            jnp.sum(grad_second, axis=0),
+            jnp.sum(grad_final, axis=0),
+        ]
+    )
+    sums = jnp.zeros_like(sums).at[:, source].set(sums)
+    halves = jnp.stack(
+        [
+            jnp.sum(grad_projected[:, 0].astype(f32), axis=0).reshape(2, half_width),
+            jnp.sum(grad_projected[:, 2].astype(f32), axis=0).reshape(2, half_width),
+        ],
+        axis=1,
+    ).reshape(2, 2 * half_width)
+    halves = jnp.concatenate(
+        [halves, jnp.sum(grad_hidden.astype(f32), axis=0).reshape(2, half_hidden)], axis=1
+    )
+    sums = sums + over_x(sums)
+    halves = halves[0] + over_x(halves[1])
+    small = jnp.concatenate([sums.reshape(-1), halves])
+    small = small + over_core(small)
+    small = small + over_y(small)
+    small = (small + over_z(small, 1)) + (over_z(small, 2) + over_z(small, 3))
+    sums = small[: 6 * width].reshape(6, width)
+    halves = small[6 * width :]
+    return (
+        block_out,
+        tokens_grad,
+        sums[0],
+        sums[1],
+        grad_first[:, : 3 * half_width].reshape(ROWS, 3, half_width),
+        halves[: 2 * half_width].reshape(2, half_width),
+        grad_first[:, 3 * half_width :],
+        sums[2],
+        sums[3],
+        sums[4],
+        grad_up,
+        halves[2 * half_width :],
+        grad_down,
+        sums[5],
+    )
+
+
 def solution(mesh):
     in_specs = (
         P("dp", "tensor", None),
@@ -263,4 +550,5 @@
         P("dp", "tensor"),
         P(),
     )
+    shards = fast_shards if mesh.shape["dp"] == 16 and mesh.shape["tensor"] == 2 else general_shards
     return jax.shard_map(shards, mesh=mesh, in_specs=in_specs, out_specs=out_specs, check_vma=False)

time: 1210 us -> 1150 us (0.950)
  waiting for transfers between devices: 598 us -> 264 us
  local copies, waits for them, and re-layouts: 59 us -> 329 us
  blocking collectives: 103 us -> 0 us
  starting transfers between devices: 1.97 us -> 67.8 us
  other arithmetic: 112 us -> 147 us
  matrix products: 310 us -> 337 us
  between operations: 15.9 us -> 2.25 us
    all_gather x12 -> x0, waiting for transfers between devices: 327 us -> none  [the longest x2 53.9 us: shards(): lax.all_gather(grad_final.astype(jnp.bfloat16), 'tensor', axis=1, tiled=T...]
    reduce_scatter x12 -> x0, waiting for transfers between devices: 266 us -> none  [the longest x2 103 us: shards(): lax.psum_scatter(second_terms, 'tensor', scatter_dimension=1, tiled=True)]
    ppermute x0 -> x72, waiting for transfers between devices: none -> 264 us  [swap(): lax.ppermute(values, axis_name, [(place, place ^ flip) for place in range...]
    reshape x0 -> x20, local copies, waits for them, and re-layouts: none -> 114 us  [the longest x9 60.3 us: from_heads(): return values.astype(bf16).reshape(mine, heads, 2, half_len, HDIM).transp...]
    psum x2 -> x0, blocking collectives: 103 us -> none  [the longest x1 62 us: shards(): grad_pair, grad_up_bias = lax.psum((grad_pair, grad_up_bias), 'dp')]
    dot_general x0 -> x8, matrix products: none -> 89.7 us  [the longest x2 42.3 us: restore(): jnp.einsum('...d,od->...o', values, order, preferred_element_type=f32)]
    ppermute x0 -> x72, starting transfers between devices: none -> 67.8 us  [swap(): lax.ppermute(values, axis_name, [(place, place ^ flip) for place in range...]
    dot_general x36 -> x14, matrix products: 310 us -> 247 us  [mixed(): return jnp.einsum(form, left, right, preferred_element_type=jnp.float32)]
  transfers between devices with their start and end apart: 24 -> 72, of which waited for: 16 -> 20; matrix products, arithmetic and copies ran while one was open for 37% -> 45% of each run, Pallas kernels for 0% -> 0%
where the time goes in v1:
time: 1150 us
  matrix products  337 us (29%)
  local copies, waits for them, and re-layouts  329 us (29%)
  waiting for transfers between devices  264 us (23%)
  other arithmetic  147 us (13%)
  starting transfers between devices  67.8 us (6%)
    ppermute x72, waiting for transfers between devices, swap(): lax.ppermute(values, axis_name, [(place, place ^ flip) for place in range...  264 us
    dot_general x14, matrix products, mixed(): return jnp.einsum(form, left, right, preferred_element_type=jnp.float32)  247 us
    ppermute x72, starting transfers between devices, swap(): lax.ppermute(values, axis_name, [(place, place ^ flip) for place in range...  67.8 us
    reshape x9, local copies, waits for them, and re-layouts, from_heads(): return values.astype(bf16).reshape(mine, heads, 2, half_len, HDIM).transp...  60.3 us
    unnamed x158, local copies, waits for them, and re-layouts  51 us
    dot_general x2, matrix products, restore(): jnp.einsum('...d,od->...o', values, order, preferred_element_type=f32)  42.3 us
    convert_element_type x1, other arithmetic, fast_shards(): grad_scores = (soft_again * (grad_soft - jnp.sum(grad_soft * soft_again,...  37.9 us
    reshape x5, local copies, waits for them, and re-layouts, to_heads(): return values.astype(bf16).reshape(2, mine, half_len, heads, HDIM).transp...  34.4 us
  transfers between devices with their start and end apart: 72, of which 20 were waited for; matrix products, arithmetic and copies ran while one was open for 45% of the time, Pallas kernels for 0%

profile of v1, /device:TPU:0, one launch (start us, length us, event | category | flops | bytes accessed | tf_op | source)
XLA Modules:
  0.0 1146.7 jit_solution(8452986449644435006)
XLA Ops:
  75.7 13.5 %collective-permute-done.4 = bf16[256,2048]{1,0:T(8,128)(2,1)} collective-permute-done((bf16[256,2048]{1,0:T(8,128)(2,1)}, bf16[256,2048]{1,0:T(8,128)(2,1)}, u32[]{:S(2)}, u32[]{:S(2)}) %collective-permute-start.4) | collective-permute-done | bytes 1048608 | tf_op jit(solution)/shard_map/ppermute | solution.py:237
  96.9 13.7 %collective-permute-done.33 = bf16[2,288,1024]{2,1,0:T(8,128)(2,1)} collective-permute-done((bf16[2,288,1024]{2,1,0:T(8,128)(2,1)}, bf16[2,288,1024]{2,1,0:T(8,128)(2,1)}, u32[]{:S(2)}, u32[]{:S(2)}) %collective-permute-start.33) | collective-permute-done | bytes 1179680 | tf_op jit(solution)/shard_map/ppermute | solution.py:237
  157.4 14.5 %reshape.551 = bf16[1024,2,2048]{2,1,0:T(2,128)(2,1)} reshape(bf16[1024,4096]{1,0:T(8,128)(2,1)} %maximum_maximum_fusion) | data formatting | bytes 16777216 | tf_op jit(solution)/shard_map/reshape | solution.py:377
  178.7 16.4 %copy.144 = bf16[1024,2,1536]{0,2,1:T(8,128)(2,1)} copy(bf16[1024,2,1536]{2,1,0:T(2,128)(2,1)} %slice.327) | data formatting | bytes 12582912
  195.1 14.0 %convolution_bitcast_fusion = f32[1152,3,2,512]{0,3,1,2:T(8,128)} fusion(bf16[1024,2,3,512]{0,3,2,1:T(8,128)(2,1)} %bitcast.185, bf16[1152,1024,1,1]{1,0,3,2:T(8,128)(2,1)S(1)} %bitcast.190), kind=kOutput, calls=%fused_computation.19 | convolution fusion | flops 7247757312 | bytes 22806528 | tf_op jit(solution)/shard_map/rd,dxcf->rcxf/dot_general | solution.py:382
  304.6 19.5 %multiply_reduce_fusion.1 = (f32[2,16,576]{2,1,0:T(8,128)S(1)}, f32[2,16,576,576]{2,3,1,0:T(8,128)}) fusion(bf16[2,16,576,64]{2,3,1,0:T(8,128)(2,1)} %reshape.555, bf16[2,16,576,64]{2,3,1,0:T(8,128)(2,1)S(1)} %reshape.556), kind=kOutput, calls=%fused_computation.7 | convolution fusion | flops 1380169728 | bytes 47259648 | tf_op jit(solution)/shard_map/ihqe,ihke->ihqk/dot_general | solution.py:11
  324.1 19.5 %fusion = f32[2,16,576]{2,1,0:T(8,128)S(1)} fusion(f32[2,16,576,576]{2,3,1,0:T(8,128)} %get-tuple-element.113, f32[2,16,576]{2,1,0:T(8,128)S(1)} %get-tuple-element.112), kind=kLoop, calls=%fused_computation.6 | loop fusion | flops 31832064 | bytes 42614784 | tf_op jit(solution)/shard_map/reduce_sum | solution.py:407
  343.6 19.3 %fusion.53 = bf16[2,16,576,64]{2,3,1,0:T(8,128)(2,1)} fusion(bf16[2,16,576,64]{2,3,1,0:T(8,128)(2,1)S(1)} %copy-done.5, f32[2,16,576,576]{2,3,1,0:T(8,128)} %get-tuple-element.113, f32[2,16,576]{2,1,0:T(8,128)S(1)} %fusion, f32[2,16,576]{2,1,0:T(8,128)S(1)} %get-tuple-element.112), kind=kOutput, calls=%fused_computation.122 | convolution fusion | flops 1402601472 | bytes 47333376 | tf_op jit(solution)/shard_map/ihqk,ihke->ihqe/dot_general | solution.py:11
  393.9 18.0 %collective-permute-done.27 = bf16[256,2048]{1,0:T(8,128)(2,1)S(1)} collective-permute-done((bf16[256,2048]{1,0:T(8,128)(2,1)}, bf16[256,2048]{1,0:T(8,128)(2,1)S(1)}, u32[]{:S(2)}, u32[]{:S(2)}) %collective-permute-start.27) | collective-permute-done | bytes 1048608 | tf_op jit(solution)/shard_map/ppermute | solution.py:237
  413.8 25.1 %multiply_convert_fusion.1 = (bf16[1152,4096]{1,0:T(8,128)(2,1)}, f32[1152,4096]{1,0:T(8,128)}) fusion(f32[4096]{0:T(1024)S(1)} %bitcast.213, bf16[256,2048]{1,0:T(8,128)(2,1)} %copy-done.62, bf16[256,2048]{1,0:T(8,128)(2,1)} %collective-permute-done.20, bf16[256,2048]{1,0:T(8,128)(2,1)} %copy-done.60, bf16[256,2048]{1,0:T(8,128)(2,1)} %collective-permute-done.18, ...), kind=kOutput, calls=%fused_computation.15 | convolution fusion | flops 9769713664 | bytes 41452544 | tf_op jit(solution)/shard_map/rd,df->rf/dot_general | solution.py:11
  440.9 27.1 %convert_reduce_fusion = (f32[4096]{0:T(1024)}, bf16[1152,4096]{1,0:T(8,128)(2,1)}) fusion(f32[1152,4096]{1,0:T(8,128)} %get-tuple-element.117, bf16[256,2048]{1,0:T(8,128)(2,1)} %collective-permute-done.31, bf16[256,2048]{1,0:T(8,128)(2,1)} %copy-done.59, bf16[256,2048]{1,0:T(8,128)(2,1)} %copy-done.58, bf16[256,2048]{1,0:T(8,128)(2,1)S(1)} %collective-permute-done.28, ...), kind=kOutput, calls=%fused_computation.14 | convolution fusion | flops 9789763584 | bytes 41439744 | tf_op jit(solution)/shard_map/ro,of->rf/dot_general | solution.py:11
  468.0 17.3 %convolution_convert_fusion.1 = bf16[1024,4096]{1,0:T(8,128)(2,1)} fusion(bf16[1152,4096]{1,0:T(8,128)(2,1)} %get-tuple-element.121, f32[1152,1024]{0,1:T(8,128)S(1)} %get-tuple-element.115, f32[1024]{0:T(1024)S(1)} %bitcast.223, f32[1024]{0:T(1024)S(1)} %bitcast.207, f32[1152]{0:T(1024)S(1)} %add_rsqrt_fusion, f32[1152]{0:T(1024)S(1)} %broadcast_multiply_fusion.4), kind=kOutput, calls=%fused_computation.25 | convolution fusion | flops 9673768960 | bytes 22561792 | tf_op jit(solution)/shard_map/rd,rf->df/dot_general | solution.py:11
  485.3 29.5 %fusion.122 = (f32[1024]{0:T(1024)}, f32[1152,1024]{1,0:T(8,128)}) fusion(bf16[1152,4096]{1,0:T(8,128)(2,1)} %get-tuple-element.121, bf16[256,2048]{1,0:T(8,128)(2,1)S(1)} %copy-done.63, bf16[256,2048]{1,0:T(8,128)(2,1)} %collective-permute-done.20, bf16[256,2048]{1,0:T(8,128)(2,1)S(1)} %copy-done.61, bf16[256,2048]{1,0:T(8,128)(2,1)} %collective-permute-done.18, ...), kind=kOutput, calls=%fused_computation.259 | convolution fusion | flops 9731963904 | bytes 22548480 | tf_op jit(solution)/shard_map/rf,df->rd/dot_general | solution.py:11
  558.4 19.5 %fusion.54 = bf16[2,16,576,64]{2,3,1,0:T(8,128)(2,1)} fusion(bf16[2,16,576,64]{2,3,1,0:T(8,128)(2,1)S(1)} %reshape.562, f32[2,16,576,576]{2,3,1,0:T(8,128)} %get-tuple-element.113, f32[2,16,576]{2,1,0:T(8,128)S(1)} %copy-done.9), kind=kOutput, calls=%fused_computation.123 | convolution fusion | flops 1391984640 | bytes 47259648 | tf_op jit(solution)/shard_map/ihqk,ihqe->ihke/dot_general | solution.py:11
  599.7 30.9 %multiply_reduce_fusion = (f32[2,16,576]{2,1,0:T(8,128)S(1)}, f32[2,16,576,576]{2,3,1,0:T(8,128)}) fusion(f32[2,16,576,576]{2,3,1,0:T(8,128)} %get-tuple-element.113, f32[2,16,576]{2,1,0:T(8,128)S(1)} %copy-done.9, bf16[2,16,576,64]{2,3,1,0:T(8,128)(2,1)S(1)} %reshape.562, bf16[2,16,576,64]{2,3,1,0:T(8,128)(2,1)S(1)} %copy-done.6), kind=kOutput, calls=%fused_computation.2 | convolution fusion | flops 1401403392 | bytes 89800704 | tf_op jit(solution)/shard_map/ihqe,ihke->ihqk/dot_general | solution.py:11
  630.6 37.9 %multiply_convert_fusion = bf16[2,16,576,576]{2,3,1,0:T(8,128)(2,1)} fusion(f32[2,16,576,576]{2,3,1,0:T(8,128)} %get-tuple-element.119, f32[2,16,576,576]{2,3,1,0:T(8,128)} %get-tuple-element.113, f32[2,16,576]{2,1,0:T(8,128)S(1)} %get-tuple-element.118, f32[2,16,576]{2,1,0:T(8,128)S(1)} %copy-done.9), kind=kLoop, calls=%fused_computation.1 | loop fusion | flops 53084160 | bytes 106315776 | tf_op jit(solution)/shard_map/convert_element_type | solution.py:441
  711.7 17.8 %convolution_convert_fusion = bf16[1024,4096]{1,0:T(8,128)(2,1)} fusion(bf16[1152,4096]{1,0:T(8,128)(2,1)} %get-tuple-element.116, f32[1152,1024]{0,1:T(8,128)} %copy.96, f32[1152]{0:T(1024)S(1)} %copy-done.39), kind=kOutput, calls=%fused_computation.24 | convolution fusion | flops 9670230016 | bytes 22548992 | tf_op jit(solution)/shard_map/ro,rf->of/dot_general | solution.py:11
  840.6 32.1 %fusion.21 = bf16[1152,1024]{1,0:T(8,128)(2,1)S(1)} fusion(s32[1024]{0:T(1024)S(1)} %copy-done.54, f32[1152,1024]{0,1:T(8,128)} %copy-done, bf16[1152,4096]{1,0:T(8,128)(2,1)} %get-tuple-element.116, f32[1152]{0:T(1024)S(1)} %copy-done.39, f32[1024]{0:T(1024)S(1)} %bitcast.221, bf16[256,2048]{1,0:T(8,128)(2,1)} %collective-permute-done.31, ...), kind=kOutput, calls=%fused_computation.65 | convolution fusion | flops 12153651200 | bytes 24916480 | tf_op jit(solution)/shard_map/...d,od->...o/dot_general | solution.py:346
  928.6 14.0 %collective-permute-done.32 = bf16[2,288,1024]{2,1,0:T(8,128)(2,1)} collective-permute-done((bf16[2,288,1024]{2,1,0:T(8,128)(2,1)}, bf16[2,288,1024]{2,1,0:T(8,128)(2,1)}, u32[]{:S(2)}, u32[]{:S(2)}) %collective-permute-start.32) | collective-permute-done | bytes 1179680 | tf_op jit(solution)/shard_map/ppermute | solution.py:237
  942.7 25.2 %collective-permute-done.34 = bf16[2,288,1024]{2,1,0:T(8,128)(2,1)S(1)} collective-permute-done((bf16[2,288,1024]{2,1,0:T(8,128)(2,1)S(1)}, bf16[2,288,1024]{2,1,0:T(8,128)(2,1)S(1)}, u32[]{:S(2)}, u32[]{:S(2)}) %collective-permute-start.34) | collective-permute-done | bytes 1179680 | tf_op jit(solution)/shard_map/ppermute | solution.py:237
  973.3 14.3 %collective-permute-done.67 = bf16[256,2048]{1,0:T(8,128)(2,1)S(1)} collective-permute-done((bf16[256,2048]{1,0:T(8,128)(2,1)S(1)}, bf16[256,2048]{1,0:T(8,128)(2,1)S(1)}, u32[]{:S(2)}, u32[]{:S(2)}) %collective-permute-start.67) | collective-permute-done | bytes 1048608 | tf_op jit(solution)/shard_map/ppermute | solution.py:237
  994.8 18.9 %collective-permute-done.47 = bf16[256,2048]{1,0:T(8,128)(2,1)S(1)} collective-permute-done((bf16[256,2048]{1,0:T(8,128)(2,1)S(1)}, bf16[256,2048]{1,0:T(8,128)(2,1)S(1)}, u32[]{:S(2)}, u32[]{:S(2)}) %collective-permute-start.47) | collective-permute-done | bytes 1048608 | tf_op jit(solution)/shard_map/ppermute | solution.py:237
  1016.4 19.8 %collective-permute-done.68 = bf16[256,2048]{1,0:T(8,128)(2,1)S(1)} collective-permute-done((bf16[256,2048]{1,0:T(8,128)(2,1)S(1)}, bf16[256,2048]{1,0:T(8,128)(2,1)S(1)}, u32[]{:S(2)}, u32[]{:S(2)}) %collective-permute-start.68) | collective-permute-done | bytes 1048608 | tf_op jit(solution)/shard_map/ppermute | solution.py:237
  1040.3 37.2 %collective-permute-done.44 = bf16[256,2048]{1,0:T(8,128)(2,1)S(1)} collective-permute-done((bf16[256,2048]{1,0:T(8,128)(2,1)S(1)}, bf16[256,2048]{1,0:T(8,128)(2,1)S(1)}, u32[]{:S(2)}, u32[]{:S(2)}) %collective-permute-start.44) | collective-permute-done | bytes 1048608 | tf_op jit(solution)/shard_map/ppermute | solution.py:237
  (441 shorter events, 629.4 us)
Async XLA Ops:
  37.7 53.9 %collective-permute-start = (bf16[2,288,1024]{2,1,0:T(8,128)(2,1)S(1)}, bf16[2,288,1024]{2,1,0:T(8,128)(2,1)S(1)}, u32[]{:S(2)}, u32[]{:S(2)}) collective-permute-start(bf16[2,288,1024]{2,1,0:T(8,128)(2,1)S(1)} %copy-done.25), channel_id=1, source_target_pairs={{0,1},{1,0},{2,3},{3,2},{4,5},{5,4},{6,7},{7,6},{8,9},{9,8},{10,11... | collective-permute-start | bytes 3538952 | tf_op jit(solution)/shard_map/ppermute | solution.py:237
  75.7 67.0 %collective-permute-start.7 = (bf16[256,2048]{1,0:T(8,128)(2,1)}, bf16[256,2048]{1,0:T(8,128)(2,1)}, u32[]{:S(2)}, u32[]{:S(2)}) collective-permute-start(bf16[256,2048]{1,0:T(8,128)(2,1)} %pad_maximum_fusion.6), channel_id=1, source_target_pairs={{0,2},{2,0},{4,6},{6,4},{8,10},{10,8},{12,14},{14,12},{16,18},{18,... | collective-permute-start | bytes 3145736 | tf_op jit(solution)/shard_map/ppermute | solution.py:237
  91.5 49.7 %collective-permute-start.16 = (bf16[256,2048]{1,0:T(8,128)(2,1)}, bf16[256,2048]{1,0:T(8,128)(2,1)}, u32[]{:S(2)}, u32[]{:S(2)}) collective-permute-start(bf16[256,2048]{1,0:T(8,128)(2,1)} %constant_dynamic-update-slice_fusion.3), channel_id=1, source_target_pairs={{0,4},{2,6},{4,0},{6,2},{8,12},{10,14},{12,8},{14,10},{16,20},{18,... | collective-permute-start | bytes 3145736 | tf_op jit(solution)/shard_map/ppermute | solution.py:237
  141.2 244.8 %collective-permute-start.26 = (bf16[256,2048]{1,0:T(8,128)(2,1)}, bf16[256,2048]{1,0:T(8,128)(2,1)}, u32[]{:S(2)}, u32[]{:S(2)}) collective-permute-start(bf16[256,2048]{1,0:T(8,128)(2,1)} %constant_dynamic-update-slice_fusion.7), channel_id=1, source_target_pairs={{0,4},{2,6},{4,0},{6,2},{8,12},{10,14},{12,8},{14,10},{16,20},{18,... | collective-permute-start | bytes 3145736 | tf_op jit(solution)/shard_map/ppermute | solution.py:237
  142.7 243.3 %collective-permute-start.25 = (bf16[256,2048]{1,0:T(8,128)(2,1)}, bf16[256,2048]{1,0:T(8,128)(2,1)}, u32[]{:S(2)}, u32[]{:S(2)}) collective-permute-start(bf16[256,2048]{1,0:T(8,128)(2,1)} %constant_dynamic-update-slice_fusion.7), channel_id=1, source_target_pairs={{0,1},{1,0},{2,3},{3,2},{4,5},{5,4},{6,7},{7,6},{8,9},{9,8},{10,11... | collective-permute-start | bytes 3145736 | tf_op jit(solution)/shard_map/ppermute | solution.py:237
  143.3 250.4 %collective-permute-start.18 = (bf16[256,2048]{1,0:T(8,128)(2,1)}, bf16[256,2048]{1,0:T(8,128)(2,1)}, u32[]{:S(2)}, u32[]{:S(2)}) collective-permute-start(bf16[256,2048]{1,0:T(8,128)(2,1)} %constant_dynamic-update-slice_fusion.3), channel_id=1, source_target_pairs={{0,2},{2,0},{4,6},{6,4},{8,10},{10,8},{12,14},{14,12},{16,18},{18,... | collective-permute-start | bytes 3145736 | tf_op jit(solution)/shard_map/ppermute | solution.py:237
  143.3 243.4 %collective-permute-start.15 = (bf16[256,2048]{1,0:T(8,128)(2,1)}, bf16[256,2048]{1,0:T(8,128)(2,1)}, u32[]{:S(2)}, u32[]{:S(2)}) collective-permute-start(bf16[256,2048]{1,0:T(8,128)(2,1)} %constant_dynamic-update-slice_fusion.3), channel_id=1, source_target_pairs={{0,1},{1,0},{2,3},{3,2},{4,5},{5,4},{6,7},{7,6},{8,9},{9,8},{10,11... | collective-permute-start | bytes 3145736 | tf_op jit(solution)/shard_map/ppermute | solution.py:237
  144.8 242.0 %collective-permute-start.17 = (bf16[256,2048]{1,0:T(8,128)(2,1)}, bf16[256,2048]{1,0:T(8,128)(2,1)}, u32[]{:S(2)}, u32[]{:S(2)}) collective-permute-start(bf16[256,2048]{1,0:T(8,128)(2,1)} %collective-permute-done.16), channel_id=1, source_target_pairs={{0,1},{1,0},{2,3},{3,2},{4,5},{5,4},{6,7},{7,6},{8,9},{9,8},{10,11... | collective-permute-start | bytes 3145736 | tf_op jit(solution)/shard_map/ppermute | solution.py:237
  393.7 45.8 %collective-permute-start.28 = (bf16[256,2048]{1,0:T(8,128)(2,1)}, bf16[256,2048]{1,0:T(8,128)(2,1)S(1)}, u32[]{:S(2)}, u32[]{:S(2)}) collective-permute-start(bf16[256,2048]{1,0:T(8,128)(2,1)} %constant_dynamic-update-slice_fusion.7), channel_id=1, source_target_pairs={{0,2},{2,0},{4,6},{6,4},{8,10},{10,8},{12,14},{14,12},{16,18},{18,... | collective-permute-start | bytes 3145736 | tf_op jit(solution)/shard_map/ppermute | solution.py:237
  733.9 183.4 %collective-permute-start.66 = (bf16[256,2048]{1,0:T(8,128)(2,1)}, bf16[256,2048]{1,0:T(8,128)(2,1)}, u32[]{:S(2)}, u32[]{:S(2)}) collective-permute-start(bf16[256,2048]{1,0:T(8,128)(2,1)} %get-tuple-element.53), channel_id=1, source_target_pairs={{0,2},{2,0},{4,6},{6,4},{8,10},{10,8},{12,14},{14,12},{16,18},{18,... | collective-permute-start | bytes 3145736 | tf_op jit(solution)/shard_map/ppermute | solution.py:237
  734.0 183.4 %collective-permute-start.63 = (bf16[256,2048]{1,0:T(8,128)(2,1)}, bf16[256,2048]{1,0:T(8,128)(2,1)}, u32[]{:S(2)}, u32[]{:S(2)}) collective-permute-start(bf16[256,2048]{1,0:T(8,128)(2,1)} %get-tuple-element.55), channel_id=1, source_target_pairs={{0,2},{2,0},{4,6},{6,4},{8,10},{10,8},{12,14},{14,12},{16,18},{18,... | collective-permute-start | bytes 3145736 | tf_op jit(solution)/shard_map/ppermute | solution.py:237
  757.8 121.5 %collective-permute-start.36 = (f32[3072]{0:T(1024)}, f32[3072]{0:T(1024)}, u32[]{:S(2)}, u32[]{:S(2)}) collective-permute-start(f32[3072]{0:T(1024)} %bitcast.46), channel_id=1, source_target_pairs={{0,1},{1,0},{2,3},{3,2},{4,5},{5,4},{6,7},{7,6},{8,9},{9,8},{10,11... | collective-permute-start | bytes 36872 | tf_op jit(solution)/shard_map/ppermute | solution.py:237
  822.8 57.2 %collective-permute-start.35 = (f32[6,1024]{0,1:T(8,128)}, f32[6,1024]{0,1:T(8,128)}, u32[]{:S(2)}, u32[]{:S(2)}) collective-permute-start(f32[6,1024]{0,1:T(8,128)} %scatter_custom_fusion), channel_id=1, source_target_pairs={{0,1},{1,0},{2,3},{3,2},{4,5},{5,4},{6,7},{7,6},{8,9},{9,8},{10,11... | collective-permute-start | bytes 73736 | tf_op jit(solution)/shard_map/ppermute | solution.py:237
  921.1 46.7 %collective-permute-start.34 = (bf16[2,288,1024]{2,1,0:T(8,128)(2,1)S(1)}, bf16[2,288,1024]{2,1,0:T(8,128)(2,1)S(1)}, u32[]{:S(2)}, u32[]{:S(2)}) collective-permute-start(bf16[2,288,1024]{2,1,0:T(8,128)(2,1)S(1)} %bitcast.196), channel_id=1, source_target_pairs={{0,1},{1,0},{2,3},{3,2},{4,5},{5,4},{6,7},{7,6},{8,9},{9,8},{10,11... | collective-permute-start | bytes 3538952 | tf_op jit(solution)/shard_map/ppermute | solution.py:237
  923.4 90.9 %collective-permute-start.62 = (bf16[256,2048]{1,0:T(8,128)(2,1)S(1)}, bf16[256,2048]{1,0:T(8,128)(2,1)S(1)}, u32[]{:S(2)}, u32[]{:S(2)}) collective-permute-start(bf16[256,2048]{1,0:T(8,128)(2,1)S(1)} %copy-done.29), channel_id=1, source_target_pairs={{0,2},{2,0},{4,6},{6,4},{8,10},{10,8},{12,14},{14,12},{16,18},{18,... | collective-permute-start | bytes 3145736 | tf_op jit(solution)/shard_map/ppermute | solution.py:237
  923.5 49.7 %collective-permute-start.65 = (bf16[256,2048]{1,0:T(8,128)(2,1)S(1)}, bf16[256,2048]{1,0:T(8,128)(2,1)S(1)}, u32[]{:S(2)}, u32[]{:S(2)}) collective-permute-start(bf16[256,2048]{1,0:T(8,128)(2,1)S(1)} %copy-done.30), channel_id=1, source_target_pairs={{0,2},{2,0},{4,6},{6,4},{8,10},{10,8},{12,14},{14,12},{16,18},{18,... | collective-permute-start | bytes 3145736 | tf_op jit(solution)/shard_map/ppermute | solution.py:237
  926.7 60.9 %collective-permute-start.67 = (bf16[256,2048]{1,0:T(8,128)(2,1)S(1)}, bf16[256,2048]{1,0:T(8,128)(2,1)S(1)}, u32[]{:S(2)}, u32[]{:S(2)}) collective-permute-start(bf16[256,2048]{1,0:T(8,128)(2,1)S(1)} %get-tuple-element.57), channel_id=1, source_target_pairs={{0,1},{1,0},{2,3},{3,2},{4,5},{5,4},{6,7},{7,6},{8,9},{9,8},{10,11... | collective-permute-start | bytes 3145736 | tf_op jit(solution)/shard_map/ppermute | solution.py:237
  942.6 47.2 %collective-permute-start.55 = (bf16[256,2048]{1,0:T(8,128)(2,1)S(1)}, bf16[256,2048]{1,0:T(8,128)(2,1)S(1)}, u32[]{:S(2)}, u32[]{:S(2)}) collective-permute-start(bf16[256,2048]{1,0:T(8,128)(2,1)S(1)} %copy-done.32), channel_id=1, source_target_pairs={{0,2},{2,0},{4,6},{6,4},{8,10},{10,8},{12,14},{14,12},{16,18},{18,... | collective-permute-start | bytes 3145736 | tf_op jit(solution)/shard_map/ppermute | solution.py:237
  991.4 44.8 %collective-permute-start.68 = (bf16[256,2048]{1,0:T(8,128)(2,1)S(1)}, bf16[256,2048]{1,0:T(8,128)(2,1)S(1)}, u32[]{:S(2)}, u32[]{:S(2)}) collective-permute-start(bf16[256,2048]{1,0:T(8,128)(2,1)S(1)} %add_convert_fusion.8), channel_id=1, source_target_pairs={{0,4},{2,6},{4,0},{6,2},{8,12},{10,14},{12,8},{14,10},{16,20},{18,... | collective-permute-start | bytes 3145736 | tf_op jit(solution)/shard_map/ppermute | solution.py:237
  994.7 86.6 %collective-permute-start.52 = (bf16[256,2048]{1,0:T(8,128)(2,1)S(1)}, bf16[256,2048]{1,0:T(8,128)(2,1)S(1)}, u32[]{:S(2)}, u32[]{:S(2)}) collective-permute-start(bf16[256,2048]{1,0:T(8,128)(2,1)S(1)} %copy-done.31), channel_id=1, source_target_pairs={{0,2},{2,0},{4,6},{6,4},{8,10},{10,8},{12,14},{14,12},{16,18},{18,... | collective-permute-start | bytes 3145736 | tf_op jit(solution)/shard_map/ppermute | solution.py:237
  1014.3 67.7 %collective-permute-start.54 = (bf16[256,2048]{1,0:T(8,128)(2,1)S(1)}, bf16[256,2048]{1,0:T(8,128)(2,1)S(1)}, u32[]{:S(2)}, u32[]{:S(2)}) collective-permute-start(bf16[256,2048]{1,0:T(8,128)(2,1)S(1)} %get-tuple-element.62), channel_id=1, source_target_pairs={{0,4},{2,6},{4,0},{6,2},{8,12},{10,14},{12,8},{14,10},{16,20},{18,... | collective-permute-start | bytes 3145736 | tf_op jit(solution)/shard_map/ppermute | solution.py:237
  1014.8 62.7 %collective-permute-start.44 = (bf16[256,2048]{1,0:T(8,128)(2,1)S(1)}, bf16[256,2048]{1,0:T(8,128)(2,1)S(1)}, u32[]{:S(2)}, u32[]{:S(2)}) collective-permute-start(bf16[256,2048]{1,0:T(8,128)(2,1)S(1)} %add_convert_fusion.26), channel_id=1, source_target_pairs={{0,4},{2,6},{4,0},{6,2},{8,12},{10,14},{12,8},{14,10},{16,20},{18,... | collective-permute-start | bytes 3145736 | tf_op jit(solution)/shard_map/ppermute | solution.py:237
  1077.5 47.7 %collective-permute-start.69 = (bf16[64,2048]{1,0:T(8,128)(2,1)S(1)}, bf16[64,2048]{1,0:T(8,128)(2,1)S(1)}, u32[]{:S(2)}, u32[]{:S(2)}) collective-permute-start(bf16[64,2048]{1,0:T(8,128)(2,1)S(1)} %get-tuple-element.84), channel_id=1, source_target_pairs={{0,8},{2,10},{4,12},{6,14},{8,0},{10,2},{12,4},{14,6},{16,24},{18,... | collective-permute-start | bytes 786440 | tf_op jit(solution)/shard_map/ppermute | solution.py:237
  1078.2 47.0 %collective-permute-start.71 = (bf16[64,2048]{1,0:T(8,128)(2,1)S(1)}, bf16[64,2048]{1,0:T(8,128)(2,1)S(1)}, u32[]{:S(2)}, u32[]{:S(2)}) collective-permute-start(bf16[64,2048]{1,0:T(8,128)(2,1)S(1)} %get-tuple-element.85), channel_id=1, source_target_pairs={{0,24},{2,26},{4,28},{6,30},{8,16},{10,18},{12,20},{14,22},{16,8},... | collective-permute-start | bytes 786440 | tf_op jit(solution)/shard_map/ppermute | solution.py:237
  (118 other events, 2515.5 us)

commit v2 on v0

--- a/solution.py
+++ b/solution.py
@@ -1,6 +1,8 @@
 import jax
 import jax.numpy as jnp
 from jax import lax
+from jax.experimental import pallas as pl
+from jax.experimental.pallas import tpu as pltpu
 from jax.sharding import PartitionSpec as P
 
 HDIM = 64
@@ -32,7 +34,7 @@
     return jnp.sum(values, axis=(0, 1))
 
 
-def shards(
+def general_shards(
     tokens,
     image_mask,
     out_grad,
@@ -229,6 +231,605 @@
     )
 
 
+ROWS = 64
+PART = 256
+VMEM_BYTES = 60 * 1024 * 1024
+LOG2_E = 1.4426950408889634
+BF16 = jnp.bfloat16
+F32 = jnp.float32
+
+
+def swap(values, axis_name, flip):
+    count = lax.axis_size(axis_name)
+    return lax.ppermute(values, axis_name, [(place, place ^ flip) for place in range(count)])
+
+
+def over_core(values):
+    return swap(values, "dp", 1)
+
+
+def over_y(values):
+    return swap(values, "dp", 2)
+
+
+def over_z(values, step):
+    return swap(values, "dp", 4 * step)
+
+
+def over_x(values):
+    return swap(values, "tensor", 1)
+
+
+def gather_pieces(own, x_first):
+    base = jnp.concatenate([own] + [over_z(own, step) for step in (1, 2, 3)], axis=0)
+    if x_first:
+        side = over_x(base)
+        near = [base, side, over_y(base), over_y(side)]
+    else:
+        side = over_y(base)
+        near = [base, over_x(base), side, over_x(side)]
+    return near + [over_core(piece) for piece in near]
+
+
+def add_low(mine, other):
+    return (mine.astype(F32) + other.astype(F32)).astype(BF16)
+
+
+def scatter_near(near, x_first):
+    if x_first:
+        pair = [add_low(near[2 * y_at], over_x(near[2 * y_at + 1])) for y_at in range(2)]
+        whole_sum = add_low(pair[0], over_y(pair[1]))
+    else:
+        pair = [add_low(near[x_at], over_y(near[2 + x_at])) for x_at in range(2)]
+        whole_sum = add_low(pair[0], over_x(pair[1]))
+    parts = [whole_sum[:ROWS]] + [
+        over_z(whole_sum[step * ROWS : (step + 1) * ROWS], step) for step in (1, 2, 3)
+    ]
+    parts = [part.astype(F32) for part in parts]
+    return (parts[0] + parts[1]) + (parts[2] + parts[3])
+
+
+def dot_nn(left, right):
+    return lax.dot_general(left, right, (((1,), (0,)), ((), ())), preferred_element_type=F32)
+
+
+def dot_nt(left, right):
+    return lax.dot_general(left, right, (((1,), (1,)), ((), ())), preferred_element_type=F32)
+
+
+def dot_tn(left, right):
+    return lax.dot_general(left, right, (((0,), (0,)), ((), ())), preferred_element_type=F32)
+
+
+def call(kernel, grid, in_specs, out_specs, out_shape, flops, moved):
+    return pl.pallas_call(
+        kernel,
+        grid=grid,
+        in_specs=in_specs,
+        out_specs=out_specs,
+        out_shape=out_shape,
+        compiler_params=pltpu.CompilerParams(vmem_limit_bytes=VMEM_BYTES),
+        cost_estimate=pl.CostEstimate(flops=int(flops), bytes_accessed=int(moved), transcendentals=0),
+    )
+
+
+def fixed(*shape, at=None):
+    place = at or (0,) * len(shape)
+    return pl.BlockSpec(shape, lambda *_: place, pipeline_mode=pl.Buffered(1))
+
+
+def struct(shape, dtype=BF16):
+    return jax.ShapeDtypeStruct(shape, dtype)
+
+
+def normal_parts(values):
+    mean_val = jnp.mean(values, axis=-1, keepdims=True)
+    centered = values - mean_val
+    inv_std = lax.rsqrt(jnp.mean(centered * centered, axis=-1, keepdims=True) + 1e-05)
+    return centered * inv_std, inv_std
+
+
+def column_sum(values):
+    return jnp.sum(values, axis=0, keepdims=True)
+
+
+def prepare(raw, order, gain, shift, keep, grads, tile=288):
+    count, width = raw.shape
+
+    def kernel(raw_ref, grad_ref, keep_ref, order_ref, gain_ref, shift_ref, rows_ref, norm_ref, final_ref, sum_ref):
+        rows = dot_nn(raw_ref[...], order_ref[...])
+        rows_ref[...] = rows.astype(BF16)
+        unit, _ = normal_parts(rows)
+        norm_ref[...] = (unit * gain_ref[...] + shift_ref[...]).astype(BF16)
+        final = dot_nn(grad_ref[...], order_ref[...]) * keep_ref[...]
+        final_ref[...] = final.astype(BF16)
+
+        @pl.when(pl.program_id(0) == 0)
+        def _():
+            sum_ref[...] = jnp.zeros_like(sum_ref)
+
+        sum_ref[...] += column_sum(final)
+
+    block = pl.BlockSpec((tile, width), lambda i: (i, 0))
+    return call(
+        kernel,
+        (count // tile,),
+        [block, block, pl.BlockSpec((tile, 1), lambda i: (i, 0)), fixed(width, width), fixed(1, width), fixed(1, width)],
+        [block, block, block, fixed(1, width)],
+        [struct((count, width))] * 3 + [struct((1, width), F32)],
+        4 * count * width * width,
+        12 * count * width,
+    )(raw, grads, keep, order, gain, shift)
+
+
+def project(normed, pieces, bias):
+    count, width = normed.shape
+    half = width // 2
+
+    def kernel(norm_ref, bias_ref, *refs):
+        parts, out_ref = refs[:8], refs[8]
+        for x_at in range(2):
+            weight = jnp.concatenate([parts[2 * at + x_at][...] for at in range(4)], axis=0)
+            columns = slice(x_at * half, (x_at + 1) * half)
+            out_ref[0, :, columns] = (
+                dot_nn(norm_ref[...], weight) + bias_ref[0, :, columns]
+            ).astype(BF16)
+
+    return call(
+        kernel,
+        (3,),
+        [fixed(count, width), pl.BlockSpec((1, 1, width), lambda j: (j, 0, 0))]
+        + [pl.BlockSpec((PART, half), lambda j: (0, j))] * 8,
+        pl.BlockSpec((1, count, width), lambda j: (j, 0, 0)),
+        struct((3, count, width)),
+        6 * count * width * width,
+        8 * count * width + 6 * width * width,
+    )(normed, bias, *pieces)
+
+
+def attend(projected, lanes=256):
+    _, _, images, half_len, width = projected.shape
+    length = 2 * half_len
+    per_step = lanes // HDIM
+
+    def kernel(proj_ref, out_ref, probs_ref):
+        queries, key_rows, value_rows = (proj_ref[at].reshape(length, lanes) for at in range(3))
+        outs = []
+        for head in range(per_step):
+            columns = slice(head * HDIM, (head + 1) * HDIM)
+            scores = dot_nt(queries[:, columns], key_rows[:, columns])
+            top = jnp.max(scores, axis=-1, keepdims=True)
+            raw = jnp.exp2((scores - top) * (LOG2_E * HDIM**-0.5))
+            probs = (raw * (1.0 / jnp.sum(raw, axis=-1, keepdims=True))).astype(BF16)
+            probs_ref[0, head] = probs
+            outs.append(dot_nn(probs, value_rows[:, columns]).astype(BF16))
+        out_ref[...] = jnp.concatenate(outs, axis=1).reshape(out_ref.shape)
+
+    heads = width // HDIM
+    return call(
+        kernel,
+        (images, width // lanes),
+        [pl.BlockSpec((3, 2, 1, half_len, lanes), lambda i, j: (0, 0, i, 0, j))],
+        [
+            pl.BlockSpec((2, 1, half_len, lanes), lambda i, j: (0, i, 0, j)),
+            pl.BlockSpec((1, per_step, length, length), lambda i, j: (i, j, 0, 0)),
+        ],
+        [struct((2, images, half_len, width)), struct((images, heads, length, length))],
+        16 * images * heads * length * length * HDIM,
+        images * heads * length * length * 2,
+    )(projected)
+
+
+def attend_back(projected, grad_context, probs, lanes=256):
+    _, _, images, half_len, width = projected.shape
+    length = 2 * half_len
+    per_step = lanes // HDIM
+    scale = HDIM**-0.5
+
+    def kernel(proj_ref, grad_ref, probs_ref, out_ref, sum_ref):
+        queries, key_rows, value_rows = (proj_ref[at].reshape(length, lanes) for at in range(3))
+        grads = grad_ref[...].reshape(length, lanes)
+        found = ([], [], [])
+        for head in range(per_step):
+            columns = slice(head * HDIM, (head + 1) * HDIM)
+            low = probs_ref[0, head]
+            found[2].append(dot_tn(low, grads[:, columns]).astype(BF16))
+            grad_soft = dot_nt(grads[:, columns], value_rows[:, columns])
+            soft = low.astype(F32)
+            scaled = soft * grad_soft
+            grad_scores = (scaled - soft * jnp.sum(scaled, axis=-1, keepdims=True)).astype(BF16)
+            found[0].append((dot_nn(grad_scores, key_rows[:, columns]) * scale).astype(BF16))
+            found[1].append((dot_tn(grad_scores, queries[:, columns]) * scale).astype(BF16))
+        for at in range(3):
+            joined = jnp.concatenate(found[at], axis=1)
+            out_ref[at] = joined.reshape(2, 1, half_len, lanes)
+            if at != 1:
+                sum_ref[0, at // 2 : at // 2 + 1] = column_sum(joined.astype(F32))
+
+    heads = width // HDIM
+    block = pl.BlockSpec((3, 2, 1, half_len, lanes), lambda i, j: (0, 0, i, 0, j))
+    return call(
+        kernel,
+        (images, width // lanes),
+        [
+            block,
+            pl.BlockSpec((2, 1, half_len, lanes), lambda i, j: (0, i, 0, j)),
+            pl.BlockSpec((1, per_step, length, length), lambda i, j: (i, j, 0, 0)),
+        ],
+        [block, pl.BlockSpec((1, 2, lanes), lambda i, j: (i, 0, j))],
+        [struct(projected.shape), struct((images, 2, width), F32)],
+        24 * images * heads * length * length * HDIM,
+        images * heads * length * length * 2,
+    )(projected, grad_context, probs)
+
+
+def add_branch(context, rows, pieces, bias, gain, shift, tile=288):
+    count, width = rows.shape
+    half = width // 2
+
+    def kernel(context_ref, rows_ref, bias_ref, gain_ref, shift_ref, *refs):
+        parts, middle_ref, norm_ref = refs[:8], refs[8], refs[9]
+        found = []
+        for at in range(4):
+            weight = jnp.concatenate([parts[2 * at][...], parts[2 * at + 1][...]], axis=1)
+            found.append(dot_nt(context_ref[...], weight))
+        middle = rows_ref[...].astype(F32) + (jnp.concatenate(found, axis=1) + bias_ref[...])
+        middle_ref[...] = middle
+        unit, _ = normal_parts(middle)
+        norm_ref[...] = (unit * gain_ref[...] + shift_ref[...]).astype(BF16)
+
+    block = pl.BlockSpec((tile, width), lambda i: (i, 0))
+    return call(
+        kernel,
+        (count // tile,),
+        [block, block] + [fixed(1, width)] * 3 + [fixed(PART, half, at=(0, 3))] * 8,
+        [block, block],
+        [struct((count, width), F32), struct((count, width))],
+        2 * count * width * width,
+        10 * count * width + 2 * width * width,
+    )(context, rows, bias, gain, shift, *pieces)
+
+
+def feed_up(second, pieces, bias, tile=512):
+    count, width = second.shape
+    columns = pieces[0].shape[1]
+
+    def kernel(second_ref, bias_ref, *refs):
+        parts, active_ref, slope_ref = refs[:8], refs[8], refs[9]
+        for x_at in range(2):
+            weight = jnp.concatenate([parts[2 * at + x_at][...] for at in range(4)], axis=0)
+            hidden = dot_nn(second_ref[...], weight) + bias_ref[x_at]
+            gate = 0.5 + 0.5 * jnp.tanh(0.851 * hidden)
+            active_ref[x_at] = (hidden * gate).astype(BF16)
+            slope_ref[x_at] = (gate * (1.0 + 1.702 * hidden * (1.0 - gate))).astype(BF16)
+
+    block = pl.BlockSpec((2, count, tile), lambda j: (0, 0, j))
+    return call(
+        kernel,
+        (columns // tile,),
+        [fixed(count, width), pl.BlockSpec((2, 1, tile), lambda j: (0, 0, j))]
+        + [pl.BlockSpec((PART, tile), lambda j: (0, j))] * 8,
+        [block, block],
+        [struct((2, count, columns))] * 2,
+        4 * count * width * columns,
+        4 * count * (width + 2 * columns) + 4 * width * columns,
+    )(second, bias, *pieces)
+
+
+def feed_down(active, middle, keep, pieces, bias, order, tile=288):
+    _, count, columns = active.shape
+    width = middle.shape[1]
+
+    def kernel(active_ref, middle_ref, keep_ref, bias_ref, order_ref, *refs):
+        parts, out_ref = refs[:8], refs[8]
+        found = []
+        for at in range(4):
+            found.append(
+                dot_nt(active_ref[0], parts[2 * at][...]) + dot_nt(active_ref[1], parts[2 * at + 1][...])
+            )
+        feed = jnp.concatenate(found, axis=1) + bias_ref[...]
+        out = ((middle_ref[...] + feed) * keep_ref[...]).astype(BF16)
+        out_ref[...] = dot_nt(out, order_ref[...]).astype(BF16)
+
+    block = pl.BlockSpec((tile, width), lambda i: (i, 0))
+    return call(
+        kernel,
+        (count // tile,),
+        [
+            pl.BlockSpec((2, tile, columns), lambda i: (0, i, 0)),
+            block,
+            pl.BlockSpec((tile, 1), lambda i: (i, 0)),
+            fixed(1, width),
+            fixed(width, width),
+        ]
+        + [fixed(PART, columns)] * 8,
+        block,
+        struct((count, width)),
+        4 * count * width * columns + 2 * count * width * width,
+        4 * count * columns + 6 * count * width + 4 * width * columns,
+    )(active, middle, keep, bias, order, *pieces)
+
+
+def gate_back(final, slope, pieces, tile=512):
+    count, width = final.shape
+    columns = pieces[0].shape[1]
+
+    def kernel(final_ref, slope_ref, *refs):
+        parts, out_ref, sum_ref = refs[:8], refs[8], refs[9]
+        for x_at in range(2):
+            weight = jnp.concatenate([parts[2 * at + x_at][...] for at in range(4)], axis=0)
+            grad = (dot_nn(final_ref[...], weight) * slope_ref[x_at].astype(F32)).astype(BF16)
+            out_ref[x_at] = grad
+            sum_ref[x_at] = column_sum(grad.astype(F32))
+
+    block = pl.BlockSpec((2, count, tile), lambda j: (0, 0, j))
+    return call(
+        kernel,
+        (columns // tile,),
+        [fixed(count, width), block] + [pl.BlockSpec((PART, tile), lambda j: (0, j))] * 8,
+        [block, pl.BlockSpec((2, 1, tile), lambda j: (0, 0, j))],
+        [struct((2, count, columns)), struct((2, 1, columns), F32)],
+        4 * count * width * columns,
+        4 * count * (width + 2 * columns) + 4 * width * columns,
+    )(final, slope, *pieces)
+
+
+def weight_half(left, rights, far, received=None, tile=512):
+    count, width = left.shape
+    right, right_spec, pick, columns = rights
+    half = width // 2
+
+    def kernel(left_ref, right_ref, *refs):
+        for y_at in range(2):
+            for x_at in range(2):
+                at = 2 * y_at + x_at
+                part = dot_tn(left_ref[:, y_at * PART : (y_at + 1) * PART], pick(right_ref, x_at))
+                if received is None:
+                    refs[at][...] = part.astype(BF16)
+                else:
+                    refs[4 + at][...] = (part + refs[at][...].astype(F32)).astype(BF16)
+
+    block = pl.BlockSpec((PART, tile), lambda j: (0, j))
+    extra = [] if received is None else list(received)
+    return call(
+        kernel,
+        (columns // tile,),
+        [fixed(count, half, at=(0, far)), right_spec] + [block] * len(extra),
+        [block] * 4,
+        [struct((PART, columns))] * 4,
+        2 * count * half * 2 * columns,
+        4 * count * columns + count * width + width * columns * (4 if extra else 2),
+    )(left, right, *extra)
+
+
+def weight_sum(left, rights, x_first, tile=512):
+    far = weight_half(left, rights, 1, None, tile)
+    received = [over_core(piece) for piece in far]
+    near = weight_half(left, rights, 0, received, tile)
+    return scatter_near(near, x_first)
+
+
+def second_back(grad_hidden, up_pieces, first_pieces, middle, final, gain, tile=288):
+    _, count, columns = grad_hidden.shape
+    width = middle.shape[1]
+    half = width // 2
+
+    def kernel(hidden_ref, middle_ref, final_ref, gain_ref, *refs):
+        ups, outs = refs[:8], refs[8:16]
+        grad_ref, branch_ref, context_ref, sum_ref = refs[16:]
+        found = []
+        for at in range(4):
+            found.append(
+                dot_nt(hidden_ref[0], ups[2 * at][...]) + dot_nt(hidden_ref[1], ups[2 * at + 1][...])
+            )
+        grad_second = jnp.concatenate(found, axis=1)
+        unit, inv_std = normal_parts(middle_ref[...])
+        grad_middle = final_ref[...].astype(F32) + normalize_back(
+            grad_second, unit, inv_std, gain_ref[...]
+        )
+        branch = grad_middle.astype(BF16)
+        grad_ref[...] = grad_middle
+        branch_ref[...] = branch
+        for x_at in range(2):
+            weight = jnp.concatenate([outs[2 * at + x_at][...] for at in range(4)], axis=0)
+            context_ref[:, x_at * half : (x_at + 1) * half] = dot_nn(branch, weight).astype(BF16)
+
+        @pl.when(pl.program_id(0) == 0)
+        def _():
+            sum_ref[...] = jnp.zeros_like(sum_ref)
+
+        sum_ref[0:1] += column_sum(grad_second * unit)
+        sum_ref[1:2] += column_sum(grad_second)
+        sum_ref[2:3] += column_sum(branch.astype(F32))
+
+    block = pl.BlockSpec((tile, width), lambda i: (i, 0))
+    return call(
+        kernel,
+        (count // tile,),
+        [pl.BlockSpec((2, tile, columns), lambda i: (0, i, 0)), block, block, fixed(1, width)]
+        + [fixed(PART, columns)] * 8
+        + [fixed(PART, half, at=(0, 3))] * 8,
+        [block, block, block, fixed(8, width)],
+        [struct((count, width), F32), struct((count, width)), struct((count, width)), struct((8, width), F32)],
+        4 * count * width * columns + 2 * count * width * width,
+        4 * count * columns + 14 * count * width + 4 * width * columns,
+    )(grad_hidden, middle, final, gain, *up_pieces, *first_pieces)
+
+
+def first_back(grad_projected, pieces, rows, grad_middle, gain, order, tile=288):
+    _, count, width = grad_projected.shape
+    half = width // 2
+
+    def kernel(grad_ref, rows_ref, middle_ref, gain_ref, order_ref, *refs):
+        parts, out_ref, sum_ref = refs[:8], refs[8], refs[9]
+        lefts = [
+            jnp.concatenate([grad_ref[at, :, x_at * half : (x_at + 1) * half] for at in range(3)], axis=1)
+            for x_at in range(2)
+        ]
+        found = []
+        for at in range(4):
+            found.append(
+                dot_nt(lefts[0], parts[2 * at][...]) + dot_nt(lefts[1], parts[2 * at + 1][...])
+            )
+        grad_normed = jnp.concatenate(found, axis=1)
+        unit, inv_std = normal_parts(rows_ref[...].astype(F32))
+        out = middle_ref[...] + normalize_back(grad_normed, unit, inv_std, gain_ref[...])
+        out_ref[...] = dot_nt(out.astype(BF16), order_ref[...]).astype(BF16)
+
+        @pl.when(pl.program_id(0) == 0)
+        def _():
+            sum_ref[...] = jnp.zeros_like(sum_ref)
+
+        sum_ref[0:1] += column_sum(grad_normed * unit)
+        sum_ref[1:2] += column_sum(grad_normed)
+
+    block = pl.BlockSpec((tile, width), lambda i: (i, 0))
+    return call(
+        kernel,
+        (count // tile,),
+        [pl.BlockSpec((3, tile, width), lambda i: (0, i, 0)), block, block, fixed(1, width), fixed(width, width)]
+        + [fixed(PART, 3 * half)] * 8,
+        [block, fixed(8, width)],
+        [struct((count, width)), struct((8, width), F32)],
+        6 * count * width * width + 2 * count * width * width,
+        16 * count * width + 6 * width * width,
+    )(grad_projected, rows, grad_middle, gain, order, *pieces)
+
+
+def fast_shards(
+    tokens,
+    image_mask,
+    out_grad,
+    norm1_gain,
+    norm1_shift,
+    qkv_weight,
+    qv_bias,
+    out_weight,
+    out_bias,
+    norm2_gain,
+    norm2_shift,
+    up_weight,
+    up_bias,
+    down_weight,
+    down_bias,
+):
+    images, half_len, width = tokens.shape
+    mine = images // 2
+    half = qkv_weight.shape[2]
+    half_hidden = up_weight.shape[1]
+    count = 2 * mine * half_len
+    me = lax.axis_index("dp")
+    side = lax.axis_index("tensor")
+    block = jnp.arange(width) // ROWS
+    core_rel, y_rel, z_rel = block // 8, (block // 4) % 2, block % 4
+    source = ((z_rel * 4 + y_rel * 2 + core_rel) ^ me) * ROWS + jnp.arange(width) % ROWS
+    order = (jnp.arange(width)[:, None] == source[None, :]).astype(BF16)
+
+    def exchange(values):
+        keep_part = lax.dynamic_slice_in_dim(values, side * mine, mine, 0)
+        send_part = lax.dynamic_slice_in_dim(values, (1 - side) * mine, mine, 0)
+        return jnp.stack([keep_part, over_x(send_part)]).reshape(count, width)
+
+    def give_back(values):
+        values = values.reshape(2, mine, half_len, width)
+        own, other = values[0], over_x(values[1])
+        low_part = jnp.where(side == 0, own, other)
+        high_part = jnp.where(side == 0, other, own)
+        return jnp.concatenate([low_part, high_part], axis=0)
+
+    first = jnp.concatenate([qkv_weight.reshape(ROWS, 3 * half), out_weight], axis=1)
+    first_pieces = gather_pieces(first, True)
+    raw = exchange(tokens)
+    raw_grad = exchange(out_grad)
+    up_pieces = gather_pieces(up_weight, False)
+    down_pieces = gather_pieces(down_weight, True)
+    biases = jnp.concatenate([qv_bias.reshape(-1), up_bias])
+    biases = jnp.stack([biases, over_x(biases)]).astype(F32)
+    bias_q = biases[:, :half].reshape(1, width)
+    bias_v = biases[:, half : 2 * half].reshape(1, width)
+    bias_qkv = jnp.stack([bias_q, jnp.zeros_like(bias_q), bias_v])
+    bias_up = biases[:, 2 * half :].reshape(2, 1, half_hidden)
+    vectors = jnp.stack([norm1_gain, norm1_shift, norm2_gain, norm2_shift, out_bias, down_bias])
+    vectors = jnp.matmul(vectors, order, preferred_element_type=F32)
+    gain_one, shift_one, gain_two, shift_two, bias_out, bias_down = (
+        vectors[at : at + 1] for at in range(6)
+    )
+    keep = lax.dynamic_slice_in_dim(image_mask.astype(F32), side * mine, mine, 0)
+    keep = jnp.broadcast_to(keep[None, :, None], (2, mine, half_len)).reshape(count, 1)
+
+    rows, normed, final, sum_final = prepare(raw, order, gain_one, shift_one, keep, raw_grad)
+    projected = project(normed, first_pieces, bias_qkv)
+    projected = projected.reshape(3, 2, mine, half_len, width)
+    context, probs = attend(projected)
+    context = context.reshape(count, width)
+    middle, second = add_branch(context, rows, first_pieces, bias_out, gain_two, shift_two)
+    active, slope = feed_up(second, up_pieces, bias_up)
+
+    def hidden_right(values, tile=512):
+        spec = pl.BlockSpec((2, count, tile), lambda j: (0, 0, j))
+        return (values, spec, lambda ref, x_at: ref[x_at], half_hidden)
+
+    grad_down = weight_sum(final, hidden_right(active), True)
+    grad_hidden, sum_hidden = gate_back(final, slope, down_pieces)
+    grad_up = weight_sum(second, hidden_right(grad_hidden), False)
+    block_out = feed_down(active, middle, keep, down_pieces, bias_down, order)
+    block_out = give_back(block_out)
+    grad_middle, grad_branch, grad_context, sums_two = second_back(
+        grad_hidden, up_pieces, first_pieces, middle, final, gain_two
+    )
+
+    def whole_right(values):
+        spec = pl.BlockSpec((count, width), lambda j: (0, 0))
+        return (values, spec, lambda ref, x_at: ref[:, x_at * half : (x_at + 1) * half], half)
+
+    grad_out = weight_sum(grad_branch, whole_right(context), True)
+    grad_context = grad_context.reshape(2, mine, half_len, width)
+    grad_projected, sums_pair = attend_back(projected, grad_context, probs)
+    grad_projected = grad_projected.reshape(3, count, width)
+    spec = pl.BlockSpec((1, count, width), lambda j: (j, 0, 0))
+    grad_qkv = weight_sum(
+        normed,
+        (grad_projected, spec, lambda ref, x_at: ref[0, :, x_at * half : (x_at + 1) * half], 3 * half),
+        False,
+    )
+    tokens_grad, sums_one = first_back(
+        grad_projected, first_pieces, rows, grad_middle, gain_one, order
+    )
+    tokens_grad = give_back(tokens_grad)
+
+    sums = jnp.concatenate([sums_one[:2], sums_two[2:3], sums_two[:2], sum_final], axis=0)
+    sums = jnp.zeros_like(sums).at[:, source].set(sums)
+    sums_pair = jnp.sum(sums_pair, axis=0)
+    halves = jnp.concatenate(
+        [sums_pair[0].reshape(2, half), sums_pair[1].reshape(2, half), sum_hidden.reshape(2, half_hidden)],
+        axis=1,
+    )
+    sums = sums + over_x(sums)
+    halves = halves[0] + over_x(halves[1])
+    small = jnp.concatenate([sums.reshape(-1), halves])
+    small = small + over_core(small)
+    small = small + over_y(small)
+    small = (small + over_z(small, 1)) + (over_z(small, 2) + over_z(small, 3))
+    sums = small[: 6 * width].reshape(6, width)
+    halves = small[6 * width :]
+    return (
+        block_out,
+        tokens_grad,
+        sums[0],
+        sums[1],
+        grad_qkv.reshape(ROWS, 3, half),
+        halves[: 2 * half].reshape(2, half),
+        grad_out,
+        sums[2],
+        sums[3],
+        sums[4],
+        grad_up,
+        halves[2 * half :],
+        grad_down,
+        sums[5],
+    )
+
+
 def solution(mesh):
     in_specs = (
         P("dp", "tensor", None),
@@ -263,4 +864,6 @@
         P("dp", "tensor"),
         P(),
     )
+    small_slice = mesh.shape["dp"] == 16 and mesh.shape["tensor"] == 2
+    shards = fast_shards if small_slice else general_shards
     return jax.shard_map(shards, mesh=mesh, in_specs=in_specs, out_specs=out_specs, check_vma=False)

time: 1210 us -> 659 us (0.54)
  waiting for transfers between devices: 598 us -> 252 us
  matrix products: 310 us -> 0.79 us
  Pallas kernels: 0 us -> 264 us
  blocking collectives: 103 us -> 0 us
  other arithmetic: 112 us -> 23.5 us
  starting transfers between devices: 1.97 us -> 75.4 us
  local copies, waits for them, and re-layouts: 59 us -> 36.3 us
  between operations: 15.9 us -> 1.69 us
    all_gather x12 -> x0, waiting for transfers between devices: 327 us -> none  [the longest x2 53.9 us: shards(): lax.all_gather(grad_final.astype(jnp.bfloat16), 'tensor', axis=1, tiled=T...]
    dot_general x36 -> x1, matrix products: 310 us -> 0.79 us  [fast_shards(): vectors = jnp.matmul(vectors, order, preferred_element_type=F32)]
    reduce_scatter x12 -> x0, waiting for transfers between devices: 266 us -> none  [the longest x2 103 us: shards(): lax.psum_scatter(second_terms, 'tensor', scatter_dimension=1, tiled=True)]
    pallas_call x0 -> x18, Pallas kernels: none -> 264 us  [the longest x8 64 us: weight_half(): call(kernel, (columns // tile,), [fixed(count, half, at=(0, far)), right_...]
    ppermute x0 -> x82, waiting for transfers between devices: none -> 252 us  [swap(): lax.ppermute(values, axis_name, [(place, place ^ flip) for place in range...]
    psum x2 -> x0, blocking collectives: 103 us -> none  [the longest x1 62 us: shards(): grad_pair, grad_up_bias = lax.psum((grad_pair, grad_up_bias), 'dp')]
    ppermute x0 -> x82, starting transfers between devices: none -> 75.4 us  [swap(): lax.ppermute(values, axis_name, [(place, place ^ flip) for place in range...]
    convert_element_type x22 -> x11, other arithmetic: 59.2 us -> 8.45 us  [the longest x8 6.2 us: add_low(): return (mine.astype(F32) + other.astype(F32)).astype(BF16)]
  transfers between devices with their start and end apart: 24 -> 82, of which waited for: 16 -> 27; matrix products, arithmetic and copies ran while one was open for 37% -> 8% of each run, Pallas kernels for 0% -> 25%
where the time goes in v2:
time: 659 us; the launch traced here: 653 us
  Pallas kernels  264 us (40%)
  waiting for transfers between devices  252 us (38%)
  starting transfers between devices  75.4 us (11%)
  local copies, waits for them, and re-layouts  36.3 us (6%)
  other arithmetic  23.5 us (4%)
    ppermute x82, waiting for transfers between devices, swap(): lax.ppermute(values, axis_name, [(place, place ^ flip) for place in range...  252 us
    ppermute x82, starting transfers between devices, swap(): lax.ppermute(values, axis_name, [(place, place ^ flip) for place in range...  75.4 us
    pallas_call x8, Pallas kernels, weight_half(): call(kernel, (columns // tile,), [fixed(count, half, at=(0, far)), right_...  64 us
    pallas_call x1, Pallas kernels, attend_back(): call(kernel, (images, width // lanes), [block, pl.BlockSpec((2, 1, half_l...  38.8 us
    pallas_call x1, Pallas kernels, attend(): call(kernel, (images, width // lanes), [pl.BlockSpec((3, 2, 1, half_len,...  30.9 us
    pallas_call x1, Pallas kernels, second_back(): call(kernel, (count // tile,), [pl.BlockSpec((2, tile, columns), lambda i...  22.2 us
    pallas_call x1, Pallas kernels, feed_up(): call(kernel, (columns // tile,), [fixed(count, width), pl.BlockSpec((2, 1...  21.9 us
    pallas_call x1, Pallas kernels, feed_down(): call(kernel, (count // tile,), [pl.BlockSpec((2, tile, columns), lambda i...  19.2 us
  transfers between devices with their start and end apart: 82, of which 27 were waited for; matrix products, arithmetic and copies ran while one was open for 8% of the time, Pallas kernels for 25%

profile of v2, /device:TPU:0, one launch (start us, length us, event | category | flops | bytes accessed | tf_op | source)
XLA Modules:
  0.0 653.2 jit_solution(931048731809940214)
XLA Ops:
  27.2 10.0 %collective-permute-done.4 = bf16[64,2048]{1,0:T(8,128)(2,1)S(1)} collective-permute-done((bf16[64,2048]{1,0:T(8,128)(2,1)S(1)}, bf16[64,2048]{1,0:T(8,128)(2,1)S(1)}, u32[]{:S(2)}, u32[]{:S(2)}) %collective-permute-start.4) | collective-permute-done | bytes 262176 | tf_op jit(solution)/shard_map/ppermute | solution.py:244
  45.0 13.8 %collective-permute-done.24 = bf16[64,2048]{1,0:T(8,128)(2,1)S(1)} collective-permute-done((bf16[64,2048]{1,0:T(8,128)(2,1)}, bf16[64,2048]{1,0:T(8,128)(2,1)S(1)}, u32[]{:S(2)}, u32[]{:S(2)}) %collective-permute-start.24) | collective-permute-done | bytes 262176 | tf_op jit(solution)/shard_map/ppermute | solution.py:244
  74.0 39.8 %collective-permute-done.2 = bf16[3072]{0:T(1024)(128)(2,1)S(1)} collective-permute-done((bf16[3072]{0:T(1024)(128)(2,1)S(1)}, bf16[3072]{0:T(1024)(128)(2,1)S(1)}, u32[]{:S(2)}, u32[]{:S(2)}) %collective-permute-start.2) | collective-permute-done | bytes 6176 | tf_op jit(solution)/shard_map/ppermute | solution.py:244
  124.9 15.4 %collective-permute-done.26.refs_1_ = bf16[256,2048]{1,0:T(8,128)(2,1)} collective-permute-done((bf16[256,2048]{1,0:T(8,128)(2,1)}, bf16[256,2048]{1,0:T(8,128)(2,1)}, u32[]{:S(2)}, u32[]{:S(2)}) %collective-permute-start.26) | collective-permute-done | bytes 1048608 | tf_op jit(solution)/shard_map/ppermute | solution.py:244
  140.3 23.7 %collective-permute-done.17.refs_2_ = bf16[256,2048]{1,0:T(8,128)(2,1)} collective-permute-done((bf16[256,2048]{1,0:T(8,128)(2,1)}, bf16[256,2048]{1,0:T(8,128)(2,1)}, u32[]{:S(2)}, u32[]{:S(2)}) %collective-permute-start.17) | collective-permute-done | bytes 1048608 | tf_op jit(solution)/shard_map/ppermute | solution.py:244
  164.6 16.6 %collective-permute-done.8.refs_3_.refs_11_ = bf16[256,2048]{1,0:T(8,128)(2,1)} collective-permute-done((bf16[256,2048]{1,0:T(8,128)(2,1)}, bf16[256,2048]{1,0:T(8,128)(2,1)}, u32[]{:S(2)}, u32[]{:S(2)}) %collective-permute-start.8) | collective-permute-done | bytes 1048608 | tf_op jit(solution)/shard_map/ppermute | solution.py:244
  187.6 10.4 %shard_map.254 = (bf16[1152,1024]{1,0:T(8,128)(2,1)}, bf16[1152,1024]{1,0:T(8,128)(2,1)}, bf16[1152,1024]{1,0:T(8,128)(2,1)}, f32[1,1024]{1,0:T(1,128)}) custom-call(bf16[1152,1024]{1,0:T(8,128)(2,1)} %bitcast.40, bf16[1152,1024]{1,0:T(8,128)(2,1)} %bitcast.41, f32[1152,1]{1,0:T(8,128)} %reshape.404.keep_ref, bf16[1024,1024]{1,0:T(8,128)(2,1)} %fusion.1.order_ref, ...), custom_call_target="tpu_custom_call" | custom-call | flops 4831838208 | bytes 14155776 | tf_op jit(solution)/shard_map/pallas_call | solution.py:354
  200.1 12.1 %shard_map.255 = bf16[3,1152,1024]{2,1,0:T(8,128)(2,1)} custom-call(bf16[1152,1024]{1,0:T(8,128)(2,1)} %get-tuple-element.66.norm_ref.left_ref, f32[3,1,1024]{2,1,0:T(1,128)} %pad_maximum_fusion.7.bias_ref, bf16[256,2048]{1,0:T(8,128)(2,1)} %copy-done, bf16[256,2048]{1,0:T(8,128)(2,1)} %collective-permute-done.6.refs_1_.refs_9_, ...), custom_call_target="tpu_custom_call" | custom-call | flops 7247757312 | bytes 15728640 | tf_op jit(solution)/shard_map/pallas_call | solution.py:378
  213.0 30.9 %shard_map.256 = (bf16[2,2,288,1024]{3,2,1,0:T(8,128)(2,1)}, bf16[2,16,576,576]{3,2,1,0:T(8,128)(2,1)}) custom-call(bf16[3,2,2,288,1024]{4,3,2,1,0:T(8,128)(2,1)} %bitcast.59), custom_call_target="tpu_custom_call" | custom-call | flops 10871635968 | bytes 21233664 | tf_op jit(solution)/shard_map/pallas_call | solution.py:409
  253.0 21.9 %shard_map.258 = (bf16[2,1152,2048]{2,1,0:T(8,128)(2,1)}, bf16[2,1152,2048]{2,1,0:T(8,128)(2,1)}) custom-call(bf16[1152,1024]{1,0:T(8,128)(2,1)} %get-tuple-element.69.second_ref.left_ref, f32[2,1,2048]{2,1,0:T(1,128)} %reshape.390.bias_ref, bf16[256,2048]{1,0:T(8,128)(2,1)} %constant_dynamic-update-slice_fusion.3.refs_0_, ...), custom_call_target="tpu_custom_call" | custom-call | flops 9663676416 | bytes 31981568 | tf_op jit(solution)/shard_map/pallas_call | solution.py:507
  275.8 18.1 %shard_map.260 = (bf16[2,1152,2048]{2,1,0:T(8,128)(2,1)}, f32[2,1,2048]{2,1,0:T(1,128)}) custom-call(bf16[1152,1024]{1,0:T(8,128)(2,1)} %get-tuple-element.72.final_ref.left_ref, bf16[2,1152,2048]{2,1,0:T(8,128)(2,1)} %get-tuple-element.73.slope_ref, bf16[256,2048]{1,0:T(8,128)(2,1)} %constant_dynamic-update-slice_fusion.7.refs_0_, ...), custom_call_target="tpu_custom_call" | custom-call | flops 9663676416 | bytes 31981568 | tf_op jit(solution)/shard_map/pallas_call | solution.py:566
  293.9 22.2 %shard_map.261 = (f32[1152,1024]{1,0:T(8,128)}, bf16[1152,1024]{1,0:T(8,128)(2,1)}, bf16[1152,1024]{1,0:T(8,128)(2,1)}, f32[8,1024]{1,0:T(8,128)}) custom-call(bf16[2,1152,2048]{2,1,0:T(8,128)(2,1)} %get-tuple-element.74.hidden_ref.right_ref, f32[1152,1024]{1,0:T(8,128)} %get-tuple-element.71.middle_ref, ...), custom_call_target="tpu_custom_call" | custom-call | flops 12079595520 | bytes 34340864 | tf_op jit(solution)/shard_map/pallas_call | solution.py:646
  317.7 38.8 %shard_map.262 = (bf16[3,2,2,288,1024]{4,3,2,1,0:T(8,128)(2,1)}, f32[2,2,1024]{2,1,0:T(2,128)}) custom-call(bf16[3,2,2,288,1024]{4,3,2,1,0:T(8,128)(2,1)} %bitcast.60, bf16[2,2,288,1024]{3,2,1,0:T(8,128)(2,1)} %bitcast.61, bf16[2,16,576,576]{3,2,1,0:T(8,128)(2,1)} %get-tuple-element.76.probs_ref), custom_call_target="tpu_custom_call" | custom-call | flops 16307453952 | bytes 21233664 | tf_op jit(solution)/shard_map/pallas_call | solution.py:451
  356.5 18.1 %shard_map.263 = (bf16[1152,1024]{1,0:T(8,128)(2,1)}, f32[8,1024]{1,0:T(8,128)}) custom-call(bf16[3,1152,1024]{2,1,0:T(8,128)(2,1)} %bitcast.56, bf16[1152,1024]{1,0:T(8,128)(2,1)} %get-tuple-element.68.rows_ref, f32[1152,1024]{1,0:T(8,128)} %get-tuple-element.78.middle_ref, f32[1,1024]{1,0:T(1,128)} %get-tuple-element.184.gain_ref, ...), custom_call_target="tpu_custom_call" | custom-call | flops 9663676416 | bytes 25165824 | tf_op jit(solution)/shard_map/pallas_call | solution.py:687
  409.6 19.2 %shard_map.259 = bf16[1152,1024]{1,0:T(8,128)(2,1)} custom-call(bf16[2,1152,2048]{2,1,0:T(8,128)(2,1)} %get-tuple-element.70.active_ref.right_ref, f32[1152,1024]{1,0:T(8,128)} %get-tuple-element.71.middle_ref, f32[1152,1]{1,0:T(8,128)} %reshape.404.keep_ref, f32[1,1024]{1,0:T(1,128)} %get-tuple-element.179.bias_ref, bf16[1024,1024]{1,0:T(8,128)(2,1)} %fusion.1.order_ref, ...), custom_call_target="tpu_custom_call" | custom-call | flops 12079595520 | bytes 24903680 | tf_op jit(solution)/shard_map/pallas_call | solution.py:535
  431.5 9.3 %shard_map.268 = (bf16[256,2048]{1,0:T(8,128)(2,1)}, bf16[256,2048]{1,0:T(8,128)(2,1)}, bf16[256,2048]{1,0:T(8,128)(2,1)}, bf16[256,2048]{1,0:T(8,128)(2,1)}) custom-call(bf16[1152,1024]{1,0:T(8,128)(2,1)} %get-tuple-element.69.second_ref.left_ref, bf16[2,1152,2048]{2,1,0:T(8,128)(2,1)} %get-tuple-element.74.hidden_ref.right_ref), custom_call_target="tpu_custom_call" | custom-call | flops 4831838208 | bytes 14811136 | tf_op jit(solution)/shard_map/pallas_call | solution.py:594
  455.3 9.2 %shard_map.270 = (bf16[256,2048]{1,0:T(8,128)(2,1)}, bf16[256,2048]{1,0:T(8,128)(2,1)}, bf16[256,2048]{1,0:T(8,128)(2,1)}, bf16[256,2048]{1,0:T(8,128)(2,1)}) custom-call(bf16[1152,1024]{1,0:T(8,128)(2,1)} %get-tuple-element.72.final_ref.left_ref, bf16[2,1152,2048]{2,1,0:T(8,128)(2,1)} %get-tuple-element.70.active_ref.right_ref), custom_call_target="tpu_custom_call" | custom-call | flops 4831838208 | bytes 14811136 | tf_op jit(solution)/shard_map/pallas_call | solution.py:594
  477.8 8.6 %shard_map.265 = (bf16[256,1536]{1,0:T(8,128)(2,1)}, bf16[256,1536]{1,0:T(8,128)(2,1)}, bf16[256,1536]{1,0:T(8,128)(2,1)}, bf16[256,1536]{1,0:T(8,128)(2,1)}) custom-call(bf16[1152,1024]{1,0:T(8,128)(2,1)} %get-tuple-element.66.norm_ref.left_ref, bf16[3,1152,1024]{2,1,0:T(8,128)(2,1)} %bitcast.58, bf16[256,1536]{1,0:T(8,128)(2,1)} %copy-done.52, ...), custom_call_target="tpu_custom_call" | custom-call | flops 3623878656 | bytes 14548992 | tf_op jit(solution)/shard_map/pallas_call | solution.py:594
  488.0 10.1 %shard_map.269 = (bf16[256,2048]{1,0:T(8,128)(2,1)}, bf16[256,2048]{1,0:T(8,128)(2,1)}, bf16[256,2048]{1,0:T(8,128)(2,1)}, bf16[256,2048]{1,0:T(8,128)(2,1)}) custom-call(bf16[1152,1024]{1,0:T(8,128)(2,1)} %get-tuple-element.69.second_ref.left_ref, bf16[2,1152,2048]{2,1,0:T(8,128)(2,1)} %get-tuple-element.74.hidden_ref.right_ref, ...), custom_call_target="tpu_custom_call" | custom-call | flops 4831838208 | bytes 19005440 | tf_op jit(solution)/shard_map/pallas_call | solution.py:594
  501.3 10.1 %shard_map.271 = (bf16[256,2048]{1,0:T(8,128)(2,1)}, bf16[256,2048]{1,0:T(8,128)(2,1)}, bf16[256,2048]{1,0:T(8,128)(2,1)}, bf16[256,2048]{1,0:T(8,128)(2,1)}) custom-call(bf16[1152,1024]{1,0:T(8,128)(2,1)} %get-tuple-element.72.final_ref.left_ref, bf16[2,1152,2048]{2,1,0:T(8,128)(2,1)} %get-tuple-element.70.active_ref.right_ref, ...), custom_call_target="tpu_custom_call" | custom-call | flops 4831838208 | bytes 19005440 | tf_op jit(solution)/shard_map/pallas_call | solution.py:594
  512.3 17.0 %collective-permute-done.34 = bf16[2,288,1024]{2,1,0:T(8,128)(2,1)} collective-permute-done((bf16[2,288,1024]{2,1,0:T(8,128)(2,1)}, bf16[2,288,1024]{2,1,0:T(8,128)(2,1)}, u32[]{:S(2)}, u32[]{:S(2)}) %collective-permute-start.34) | collective-permute-done | bytes 1179680 | tf_op jit(solution)/shard_map/ppermute | solution.py:244
  541.4 37.8 %collective-permute-done.67 = bf16[256,2048]{1,0:T(8,128)(2,1)S(1)} collective-permute-done((bf16[256,2048]{1,0:T(8,128)(2,1)}, bf16[256,2048]{1,0:T(8,128)(2,1)S(1)}, u32[]{:S(2)}, u32[]{:S(2)}) %collective-permute-start.67) | collective-permute-done | bytes 1048608 | tf_op jit(solution)/shard_map/ppermute | solution.py:244
  611.3 14.7 %collective-permute-done.76 = bf16[256,2048]{1,0:T(8,128)(2,1)S(1)} collective-permute-done((bf16[256,2048]{1,0:T(8,128)(2,1)S(1)}, bf16[256,2048]{1,0:T(8,128)(2,1)S(1)}, u32[]{:S(2)}, u32[]{:S(2)}) %collective-permute-start.76) | collective-permute-done | bytes 1048608 | tf_op jit(solution)/shard_map/ppermute | solution.py:244
  642.1 9.9 %collective-permute-done.80 = bf16[64,2048]{1,0:T(8,128)(2,1)S(1)} collective-permute-done((bf16[64,2048]{1,0:T(8,128)(2,1)S(1)}, bf16[64,2048]{1,0:T(8,128)(2,1)S(1)}, u32[]{:S(2)}, u32[]{:S(2)}) %collective-permute-start.80) | collective-permute-done | bytes 262176 | tf_op jit(solution)/shard_map/ppermute | solution.py:244
  (362 shorter events, 213.6 us)
Async XLA Ops:
  8.1 53.7 %collective-permute-start.14 = (bf16[64,2048]{1,0:T(8,128)(2,1)}, bf16[64,2048]{1,0:T(8,128)(2,1)}, u32[]{:S(2)}, u32[]{:S(2)}) collective-permute-start(bf16[64,2048]{1,0:T(8,128)(2,1)} %param.26), channel_id=1, source_target_pairs={{0,16},{2,18},{4,20},{6,22},{8,24},{10,26},{12,28},{14,30},{16,0},... | collective-permute-start | bytes 786440 | tf_op jit(solution)/shard_map/ppermute | solution.py:244
  40.0 75.4 %collective-permute-start = (bf16[2,288,1024]{2,1,0:T(8,128)(2,1)}, bf16[2,288,1024]{2,1,0:T(8,128)(2,1)S(1)}, u32[]{:S(2)}, u32[]{:S(2)}) collective-permute-start(bf16[2,288,1024]{2,1,0:T(8,128)(2,1)} %get-tuple-element.159), channel_id=1, source_target_pairs={{0,1},{1,0},{2,3},{3,2},{4,5},{5,4},{6,7},{7,6},{8,9},{9,8},{10,11... | collective-permute-start | bytes 3538952 | tf_op jit(solution)/shard_map/ppermute | solution.py:244
  42.8 74.1 %collective-permute-start.1 = (bf16[2,288,1024]{2,1,0:T(8,128)(2,1)S(1)}, bf16[2,288,1024]{2,1,0:T(8,128)(2,1)S(1)}, u32[]{:S(2)}, u32[]{:S(2)}) collective-permute-start(bf16[2,288,1024]{2,1,0:T(8,128)(2,1)S(1)} %copy-done.4), channel_id=1, source_target_pairs={{0,1},{1,0},{2,3},{3,2},{4,5},{5,4},{6,7},{7,6},{8,9},{9,8},{10,11... | collective-permute-start | bytes 3538952 | tf_op jit(solution)/shard_map/ppermute | solution.py:244
  58.9 58.5 %collective-permute-start.6 = (bf16[256,2048]{1,0:T(8,128)(2,1)S(1)}, bf16[256,2048]{1,0:T(8,128)(2,1)}, u32[]{:S(2)}, u32[]{:S(2)}) collective-permute-start(bf16[256,2048]{1,0:T(8,128)(2,1)S(1)} %pad_maximum_fusion.4.refs_0_.refs_8_), channel_id=1, source_target_pairs={{0,1},{1,0},{2,3},{3,2},{4,5},{5,4},{6,7},{7,6},{8,9},{9,8},{10,11... | collective-permute-start | bytes 3145736 | tf_op jit(solution)/shard_map/ppermute | solution.py:244
  66.6 55.4 %collective-permute-start.27 = (bf16[256,2048]{1,0:T(8,128)(2,1)}, bf16[256,2048]{1,0:T(8,128)(2,1)}, u32[]{:S(2)}, u32[]{:S(2)}) collective-permute-start(bf16[256,2048]{1,0:T(8,128)(2,1)} %constant_dynamic-update-slice_fusion.7.refs_0_), channel_id=1, source_target_pairs={{0,4},{2,6},{4,0},{6,2},{8,12},{10,14},{12,8},{14,10},{16,20},{18,... | collective-permute-start | bytes 3145736 | tf_op jit(solution)/shard_map/ppermute | solution.py:244
  71.8 42.1 %collective-permute-start.2 = (bf16[3072]{0:T(1024)(128)(2,1)S(1)}, bf16[3072]{0:T(1024)(128)(2,1)S(1)}, u32[]{:S(2)}, u32[]{:S(2)}) collective-permute-start(bf16[3072]{0:T(1024)(128)(2,1)S(1)} %constant_dynamic-update-slice_fusion.11), channel_id=1, source_target_pairs={{0,1},{1,0},{2,3},{3,2},{4,5},{5,4},{6,7},{7,6},{8,9},{9,8},{10,11... | collective-permute-start | bytes 18440 | tf_op jit(solution)/shard_map/ppermute | solution.py:244
  115.4 48.7 %collective-permute-start.7 = (bf16[256,2048]{1,0:T(8,128)(2,1)S(1)}, bf16[256,2048]{1,0:T(8,128)(2,1)}, u32[]{:S(2)}, u32[]{:S(2)}) collective-permute-start(bf16[256,2048]{1,0:T(8,128)(2,1)S(1)} %pad_maximum_fusion.4.refs_0_.refs_8_), channel_id=1, source_target_pairs={{0,4},{2,6},{4,0},{6,2},{8,12},{10,14},{12,8},{14,10},{16,20},{18,... | collective-permute-start | bytes 3145736 | tf_op jit(solution)/shard_map/ppermute | solution.py:244
  116.9 47.1 %collective-permute-start.17 = (bf16[256,2048]{1,0:T(8,128)(2,1)}, bf16[256,2048]{1,0:T(8,128)(2,1)}, u32[]{:S(2)}, u32[]{:S(2)}) collective-permute-start(bf16[256,2048]{1,0:T(8,128)(2,1)} %constant_dynamic-update-slice_fusion.3.refs_0_), channel_id=1, source_target_pairs={{0,4},{2,6},{4,0},{6,2},{8,12},{10,14},{12,8},{14,10},{16,20},{18,... | collective-permute-start | bytes 3145736 | tf_op jit(solution)/shard_map/ppermute | solution.py:244
  117.9 63.2 %collective-permute-start.8 = (bf16[256,2048]{1,0:T(8,128)(2,1)}, bf16[256,2048]{1,0:T(8,128)(2,1)}, u32[]{:S(2)}, u32[]{:S(2)}) collective-permute-start(bf16[256,2048]{1,0:T(8,128)(2,1)} %collective-permute-done.6.refs_1_.refs_9_), channel_id=1, source_target_pairs={{0,4},{2,6},{4,0},{6,2},{8,12},{10,14},{12,8},{14,10},{16,20},{18,... | collective-permute-start | bytes 3145736 | tf_op jit(solution)/shard_map/ppermute | solution.py:244
  122.0 65.0 %collective-permute-start.16 = (bf16[256,2048]{1,0:T(8,128)(2,1)}, bf16[256,2048]{1,0:T(8,128)(2,1)}, u32[]{:S(2)}, u32[]{:S(2)}) collective-permute-start(bf16[256,2048]{1,0:T(8,128)(2,1)} %constant_dynamic-update-slice_fusion.3.refs_0_), channel_id=1, source_target_pairs={{0,1},{1,0},{2,3},{3,2},{4,5},{5,4},{6,7},{7,6},{8,9},{9,8},{10,11... | collective-permute-start | bytes 3145736 | tf_op jit(solution)/shard_map/ppermute | solution.py:244
  140.3 57.7 %collective-permute-start.9 = (bf16[256,2048]{1,0:T(8,128)(2,1)S(1)}, bf16[256,2048]{1,0:T(8,128)(2,1)}, u32[]{:S(2)}, u32[]{:S(2)}) collective-permute-start(bf16[256,2048]{1,0:T(8,128)(2,1)S(1)} %pad_maximum_fusion.4.refs_0_.refs_8_), channel_id=1, source_target_pairs={{0,2},{2,0},{4,6},{6,4},{8,10},{10,8},{12,14},{14,12},{16,18},{18,... | collective-permute-start | bytes 3145736 | tf_op jit(solution)/shard_map/ppermute | solution.py:244
  198.0 45.9 %collective-permute-start.19 = (bf16[256,2048]{1,0:T(8,128)(2,1)}, bf16[256,2048]{1,0:T(8,128)(2,1)}, u32[]{:S(2)}, u32[]{:S(2)}) collective-permute-start(bf16[256,2048]{1,0:T(8,128)(2,1)} %constant_dynamic-update-slice_fusion.3.refs_0_), channel_id=1, source_target_pairs={{0,2},{2,0},{4,6},{6,4},{8,10},{10,8},{12,14},{14,12},{16,18},{18,... | collective-permute-start | bytes 3145736 | tf_op jit(solution)/shard_map/ppermute | solution.py:244
  198.3 46.2 %collective-permute-start.21 = (bf16[256,2048]{1,0:T(8,128)(2,1)}, bf16[256,2048]{1,0:T(8,128)(2,1)}, u32[]{:S(2)}, u32[]{:S(2)}) collective-permute-start(bf16[256,2048]{1,0:T(8,128)(2,1)} %collective-permute-done.17.refs_2_), channel_id=1, source_target_pairs={{0,2},{2,0},{4,6},{6,4},{8,10},{10,8},{12,14},{14,12},{16,18},{18,... | collective-permute-start | bytes 3145736 | tf_op jit(solution)/shard_map/ppermute | solution.py:244
  198.6 45.9 %collective-permute-start.28 = (bf16[256,2048]{1,0:T(8,128)(2,1)}, bf16[256,2048]{1,0:T(8,128)(2,1)S(1)}, u32[]{:S(2)}, u32[]{:S(2)}) collective-permute-start(bf16[256,2048]{1,0:T(8,128)(2,1)} %collective-permute-done.26.refs_1_), channel_id=1, source_target_pairs={{0,4},{2,6},{4,0},{6,2},{8,12},{10,14},{12,8},{14,10},{16,20},{18,... | collective-permute-start | bytes 3145736 | tf_op jit(solution)/shard_map/ppermute | solution.py:244
  200.1 44.9 %collective-permute-start.20 = (bf16[256,2048]{1,0:T(8,128)(2,1)}, bf16[256,2048]{1,0:T(8,128)(2,1)}, u32[]{:S(2)}, u32[]{:S(2)}) collective-permute-start(bf16[256,2048]{1,0:T(8,128)(2,1)} %collective-permute-done.16.refs_1_), channel_id=1, source_target_pairs={{0,2},{2,0},{4,6},{6,4},{8,10},{10,8},{12,14},{14,12},{16,18},{18,... | collective-permute-start | bytes 3145736 | tf_op jit(solution)/shard_map/ppermute | solution.py:244
  213.0 40.0 %collective-permute-start.22 = (bf16[256,2048]{1,0:T(8,128)(2,1)}, bf16[256,2048]{1,0:T(8,128)(2,1)}, u32[]{:S(2)}, u32[]{:S(2)}) collective-permute-start(bf16[256,2048]{1,0:T(8,128)(2,1)} %collective-permute-done.18.refs_3_), channel_id=1, source_target_pairs={{0,2},{2,0},{4,6},{6,4},{8,10},{10,8},{12,14},{14,12},{16,18},{18,... | collective-permute-start | bytes 3145736 | tf_op jit(solution)/shard_map/ppermute | solution.py:244
  399.8 50.8 %collective-permute-start.42 = (bf16[256,1536]{1,0:T(8,128)(2,1)}, bf16[256,1536]{1,0:T(8,128)(2,1)S(1)}, u32[]{:S(2)}, u32[]{:S(2)}) collective-permute-start(bf16[256,1536]{1,0:T(8,128)(2,1)} %get-tuple-element.85), channel_id=1, source_target_pairs={{0,2},{2,0},{4,6},{6,4},{8,10},{10,8},{12,14},{14,12},{16,18},{18,... | collective-permute-start | bytes 2359304 | tf_op jit(solution)/shard_map/ppermute | solution.py:244
  400.6 52.4 %collective-permute-start.43 = (bf16[256,1536]{1,0:T(8,128)(2,1)S(1)}, bf16[256,1536]{1,0:T(8,128)(2,1)S(1)}, u32[]{:S(2)}, u32[]{:S(2)}) collective-permute-start(bf16[256,1536]{1,0:T(8,128)(2,1)S(1)} %copy-done.54), channel_id=1, source_target_pairs={{0,2},{2,0},{4,6},{6,4},{8,10},{10,8},{12,14},{14,12},{16,18},{18,... | collective-permute-start | bytes 2359304 | tf_op jit(solution)/shard_map/ppermute | solution.py:244
  476.8 52.6 %collective-permute-start.34 = (bf16[2,288,1024]{2,1,0:T(8,128)(2,1)}, bf16[2,288,1024]{2,1,0:T(8,128)(2,1)}, u32[]{:S(2)}, u32[]{:S(2)}) collective-permute-start(bf16[2,288,1024]{2,1,0:T(8,128)(2,1)} %bitcast.45), channel_id=1, source_target_pairs={{0,1},{1,0},{2,3},{3,2},{4,5},{5,4},{6,7},{7,6},{8,9},{9,8},{10,11... | collective-permute-start | bytes 3538952 | tf_op jit(solution)/shard_map/ppermute | solution.py:244
  498.0 82.7 %collective-permute-start.46 = (bf16[256,1536]{1,0:T(8,128)(2,1)}, bf16[256,1536]{1,0:T(8,128)(2,1)}, u32[]{:S(2)}, u32[]{:S(2)}) collective-permute-start(bf16[256,1536]{1,0:T(8,128)(2,1)} %get-tuple-element.90), channel_id=1, source_target_pairs={{0,4},{2,6},{4,0},{6,2},{8,12},{10,14},{12,8},{14,10},{16,20},{18,... | collective-permute-start | bytes 2359304 | tf_op jit(solution)/shard_map/ppermute | solution.py:244
  500.1 102.2 %collective-permute-start.66 = (bf16[256,2048]{1,0:T(8,128)(2,1)}, bf16[256,2048]{1,0:T(8,128)(2,1)}, u32[]{:S(2)}, u32[]{:S(2)}) collective-permute-start(bf16[256,2048]{1,0:T(8,128)(2,1)} %get-tuple-element.107), channel_id=1, source_target_pairs={{0,4},{2,6},{4,0},{6,2},{8,12},{10,14},{12,8},{14,10},{16,20},{18,... | collective-permute-start | bytes 3145736 | tf_op jit(solution)/shard_map/ppermute | solution.py:244
  511.4 67.9 %collective-permute-start.67 = (bf16[256,2048]{1,0:T(8,128)(2,1)}, bf16[256,2048]{1,0:T(8,128)(2,1)S(1)}, u32[]{:S(2)}, u32[]{:S(2)}) collective-permute-start(bf16[256,2048]{1,0:T(8,128)(2,1)} %get-tuple-element.109), channel_id=1, source_target_pairs={{0,4},{2,6},{4,0},{6,2},{8,12},{10,14},{12,8},{14,10},{16,20},{18,... | collective-permute-start | bytes 3145736 | tf_op jit(solution)/shard_map/ppermute | solution.py:244
  529.3 56.1 %collective-permute-start.77 = (bf16[256,2048]{1,0:T(8,128)(2,1)}, bf16[256,2048]{1,0:T(8,128)(2,1)S(1)}, u32[]{:S(2)}, u32[]{:S(2)}) collective-permute-start(bf16[256,2048]{1,0:T(8,128)(2,1)} %get-tuple-element.117), channel_id=1, source_target_pairs={{0,1},{1,0},{2,3},{3,2},{4,5},{5,4},{6,7},{7,6},{8,9},{9,8},{10,11... | collective-permute-start | bytes 3145736 | tf_op jit(solution)/shard_map/ppermute | solution.py:244
  537.1 43.7 %collective-permute-start.48 = (bf16[256,1536]{1,0:T(8,128)(2,1)S(1)}, bf16[256,1536]{1,0:T(8,128)(2,1)S(1)}, u32[]{:S(2)}, u32[]{:S(2)}) collective-permute-start(bf16[256,1536]{1,0:T(8,128)(2,1)S(1)} %add_convert_fusion.7), channel_id=1, source_target_pairs={{0,1},{1,0},{2,3},{3,2},{4,5},{5,4},{6,7},{7,6},{8,9},{9,8},{10,11... | collective-permute-start | bytes 2359304 | tf_op jit(solution)/shard_map/ppermute | solution.py:244
  (115 other events, 1766.0 us)

commit v3 on v0

--- a/solution.py
+++ b/solution.py
@@ -1,6 +1,8 @@
 import jax
 import jax.numpy as jnp
 from jax import lax
+from jax.experimental import pallas as pl
+from jax.experimental.pallas import tpu as pltpu
 from jax.sharding import PartitionSpec as P
 
 HDIM = 64
@@ -32,7 +34,7 @@
     return jnp.sum(values, axis=(0, 1))
 
 
-def shards(
+def general_shards(
     tokens,
     image_mask,
     out_grad,
@@ -229,6 +231,870 @@
     )
 
 
+ROWS = 64
+PART = 256
+VMEM_BYTES = 60 * 1024 * 1024
+COST_PART = 0.6
+FORWARD_PART = 0.8
+LOG2_E = 1.4426950408889634
+BF16 = jnp.bfloat16
+F32 = jnp.float32
+
+
+def swap(values, axis_name, flip):
+    count = lax.axis_size(axis_name)
+    return lax.ppermute(values, axis_name, [(place, place ^ flip) for place in range(count)])
+
+
+def over_core(values):
+    return swap(values, "dp", 1)
+
+
+def over_y(values):
+    return swap(values, "dp", 2)
+
+
+def over_z(values, step):
+    return swap(values, "dp", 4 * step)
+
+
+def over_x(values):
+    return swap(values, "tensor", 1)
+
+
+def late(values, *marks):
+    return lax.optimization_barrier((values, *marks))[0]
+
+
+def dot_nn(left, right):
+    return lax.dot_general(left, right, (((1,), (0,)), ((), ())), preferred_element_type=F32)
+
+
+def dot_nt(left, right):
+    return lax.dot_general(left, right, (((1,), (1,)), ((), ())), preferred_element_type=F32)
+
+
+def dot_tn(left, right):
+    return lax.dot_general(left, right, (((0,), (0,)), ((), ())), preferred_element_type=F32)
+
+
+def call(
+    kernel, grid, in_specs, out_specs, out_shape, flops, moved, after=(), aliases=None, scalars=0, part=None
+):
+    given, waits = scalars + len(in_specs), len(after)
+    part = COST_PART if part is None else part
+
+    def run(*refs):
+        kernel(*refs[:given], *refs[given + waits :])
+
+    function = pl.pallas_call(
+        run,
+        grid_spec=pltpu.PrefetchScalarGridSpec(
+            num_scalar_prefetch=scalars,
+            grid=grid,
+            in_specs=list(in_specs) + [pl.BlockSpec(memory_space=pl.ANY)] * waits,
+            out_specs=out_specs,
+        ),
+        out_shape=out_shape,
+        input_output_aliases=aliases or {},
+        compiler_params=pltpu.CompilerParams(vmem_limit_bytes=VMEM_BYTES),
+        cost_estimate=pl.CostEstimate(
+            flops=int(flops * part), bytes_accessed=int(moved * part), transcendentals=0
+        ),
+    )
+    return lambda *arrays: function(*arrays, *after)
+
+
+def fixed(*shape, at=None):
+    place = at or (0,) * len(shape)
+    return pl.BlockSpec(shape, lambda *_: place, pipeline_mode=pl.Buffered(1))
+
+
+def far_list(near, far):
+    return list(near) + [far[last].at[y_at] for y_at in range(2) for last in range(2)]
+
+
+def piece_specs(columns, at=0):
+    return [fixed(PART, columns, at=(0, at))] * 4 + [fixed(2, PART, columns, at=(0, 0, at))] * 2
+
+
+def piece_tiles(tile, near=4, far=2):
+    return [pl.BlockSpec((PART, tile), lambda j: (0, j))] * near + [
+        pl.BlockSpec((2, PART, tile), lambda j: (0, 0, j))
+    ] * far
+
+
+def struct(shape, dtype=BF16):
+    return jax.ShapeDtypeStruct(shape, dtype)
+
+
+ANYWHERE = pl.BlockSpec(memory_space=pl.ANY)
+
+
+def normal_parts(values):
+    mean_val = jnp.mean(values, axis=-1, keepdims=True)
+    centered = values - mean_val
+    inv_std = lax.rsqrt(jnp.mean(centered * centered, axis=-1, keepdims=True) + 1e-05)
+    return centered * inv_std, inv_std
+
+
+def column_sum(values):
+    return jnp.sum(values, axis=0, keepdims=True)
+
+
+def combine(arrays, pieces, dtype=BF16, tile=1024, after=()):
+    columns = arrays[0].shape[-1]
+    rows = arrays[0].size // columns // pieces
+    arrays = [values.reshape(pieces, rows, columns) for values in arrays]
+    given = len(arrays)
+
+    def kernel(*refs):
+        for at in range(pieces):
+            parts = [ref[at].astype(F32) for ref in refs[:given]]
+            while len(parts) > 1:
+                parts = [sum(parts[start : start + 2]) for start in range(0, len(parts), 2)]
+            refs[given + at][...] = parts[0].astype(dtype)
+
+    return call(
+        kernel,
+        (columns // tile,),
+        [pl.BlockSpec((pieces, rows, tile), lambda j: (0, 0, j))] * given,
+        [pl.BlockSpec((rows, tile), lambda j: (0, j))] * pieces,
+        [struct((rows, columns), dtype)] * pieces,
+        0,
+        2 * pieces * rows * columns * (given + 1),
+        after,
+    )(*arrays)
+
+
+def first_step():
+    return pl.program_id(0) == 0
+
+
+def setup(places, vectors, after=()):
+    width = vectors[0].shape[1]
+    given = len(vectors)
+
+    def kernel(place_ref, *refs):
+        order_ref = refs[given]
+        source = lax.broadcasted_iota(jnp.int32, (width, width), 0)
+        target = lax.broadcasted_iota(jnp.int32, (width, width), 1)
+        at = target // ROWS
+        z_rel, y_rel, core_rel = at % 4, (at // 4) % 2, at // 8
+        place = (z_rel * 4 + y_rel * 2 + core_rel) ^ place_ref[1]
+        hit = source == place * ROWS + target % ROWS
+        order = jnp.where(hit, 1.0, 0.0).astype(BF16)
+        order_ref[...] = order
+        rows = jnp.concatenate([ref[...].astype(F32) for ref in refs[:given]] + [jnp.zeros((8 - given, width), F32)], axis=0)
+        moved = dot_nn(rows.astype(BF16), order)
+        for vector_at in range(given):
+            refs[given + 1 + vector_at][...] = moved[vector_at : vector_at + 1]
+
+    row = fixed(1, width)
+    return call(
+        kernel,
+        (1,),
+        [row] * given,
+        [fixed(width, width)] + [row] * given,
+        [struct((width, width))] + [struct((1, width), F32)] * given,
+        16 * width * width,
+        2 * width * width,
+        after,
+        None,
+        1,
+        part=FORWARD_PART,
+    )(places, *vectors)
+
+
+def image_block(height, width, offset):
+    return pl.BlockSpec((1, height, width), lambda i, side: (offset(side) + i, 0, 0))
+
+
+def prepare(side, images, order, gain, shift, half_at, before=None, after=()):
+    _, height, width = images.shape
+    mine = 2
+
+    def kernel(side_ref, raw_ref, order_ref, gain_ref, shift_ref, *refs):
+        rows_ref, norm_ref = refs[-2:]
+        rows = dot_nn(raw_ref[0], order_ref[...])
+        rows_ref[...] = rows.astype(BF16)
+        unit, _ = normal_parts(rows)
+        norm_ref[...] = (unit * gain_ref[...] + shift_ref[...]).astype(BF16)
+
+    offset = (lambda side_ref: side_ref[0] * mine) if half_at == 0 else (lambda side_ref: 0)
+    out = pl.BlockSpec((height, width), lambda i, _: (half_at * mine + i, 0))
+    old = () if before is None else before
+    return call(
+        kernel,
+        (mine,),
+        [image_block(height, width, offset), fixed(width, width), fixed(1, width), fixed(1, width)]
+        + [ANYWHERE] * len(old),
+        [out, out],
+        [struct((2 * mine * height, width))] * 2,
+        2 * mine * height * width * width,
+        6 * mine * height * width,
+        after,
+        {5: 0, 6: 1} if old else None,
+        1,
+        part=FORWARD_PART,
+    )(side, images, order, gain, shift, *old)
+
+
+def mask_grad(side, images, order, half_at, before=None, after=()):
+    _, height, width = images.shape
+    mine = 2
+
+    def kernel(side_ref, raw_ref, order_ref, *refs):
+        final_ref, plain_ref, sum_ref = refs[-3:]
+        keep = side_ref[2 + side_ref[0] * mine + pl.program_id(0)].astype(F32)
+        plain = (raw_ref[0].astype(F32) * keep).astype(BF16)
+        plain_ref[...] = plain
+        final = dot_nn(plain, order_ref[...])
+        final_ref[...] = final.astype(BF16)
+
+        @pl.when(first_step())
+        def _():
+            sum_ref[...] = jnp.zeros_like(sum_ref)
+
+        sum_ref[...] += column_sum(final)
+
+    offset = (lambda side_ref: side_ref[0] * mine) if half_at == 0 else (lambda side_ref: 0)
+    old = () if before is None else before
+    out = pl.BlockSpec((height, width), lambda i, _: (half_at * mine + i, 0))
+    return call(
+        kernel,
+        (mine,),
+        [image_block(height, width, offset), fixed(width, width)] + [ANYWHERE] * len(old),
+        [out, out, fixed(1, width)],
+        [struct((2 * mine * height, width))] * 2 + [struct((1, width), F32)],
+        2 * mine * height * width * width,
+        6 * mine * height * width,
+        after,
+        {3: 0, 4: 1} if old else None,
+        1,
+        part=FORWARD_PART,
+    )(side, images, order, *old)
+
+
+def project(normed, parts, bias, after=()):
+    count, width = normed.shape
+    half = bias.shape[-1]
+
+    def kernel(norm_ref, bias_ref, *refs):
+        weight = jnp.concatenate([refs[0][...], refs[1][...], refs[2][0], refs[2][1]], axis=0)
+        refs[3][0] = (dot_nn(norm_ref[...], weight) + bias_ref[0]).astype(BF16)
+
+    return call(
+        kernel,
+        (3,),
+        [fixed(count, width), pl.BlockSpec((1, 1, half), lambda j: (j, 0, 0))]
+        + piece_tiles(half, 2, 1),
+        pl.BlockSpec((1, count, half), lambda j: (j, 0, 0)),
+        struct((3, count, half)),
+        6 * count * width * half,
+        2 * count * (width + 3 * half) + 6 * width * half,
+        after,
+        part=FORWARD_PART,
+    )(normed, bias, *parts)
+
+
+def attend(projected, first_image, last_image, before=None, lanes=256, after=()):
+    _, _, images, half_len, half = projected.shape
+    length = 2 * half_len
+    per_step = lanes // HDIM
+
+    def kernel(proj_ref, *refs):
+        out_ref, probs_ref = refs[-2:]
+        queries, key_rows, value_rows = (proj_ref[at].reshape(length, lanes) for at in range(3))
+        outs = []
+        for head in range(per_step):
+            columns = slice(head * HDIM, (head + 1) * HDIM)
+            scores = dot_nt(queries[:, columns], key_rows[:, columns])
+            top = jnp.max(scores, axis=-1, keepdims=True)
+            raw = jnp.exp2((scores - top) * (LOG2_E * HDIM**-0.5))
+            probs = (raw * (1.0 / jnp.sum(raw, axis=-1, keepdims=True))).astype(BF16)
+            probs_ref[0, head] = probs
+            outs.append(dot_nn(probs, value_rows[:, columns]).astype(BF16))
+        out_ref[...] = jnp.concatenate(outs, axis=1).reshape(out_ref.shape)
+
+    heads = half // HDIM
+    old = () if before is None else before
+    return call(
+        kernel,
+        (last_image - first_image, half // lanes),
+        [pl.BlockSpec((3, 2, 1, half_len, lanes), lambda i, j: (0, 0, first_image + i, 0, j))]
+        + [ANYWHERE] * len(old),
+        [
+            pl.BlockSpec((2, 1, half_len, lanes), lambda i, j: (0, first_image + i, 0, j)),
+            pl.BlockSpec((1, per_step, length, length), lambda i, j: (first_image + i, j, 0, 0)),
+        ],
+        [struct((2, images, half_len, half)), struct((images, heads, length, length))],
+        24 * (last_image - first_image) * heads * length * length * HDIM,
+        (last_image - first_image) * heads * length * length * 2,
+        after,
+        {1: 0, 2: 1} if old else None,
+        part=FORWARD_PART,
+    )(projected, *old)
+
+
+def attend_back(projected, grad_context, probs, lanes=256, after=()):
+    _, _, images, half_len, half = projected.shape
+    length = 2 * half_len
+    per_step = lanes // HDIM
+    scale = HDIM**-0.5
+
+    def kernel(proj_ref, grad_ref, probs_ref, out_ref, sum_ref):
+        queries, key_rows, value_rows = (proj_ref[at].reshape(length, lanes) for at in range(3))
+        grads = grad_ref[...].reshape(length, lanes)
+        found = ([], [], [])
+        for head in range(per_step):
+            columns = slice(head * HDIM, (head + 1) * HDIM)
+            low = probs_ref[0, head]
+            found[2].append(dot_tn(low, grads[:, columns]).astype(BF16))
+            grad_soft = dot_nt(grads[:, columns], value_rows[:, columns])
+            soft = low.astype(F32)
+            scaled = soft * grad_soft
+            grad_scores = (scaled - soft * jnp.sum(scaled, axis=-1, keepdims=True)).astype(BF16)
+            found[0].append((dot_nn(grad_scores, key_rows[:, columns]) * scale).astype(BF16))
+            found[1].append((dot_tn(grad_scores, queries[:, columns]) * scale).astype(BF16))
+        for at in range(3):
+            joined = jnp.concatenate(found[at], axis=1)
+            out_ref[at] = joined.reshape(2, 1, half_len, lanes)
+            if at != 1:
+                sum_ref[0, at // 2 : at // 2 + 1] = column_sum(joined.astype(F32))
+
+    heads = half // HDIM
+    block = pl.BlockSpec((3, 2, 1, half_len, lanes), lambda i, j: (0, 0, i, 0, j))
+    return call(
+        kernel,
+        (images, half // lanes),
+        [
+            block,
+            pl.BlockSpec((2, 1, half_len, lanes), lambda i, j: (0, i, 0, j)),
+            pl.BlockSpec((1, per_step, length, length), lambda i, j: (i, j, 0, 0)),
+        ],
+        [block, pl.BlockSpec((1, 2, lanes), lambda i, j: (i, 0, j))],
+        [struct(projected.shape), struct((images, 2, half), F32)],
+        32 * images * heads * length * length * HDIM,
+        images * heads * length * length * 2,
+        after,
+    )(projected, grad_context, probs)
+
+
+def add_branch(contexts, rows, pieces, bias, gain, shift, tile=288, after=()):
+    count, width = rows.shape
+    half = width // 2
+
+    def kernel(low_ref, high_ref, rows_ref, bias_ref, gain_ref, shift_ref, *refs):
+        parts, (middle_ref, norm_ref) = far_list(refs[:4], refs[4:6]), refs[6:]
+        found = []
+        for at in range(4):
+            found.append(dot_nt(low_ref[...], parts[2 * at][...]) + dot_nt(high_ref[...], parts[2 * at + 1][...]))
+        middle = rows_ref[...].astype(F32) + (jnp.concatenate(found, axis=1) + bias_ref[...])
+        middle_ref[...] = middle
+        unit, _ = normal_parts(middle)
+        norm_ref[...] = (unit * gain_ref[...] + shift_ref[...]).astype(BF16)
+
+    block = pl.BlockSpec((tile, width), lambda i: (i, 0))
+    half_block = pl.BlockSpec((tile, half), lambda i: (i, 0))
+    return call(
+        kernel,
+        (count // tile,),
+        [half_block, half_block, block] + [fixed(1, width)] * 3 + piece_specs(half, 3),
+        [block, block],
+        [struct((count, width), F32), struct((count, width))],
+        2 * count * width * width,
+        10 * count * width + 2 * width * width,
+        after,
+        part=FORWARD_PART,
+    )(*contexts, rows, bias, gain, shift, *pieces)
+
+
+def feed_up(second, parts, bias, tile=512, after=()):
+    count, width = second.shape
+    columns = parts[0].shape[1]
+
+    def kernel(second_ref, bias_ref, *refs):
+        weight = jnp.concatenate([refs[0][...], refs[1][...], refs[2][0], refs[2][1]], axis=0)
+        hidden = dot_nn(second_ref[...], weight) + bias_ref[...]
+        gate = 0.5 + 0.5 * jnp.tanh(0.851 * hidden)
+        refs[3][...] = (hidden * gate).astype(BF16)
+        refs[4][...] = (gate * (1.0 + 1.702 * hidden * (1.0 - gate))).astype(BF16)
+
+    block = pl.BlockSpec((count, tile), lambda j: (0, j))
+    return call(
+        kernel,
+        (columns // tile,),
+        [fixed(count, width), pl.BlockSpec((1, tile), lambda j: (0, j))] + piece_tiles(tile, 2, 1),
+        [block, block],
+        [struct((count, columns))] * 2,
+        2 * count * width * columns,
+        2 * count * (width + 2 * columns) + 2 * width * columns,
+        after,
+        part=FORWARD_PART,
+    )(second, bias, *parts)
+
+
+def feed_down(side, first_tile, last_tile, actives, middle, gathered, bias, order, before=None, tile=288, after=()):
+    count, columns = actives[0].shape
+    width = middle.shape[1]
+    mine = count // tile // 2
+    slices = gathered.shape[0]
+    half_at = first_tile // mine
+    old = () if before is None else (before,)
+
+    def kernel(side_ref, low_ref, high_ref, middle_ref, bias_ref, order_ref, *refs):
+        keep = side_ref[2 + side_ref[0] * mine + first_tile % mine + pl.program_id(0)].astype(F32)
+        parts, out_ref = refs[:2], refs[-1]
+        feed = dot_nt(low_ref[...], parts[0][...].reshape(width, columns))
+        feed = feed + dot_nt(high_ref[...], parts[1][...].reshape(width, columns))
+        middle = middle_ref[...]
+        top = middle.astype(BF16)
+        rest = (middle - top.astype(F32)).astype(BF16)
+        middle = dot_nt(top, order_ref[...]) + dot_nt(rest, order_ref[...])
+        out_ref[0] = ((middle + (feed + bias_ref[...])) * keep).astype(BF16)
+
+    hidden = pl.BlockSpec((tile, columns), lambda i, _: (first_tile + i, 0))
+    offset = (lambda ref: ref[0] * mine + first_tile) if half_at == 0 else (lambda ref: first_tile - mine)
+
+    def weight(x_at):
+        return pl.BlockSpec(
+            (slices, 1, ROWS, columns),
+            lambda i, ref: (0, jnp.bitwise_xor(ref[0], x_at), 0, 0),
+            pipeline_mode=pl.Buffered(1),
+        )
+
+    return call(
+        kernel,
+        (last_tile - first_tile,),
+        [
+            hidden,
+            hidden,
+            pl.BlockSpec((tile, width), lambda i, _: (first_tile + i, 0)),
+            fixed(1, width),
+            fixed(width, width),
+            weight(0),
+            weight(1),
+        ]
+        + [ANYWHERE] * len(old),
+        image_block(tile, width, offset),
+        struct(((2 - half_at) * mine, tile, width)),
+        2 * count * width * columns + count * width * width,
+        2 * count * columns + 3 * count * width + 4 * width * columns,
+        after,
+        {8: 0} if old else None,
+        1,
+    )(side, *actives, middle, bias, order, gathered, gathered, *old)
+
+
+def gate_back(side, plain, slopes, gathered, tile=512, after=()):
+    count, width = plain.shape
+    slices, _, _, columns = gathered.shape
+
+    def kernel(side_ref, plain_ref, low_ref, high_ref, *refs):
+        parts, outs, sums = refs[:2], refs[2:4], refs[4:6]
+        for x_at, slope_ref in enumerate((low_ref, high_ref)):
+            weight = parts[x_at][...].reshape(width, tile)
+            grad = (dot_nn(plain_ref[...], weight) * slope_ref[...].astype(F32)).astype(BF16)
+            outs[x_at][...] = grad
+            sums[x_at][...] = column_sum(grad.astype(F32))
+
+    block = pl.BlockSpec((count, tile), lambda j, _: (0, j))
+    sum_block = pl.BlockSpec((1, tile), lambda j, _: (0, j))
+
+    def weight(x_at):
+        return pl.BlockSpec((slices, 1, ROWS, tile), lambda j, ref: (0, jnp.bitwise_xor(ref[0], x_at), 0, j))
+
+    return call(
+        kernel,
+        (columns // tile,),
+        [fixed(count, width), block, block, weight(0), weight(1)],
+        [block, block, sum_block, sum_block],
+        [struct((count, columns))] * 2 + [struct((1, columns), F32)] * 2,
+        4 * count * width * columns,
+        4 * count * (width + 2 * columns) + 4 * width * columns,
+        after,
+        None,
+        1,
+    )(side, plain, *slopes, gathered, gathered)
+
+
+def sums_down(final, actives, tile=512, after=()):
+    count, width = final.shape
+    columns = actives[0].shape[1]
+
+    def kernel(final_ref, low_ref, high_ref, *outs):
+        for x_at, right_ref in enumerate((low_ref, high_ref)):
+            for core in range(2):
+                for y_at in range(2):
+                    start = (2 * core + y_at) * PART
+                    part = dot_tn(final_ref[:, start : start + PART], right_ref[...]).astype(BF16)
+                    for z_at in range(4):
+                        row = (2 * (z_at % 2) + x_at) * ROWS
+                        outs[core][y_at, z_at // 2, row : row + ROWS, :] = part[z_at * ROWS : (z_at + 1) * ROWS]
+
+    right = pl.BlockSpec((count, tile), lambda j: (0, j))
+    return call(
+        kernel,
+        (columns // tile,),
+        [fixed(count, width), right, right],
+        [pl.BlockSpec((2, 2, PART, tile), lambda j: (0, 0, 0, j))] * 2,
+        [struct((2, 2, PART, columns))] * 2,
+        4 * count * width * columns,
+        4 * count * columns + 2 * count * width + 4 * width * columns,
+        after,
+    )(final, *actives)
+
+
+def sums_up(second, grads, tile=512, after=()):
+    count, width = second.shape
+    columns = grads[0].shape[1]
+
+    def kernel(second_ref, low_ref, high_ref, *outs):
+        for x_at, right_ref in enumerate((low_ref, high_ref)):
+            for core in range(2):
+                for y_at in range(2):
+                    start = (2 * core + y_at) * PART
+                    part = dot_tn(second_ref[:, start : start + PART], right_ref[...])
+                    outs[core][x_at, y_at] = part.astype(BF16)
+
+    right = pl.BlockSpec((count, tile), lambda j: (0, j))
+    return call(
+        kernel,
+        (columns // tile,),
+        [fixed(count, width), right, right],
+        [pl.BlockSpec((2, 2, PART, tile), lambda j: (0, 0, 0, j))] * 2,
+        [struct((2, 2, PART, columns))] * 2,
+        4 * count * width * columns,
+        4 * count * columns + 2 * count * width + 4 * width * columns,
+        after,
+    )(second, *grads)
+
+
+def sums_first(normed, branch, grad_projected, context, after=()):
+    count, width = normed.shape
+    half = context.shape[1]
+
+    def kernel(norm_ref, branch_ref, grad_ref, context_ref, *outs):
+        def work(left_ref, right):
+            for core in range(2):
+                for y_at in range(2):
+                    start = (2 * core + y_at) * PART
+                    outs[core][y_at] = dot_tn(left_ref[:, start : start + PART], right).astype(BF16)
+
+        @pl.when(pl.program_id(0) < 3)
+        def _():
+            work(norm_ref, grad_ref[0])
+
+        @pl.when(pl.program_id(0) == 3)
+        def _():
+            work(branch_ref, context_ref[...])
+
+    left = fixed(count, width)
+    return call(
+        kernel,
+        (4,),
+        [left, left, pl.BlockSpec((1, count, half), lambda j: (jnp.minimum(j, 2), 0, 0)), fixed(count, half)],
+        [pl.BlockSpec((2, PART, half), lambda j: (0, 0, j))] * 2,
+        [struct((2, PART, 4 * half))] * 2,
+        8 * count * width * half,
+        2 * count * (2 * width + 4 * half) + 8 * width * half,
+        after,
+    )(normed, branch, grad_projected, context)
+
+
+def second_back(grads, up_pieces, first_pieces, middle, final, gain, tile=288, after=()):
+    count, columns = grads[0].shape
+    width = middle.shape[1]
+    half = width // 2
+
+    def kernel(low_ref, high_ref, middle_ref, final_ref, gain_ref, *refs):
+        ups, outs = far_list(refs[:4], refs[4:6]), far_list(refs[6:10], refs[10:12])
+        grad_ref, branch_ref, context_low_ref, context_high_ref, sum_ref = refs[12:]
+        found = []
+        for at in range(4):
+            found.append(dot_nt(low_ref[...], ups[2 * at][...]) + dot_nt(high_ref[...], ups[2 * at + 1][...]))
+        grad_second = jnp.concatenate(found, axis=1)
+        unit, inv_std = normal_parts(middle_ref[...])
+        grad_middle = final_ref[...].astype(F32) + normalize_back(
+            grad_second, unit, inv_std, gain_ref[...]
+        )
+        branch = grad_middle.astype(BF16)
+        grad_ref[...] = grad_middle
+        branch_ref[...] = branch
+        for x_at, context_ref in enumerate((context_low_ref, context_high_ref)):
+            weight = jnp.concatenate([outs[2 * at + x_at][...] for at in range(4)], axis=0)
+            context_ref[...] = dot_nn(branch, weight).astype(BF16)
+
+        @pl.when(first_step())
+        def _():
+            sum_ref[...] = jnp.zeros_like(sum_ref)
+
+        sum_ref[0:1] += column_sum(grad_second * unit)
+        sum_ref[1:2] += column_sum(grad_second)
+        sum_ref[2:3] += column_sum(branch.astype(F32))
+
+    block = pl.BlockSpec((tile, width), lambda i: (i, 0))
+    half_block = pl.BlockSpec((tile, half), lambda i: (i, 0))
+    hidden = pl.BlockSpec((tile, columns), lambda i: (i, 0))
+    return call(
+        kernel,
+        (count // tile,),
+        [hidden, hidden, block, block, fixed(1, width)]
+        + piece_specs(columns)
+        + piece_specs(half, 3),
+        [block, block, half_block, half_block, fixed(8, width)],
+        [struct((count, width), F32), struct((count, width))]
+        + [struct((count, half))] * 2
+        + [struct((8, width), F32)],
+        4 * count * width * columns + 2 * count * width * width,
+        4 * count * columns + 14 * count * width + 4 * width * columns,
+        after,
+    )(*grads, middle, final, gain, *up_pieces, *first_pieces)
+
+
+def first_back(side, half_at, grads, pieces, rows, grad_middle, gain, order, tile=288, after=()):
+    _, count, half = grads[0].shape
+    width = rows.shape[1]
+    mine = count // tile // 2
+
+    def kernel(side_ref, low_ref, high_ref, rows_ref, middle_ref, gain_ref, order_ref, *refs):
+        parts, (out_ref, sum_ref) = far_list(refs[:4], refs[4:6]), refs[6:]
+        lefts = [jnp.concatenate([ref[at] for at in range(3)], axis=1) for ref in (low_ref, high_ref)]
+        found = []
+        for at in range(4):
+            found.append(
+                dot_nt(lefts[0], parts[2 * at][...]) + dot_nt(lefts[1], parts[2 * at + 1][...])
+            )
+        grad_normed = jnp.concatenate(found, axis=1)
+        unit, inv_std = normal_parts(rows_ref[...].astype(F32))
+        out = middle_ref[...] + normalize_back(grad_normed, unit, inv_std, gain_ref[...])
+        out_ref[0] = dot_nt(out.astype(BF16), order_ref[...]).astype(BF16)
+
+        @pl.when(first_step())
+        def _():
+            sum_ref[...] = jnp.zeros_like(sum_ref)
+
+        sum_ref[0:1] += column_sum(grad_normed * unit)
+        sum_ref[1:2] += column_sum(grad_normed)
+
+    start = half_at * mine
+    block = pl.BlockSpec((tile, width), lambda i, _: (start + i, 0))
+    grad_block = pl.BlockSpec((3, tile, half), lambda i, _: (0, start + i, 0))
+    offset = (lambda ref: ref[0] * mine) if half_at == 0 else (lambda ref: 0)
+    return call(
+        kernel,
+        (mine,),
+        [grad_block, grad_block, block, block, fixed(1, width), fixed(width, width)]
+        + piece_specs(3 * half),
+        [image_block(tile, width, offset), fixed(8, width)],
+        [struct(((2 - half_at) * mine, tile, width)), struct((8, width), F32)],
+        4 * count * width * width,
+        8 * count * width + 6 * width * width,
+        after,
+        None,
+        1,
+    )(side, *grads, rows, grad_middle, gain, order, *pieces)
+
+
+def fast_shards(
+    tokens,
+    image_mask,
+    out_grad,
+    norm1_gain,
+    norm1_shift,
+    qkv_weight,
+    qv_bias,
+    out_weight,
+    out_bias,
+    norm2_gain,
+    norm2_shift,
+    up_weight,
+    up_bias,
+    down_weight,
+    down_bias,
+):
+    images, half_len, width = tokens.shape
+    mine = images // 2
+    half = qkv_weight.shape[2]
+    half_hidden = up_weight.shape[1]
+    count = 2 * mine * half_len
+    me = lax.axis_index("dp")
+    side = lax.axis_index("tensor")
+    side_array = jnp.concatenate([jnp.stack([side, me]).astype(jnp.int32), image_mask])
+    biases = jnp.concatenate([qv_bias.reshape(-1), up_bias])
+    bias_rows = jnp.pad(biases, (0, 16 * half_hidden - biases.size)).reshape(16, half_hidden)
+
+    def split_bias(bias):
+        bias = bias.astype(F32)
+        parts = jnp.stack([bias[:half], jnp.zeros((half,), F32), bias[half : 2 * half]])
+        return parts[:, None], bias[None, 2 * half :]
+
+    vectors = (norm1_gain, norm1_shift, norm2_gain, norm2_shift, out_bias)
+    bias_down = down_bias.astype(F32).reshape(1, width)
+    order, gain_one, shift_one, gain_two, shift_two, bias_out = setup(
+        side_array, [vector.reshape(1, width) for vector in vectors]
+    )
+
+    def for_partner(values):
+        return over_x(lax.dynamic_slice_in_dim(values, (1 - side) * mine, mine, 0))
+
+    def from_partner(values, send):
+        return lax.dynamic_update_slice_in_dim(values, over_x(send), (1 - side) * mine, 0)
+
+    def z_all(values):
+        return jnp.concatenate([values] + [over_z(values, step) for step in (1, 2, 3)], axis=0)
+
+    own = prepare(side_array, tokens, order, gain_one, shift_one, 0)
+    *final, sum_own = mask_grad(side_array, out_grad, order, 0, after=own[:1])
+    tokens_partner = for_partner(tokens)
+    first = jnp.concatenate([qkv_weight.reshape(ROWS, 3 * half), out_weight], axis=1)
+    first_base = late(z_all(first), final[0])
+    down_all = lax.all_gather(late(down_weight, first_base), ("dp", "tensor"))
+    down_all = down_all.reshape(-1, 2, ROWS, half_hidden)
+    first_x = over_x(jnp.concatenate([late(first_base, tokens_partner), bias_rows], axis=0))
+    rows, normed = prepare(
+        side_array, tokens_partner, order, gain_one, shift_one, 1, own, after=[first_base]
+    )
+    first_y = over_y(late(first_base, normed))
+    up_base = z_all(late(up_weight, first_base))
+    first_xy = over_y(late(first_x, first_y))
+    first_far = [over_core(jnp.stack(late([first_base, first_y], first_x, up_base)))]
+    up_x = over_x(late(up_base, first_x))
+    grad_partner = for_partner(late(out_grad, up_x))
+
+    biases = [split_bias(biases), split_bias(first_x[4 * ROWS :].reshape(-1)[: biases.size])]
+    heads_shape = (3, 2, mine, half_len, half)
+    projected, contexts, probs = [None, None], [None, None], [None, None]
+    projected[0] = project(
+        normed, [first_base, first_y] + first_far, biases[0][0]
+    ).reshape(heads_shape)
+    begun = attend(projected[0], 0, 1, lanes=128)
+    first_far += [over_core(jnp.stack(late([first_x, first_xy], begun[0])))]
+    first_pieces = [first_base, first_x, first_y, first_xy] + first_far
+    up_y = over_y(late(up_base, first_xy))
+    contexts[0], probs[0] = attend(projected[0], 1, 2, begun, lanes=128)
+    projected[1] = project(
+        normed, [first_x, first_xy] + first_far[1:], biases[1][0], after=[contexts[0], up_x]
+    ).reshape(heads_shape)
+    contexts[1], probs[1] = attend(projected[1], 0, 2, after=[up_y])
+    contexts = [values.reshape(count, half) for values in contexts]
+
+    up_xy = over_y(late(up_x, up_y, contexts[1]))
+    up_far = [over_core(jnp.stack(late([up_base, up_y], contexts[1])))]
+    middle, second = add_branch(
+        contexts, rows, first_pieces, bias_out, gain_two, shift_two
+    )
+    actives, slopes = [None, None], [None, None]
+    actives[0], slopes[0] = feed_up(second, [up_base, up_y] + up_far, biases[0][1], after=[grad_partner])
+    *final, sum_partner = mask_grad(side_array, grad_partner, order, 1, final, after=[actives[0]])
+    up_far += [over_core(jnp.stack(late([up_x, up_xy], actives[0])))]
+    up_pieces = [up_base, up_x, up_y, up_xy] + up_far
+    actives[1], slopes[1] = feed_up(second, [up_x, up_xy] + up_far[1:], biases[1][1], after=final[:1])
+
+    final, plain = final
+    down_sums, down_sent = sums_down(final, actives)
+    down_sent = over_core(down_sent)
+    grads_sums = gate_back(side_array, plain, slopes, down_all, after=[down_sums])
+    grads, sum_hidden = grads_sums[:2], grads_sums[2:]
+    down_sums = combine([down_sums, down_sent], 2, after=grads[:1])
+    down_sent = over_y(down_sums[1])
+    up_sums, up_sent = sums_up(second, grads, after=down_sums[:1])
+    up_sent = over_core(up_sent)
+    grad_middle, branch, *grad_contexts, sums_two = second_back(
+        grads, up_pieces, first_pieces, middle, final, gain_two, after=[up_sums]
+    )
+    up_sums = combine([up_sums, up_sent], 2, after=[branch])
+    up_sent = over_x(up_sums[1])
+
+    def heads_back(x_at, after):
+        grad_context = grad_contexts[x_at].reshape(2, mine, half_len, half)
+        grad, sums = attend_back(projected[x_at], grad_context, probs[x_at], after=after)
+        return grad.reshape(3, count, half), jnp.sum(sums, axis=0)
+
+    grads_qkv, sums_qkv = [None, None], [None, None]
+    grads_qkv[1], sums_qkv[1] = heads_back(1, up_sums[:1])
+    down_sums = combine([down_sums[0], down_sent], 2, after=[grads_qkv[1]])
+    down_sent = over_z(down_sums[1], 2)
+    high, high_sent = sums_first(normed, branch, grads_qkv[1], contexts[1], after=down_sums[:1])
+    high_sent = over_core(high_sent)
+    out_send = feed_down(side_array, 2, 4, actives, middle, down_all, bias_down, order, after=[high])
+    high = combine([high, high_sent], 2, after=[out_send])
+    high_sent = over_y(high[1])
+    grads_qkv[0], sums_qkv[0] = heads_back(0, high[:1])
+    up_sums = combine([up_sums[0], up_sent], 2, after=[grads_qkv[0]])
+    up_sent = over_y(up_sums[1])
+    (high,) = combine([high[0], high_sent], 1, after=up_sums[:1])
+    high_sent = over_x(high)
+    down_sums = combine([down_sums[0], down_sent], 2, after=[high])
+    down_sent = over_z(down_sums[1], 1)
+    low, low_sent = sums_first(normed, branch, grads_qkv[0], contexts[0], after=down_sums[:1])
+    low = combine([low, over_core(low_sent)], 2)
+    low_sent = over_y(low[1])
+    send, sums_partner = first_back(
+        side_array, 1, grads_qkv, first_pieces, rows, grad_middle, gain_one, order, after=low[:1]
+    )
+    full, sums_own = first_back(
+        side_array, 0, grads_qkv, first_pieces, rows, grad_middle, gain_one, order, after=[send]
+    )
+    up_sums = combine([up_sums[0], up_sent], 2, after=[full])
+    up_sent = over_z(up_sums[1], 2)
+    low = combine([low[0], low_sent, high_sent], 4, after=up_sums[:1])
+    low_sent = [over_z(low[step], step) for step in (1, 2, 3)]
+    down_sums = combine([down_sums[0], down_sent], 2, after=low[:1])
+    down_sent = over_x(down_sums[1])
+    out_begun = feed_down(
+        side_array, 0, 1, actives, middle, down_all, bias_down, order, after=down_sums[:1]
+    )
+    tokens_grad = from_partner(full, send)
+    up_sums = combine([up_sums[0], up_sent], 2, after=[out_begun])
+    up_sent = over_z(up_sums[1], 1)
+    out_full = feed_down(
+        side_array, 1, 2, actives, middle, down_all, bias_down, order, out_begun, after=[tokens_grad, up_sums[0]]
+    )
+    (grad_down,) = combine([down_sums[0], down_sent], 1, F32, after=[out_full])
+    block_out = from_partner(out_full, out_send)
+    (grad_up,) = combine([up_sums[0], up_sent], 1, F32, after=[grad_down])
+    (grad_first,) = combine([low[0]] + low_sent, 1, F32, after=[grad_up, tokens_grad])
+
+    sums = jnp.concatenate(
+        [(sums_own + sums_partner)[:2], sums_two[2:3], sums_two[:2], sum_own + sum_partner], axis=0
+    )
+    sums = jnp.einsum("td,od->to", sums, order.astype(F32), precision=lax.Precision.HIGHEST)
+    halves = [
+        jnp.concatenate([sums_qkv[x_at].reshape(-1), sum_hidden[x_at][0]]) for x_at in range(2)
+    ]
+    small = jnp.concatenate([halves[0], sums.reshape(-1), halves[1]])
+    small = small + over_core(small)
+    small = late(small, out_begun)
+    small = small + over_y(small)
+    small = late(small, out_full)
+    small = (small + over_z(small, 1)) + (over_z(small, 2) + over_z(small, 3))
+    halves_size = 2 * half + half_hidden
+    small = late(small, grad_first)
+    small = small[:-halves_size] + over_x(
+        jnp.concatenate([small[-halves_size:], small[halves_size:-halves_size]])
+    )
+    halves = small[:halves_size]
+    sums = small[halves_size:].reshape(6, width)
+    return (
+        block_out,
+        tokens_grad,
+        sums[0],
+        sums[1],
+        grad_first[:, : 3 * half].reshape(ROWS, 3, half),
+        halves[: 2 * half].reshape(2, half),
+        grad_first[:, 3 * half :],
+        sums[2],
+        sums[3],
+        sums[4],
+        grad_up,
+        halves[2 * half :],
+        grad_down,
+        sums[5],
+    )
+
+
 def solution(mesh):
     in_specs = (
         P("dp", "tensor", None),
@@ -263,4 +1129,6 @@
         P("dp", "tensor"),
         P(),
     )
+    small_slice = mesh.shape["dp"] == 16 and mesh.shape["tensor"] == 2
+    shards = fast_shards if small_slice else general_shards
     return jax.shard_map(shards, mesh=mesh, in_specs=in_specs, out_specs=out_specs, check_vma=False)

time: 1210 us -> 582 us (0.48)
  waiting for transfers between devices: 598 us -> 123 us
  Pallas kernels: 0 us -> 347 us
  matrix products: 310 us -> 1.72 us
  blocking collectives: 103 us -> 0 us
  other arithmetic: 112 us -> 11.8 us
  starting transfers between devices: 1.97 us -> 44.7 us
  local copies, waits for them, and re-layouts: 59 us -> 29.9 us
    pallas_call x0 -> x41, Pallas kernels: none -> 347 us  [call(): return lambda *arrays: function(*arrays, *after)]
    all_gather x12 -> x1, waiting for transfers between devices: 327 us -> 0.01 us  [fast_shards(): down_all = lax.all_gather(late(down_weight, first_base), ('dp', 'tensor'))]
    dot_general x36 -> x1, matrix products: 310 us -> 1.72 us  [fast_shards(): jnp.einsum('td,od->to', sums, order.astype(F32), precision=lax.Precision....]
    reduce_scatter x12 -> x0, waiting for transfers between devices: 266 us -> none  [the longest x2 103 us: shards(): lax.psum_scatter(second_terms, 'tensor', scatter_dimension=1, tiled=True)]
    ppermute x0 -> x44, waiting for transfers between devices: none -> 123 us  [swap(): lax.ppermute(values, axis_name, [(place, place ^ flip) for place in range...]
    psum x2 -> x0, blocking collectives: 103 us -> none  [the longest x1 62 us: shards(): grad_pair, grad_up_bias = lax.psum((grad_pair, grad_up_bias), 'dp')]
    convert_element_type x22 -> x1, other arithmetic: 59.2 us -> 0.01 us  [split_bias(): bias = bias.astype(F32)]
    ppermute x0 -> x44, starting transfers between devices: none -> 44.7 us  [swap(): lax.ppermute(values, axis_name, [(place, place ^ flip) for place in range...]
  transfers between devices with their start and end apart: 24 -> 45, of which waited for: 16 -> 15; matrix products, arithmetic and copies ran while one was open for 37% -> 5% of each run, Pallas kernels for 0% -> 52%
where the time goes in v3:
time: 582 us; the launch traced here: 573 us
  Pallas kernels  347 us (60%)
  waiting for transfers between devices  123 us (21%)
  starting transfers between devices  44.7 us (8%)
  local copies, waits for them, and re-layouts  29.9 us (5%)
  between operations  15.1 us (3%)
  other arithmetic  11.8 us (2%)
    pallas_call x41, Pallas kernels, call(): return lambda *arrays: function(*arrays, *after)  347 us
    ppermute x44, waiting for transfers between devices, swap(): lax.ppermute(values, axis_name, [(place, place ^ flip) for place in range...  123 us
    ppermute x44, starting transfers between devices, swap(): lax.ppermute(values, axis_name, [(place, place ^ flip) for place in range...  44.7 us
    unnamed x104, local copies, waits for them, and re-layouts  13.4 us
  transfers between devices with their start and end apart: 45, of which 15 were waited for; matrix products, arithmetic and copies ran while one was open for 5% of the time, Pallas kernels for 52%

profile of v3, /device:TPU:0, one launch (start us, length us, event | category | flops | bytes accessed | tf_op | source)
XLA Modules:
  0.0 572.6 jit_solution(4239579733882718328)
XLA Ops:
  56.9 22.2 %collective-permute-done.7 = bf16[64,2048]{1,0:T(8,128)(2,1)S(1)} collective-permute-done((bf16[64,2048]{1,0:T(8,128)(2,1)S(1)}, bf16[64,2048]{1,0:T(8,128)(2,1)S(1)}, u32[]{:S(2)}, u32[]{:S(2)}) %collective-permute-start.7) | collective-permute-done | bytes 262176 | tf_op jit(solution)/shard_map/ppermute | solution.py:246
  94.4 10.1 %shard_map.259 = (bf16[2,2,288,512]{3,2,1,0:T(8,128)(2,1)}, bf16[2,8,576,576]{3,2,1,0:T(8,128)(2,1)}) custom-call(bf16[3,2,2,288,512]{4,3,2,1,0:T(8,128)(2,1)} %bitcast.105), custom_call_target="tpu_custom_call" | custom-call | flops 3261490688 | bytes 4246732 | tf_op jit(solution)/shard_map/pallas_call | solution.py:305
  104.5 13.5 %collective-permute-done.10.refs_3_.refs_9_.refs_14_.refs_10_ = bf16[272,2048]{1,0:T(8,128)(2,1)S(1)} collective-permute-done((bf16[272,2048]{1,0:T(8,128)(2,1)S(1)}, bf16[272,2048]{1,0:T(8,128)(2,1)S(1)}, u32[]{:S(2)}, u32[]{:S(2)}) %collective-permute-start.10) | collective-permute-done | bytes 1114144 | tf_op jit(solution)/shard_map/ppermute | solution.py:246
  121.2 10.2 %shard_map.260 = (bf16[2,2,288,512]{3,2,1,0:T(8,128)(2,1)}, bf16[2,8,576,576]{3,2,1,0:T(8,128)(2,1)}) custom-call(bf16[3,2,2,288,512]{4,3,2,1,0:T(8,128)(2,1)} %bitcast.106, bf16[2,2,288,512]{3,2,1,0:T(8,128)(2,1)} %get-tuple-element.125.refs_1_, bf16[2,8,576,576]{3,2,1,0:T(8,128)(2,1)} %get-tuple-element.126.refs_2_), custom_call_target="tpu_custom_call", output_to_operand_aliasing={{0}: (1, {}), {1}: (2, {})} | custom-call | flops 3261490688 | bytes 4246732 | tf_op jit(solution)/shard_map/pallas_call | solution.py:305
  131.4 14.4 %collective-permute-done.12.refs_6_.refs_2_ = bf16[256,2048]{1,0:T(8,128)(2,1)S(1)} collective-permute-done((bf16[256,2048]{1,0:T(8,128)(2,1)}, bf16[256,2048]{1,0:T(8,128)(2,1)S(1)}, u32[]{:S(2)}, u32[]{:S(2)}) %collective-permute-start.12) | collective-permute-done | bytes 1048608 | tf_op jit(solution)/shard_map/ppermute | solution.py:246
  155.0 17.2 %shard_map.262 = (bf16[2,2,288,512]{3,2,1,0:T(8,128)(2,1)}, bf16[2,8,576,576]{3,2,1,0:T(8,128)(2,1)}) custom-call(bf16[3,2,2,288,512]{4,3,2,1,0:T(8,128)(2,1)} %bitcast.103, bf16[256,2048]{1,0:T(8,128)(2,1)} %collective-permute-done.13.refs_1_.refs_3_.refs_7_), custom_call_target="tpu_custom_call" | custom-call | flops 6522981376 | bytes 8493465 | tf_op jit(solution)/shard_map/pallas_call | solution.py:305
  187.2 18.0 %collective-permute-done.15.refs_5_.refs_1_ = bf16[2,288,1024]{2,1,0:T(8,128)(2,1)S(1)} collective-permute-done((bf16[2,288,1024]{2,1,0:T(8,128)(2,1)}, bf16[2,288,1024]{2,1,0:T(8,128)(2,1)S(1)}, u32[]{:S(2)}, u32[]{:S(2)}) %collective-permute-start.15) | collective-permute-done | bytes 1179680 | tf_op jit(solution)/shard_map/ppermute | solution.py:246
  206.1 12.3 %shard_map.264 = (bf16[1152,2048]{1,0:T(8,128)(2,1)}, bf16[1152,2048]{1,0:T(8,128)(2,1)}) custom-call(bf16[1152,1024]{1,0:T(8,128)(2,1)} %get-tuple-element.138.refs_0_, f32[1,2048]{1,0:T(1,128)} %bitcast.141, bf16[256,2048]{1,0:T(8,128)(2,1)} %constant_dynamic-update-slice_fusion.3.refs_2_.refs_5_, ...), custom_call_target="tpu_custom_call" | custom-call | flops 3865470464 | bytes 12792627 | tf_op jit(solution)/shard_map/pallas_call | solution.py:305
  225.8 12.3 %shard_map.266 = (bf16[1152,2048]{1,0:T(8,128)(2,1)}, bf16[1152,2048]{1,0:T(8,128)(2,1)}) custom-call(bf16[1152,1024]{1,0:T(8,128)(2,1)} %get-tuple-element.138.refs_0_, f32[1,2048]{1,0:T(1,128)} %bitcast.142, bf16[256,2048]{1,0:T(8,128)(2,1)} %copy-done.10, bf16[256,2048]{1,0:T(8,128)(2,1)} %copy-done.15, ...), custom_call_target="tpu_custom_call" | custom-call | flops 3865470464 | bytes 12792627 | tf_op jit(solution)/shard_map/pallas_call | solution.py:305
  238.1 15.2 %shard_map.267 = (bf16[2,2,256,2048]{3,2,1,0:T(8,128)(2,1)}, bf16[2,2,256,2048]{3,2,1,0:T(8,128)(2,1)}) custom-call(bf16[1152,1024]{1,0:T(8,128)(2,1)} %get-tuple-element.147.refs_5_.refs_0_.refs_3_, bf16[1152,2048]{1,0:T(8,128)(2,1)} %get-tuple-element.142.refs_5_.refs_1_, bf16[1152,2048]{1,0:T(8,128)(2,1)} %get-tuple-element.148.refs_2_), custom_call_target="tpu_custom_call" | custom-call | flops 5798205952 | bytes 12111052 | tf_op jit(solution)/shard_map/pallas_call | solution.py:305
  253.8 17.3 %shard_map.268 = (bf16[1152,2048]{1,0:T(8,128)(2,1)}, bf16[1152,2048]{1,0:T(8,128)(2,1)}, f32[1,2048]{1,0:T(1,128)}, f32[1,2048]{1,0:T(1,128)}) custom-call(s32[6]{0:T(128)} %pad_add_fusion.refs_0_, bf16[1152,1024]{1,0:T(8,128)(2,1)} %get-tuple-element.153.refs_1_, bf16[1152,2048]{1,0:T(8,128)(2,1)} %get-tuple-element.154.refs_2_, ...), custom_call_target="tpu_custom_call" | custom-call | flops 5798205952 | bytes 19188940 | tf_op jit(solution)/shard_map/pallas_call | solution.py:305
  276.4 15.2 %shard_map.270 = (bf16[2,2,256,2048]{3,2,1,0:T(8,128)(2,1)}, bf16[2,2,256,2048]{3,2,1,0:T(8,128)(2,1)}) custom-call(bf16[1152,1024]{1,0:T(8,128)(2,1)} %get-tuple-element.138.refs_0_, bf16[1152,2048]{1,0:T(8,128)(2,1)} %get-tuple-element.156.refs_2_.refs_1_.refs_0_, bf16[1152,2048]{1,0:T(8,128)(2,1)} %get-tuple-element.159.refs_2_.refs_1_, ...), custom_call_target="tpu_custom_call" | custom-call | flops 5798205952 | bytes 12111052 | tf_op jit(solution)/shard_map/pallas_call | solution.py:305
  293.1 22.2 %shard_map.271 = (f32[1152,1024]{1,0:T(8,128)}, bf16[1152,1024]{1,0:T(8,128)(2,1)}, bf16[1152,512]{1,0:T(8,128)(2,1)}, bf16[1152,512]{1,0:T(8,128)(2,1)}, f32[8,1024]{1,0:T(8,128)}) custom-call(bf16[1152,2048]{1,0:T(8,128)(2,1)} %get-tuple-element.156.refs_2_.refs_1_.refs_0_, bf16[1152,2048]{1,0:T(8,128)(2,1)} %get-tuple-element.159.refs_2_.refs_1_, ...), custom_call_target="tpu_custom_call" | custom-call | flops 7247757312 | bytes 20604518 | tf_op jit(solution)/shard_map/pallas_call | solution.py:305
  320.5 21.1 %shard_map.273 = (bf16[3,2,2,288,512]{4,3,2,1,0:T(8,128)(2,1)}, f32[2,2,512]{2,1,0:T(2,128)}) custom-call(bf16[3,2,2,288,512]{4,3,2,1,0:T(8,128)(2,1)} %bitcast.104, bf16[2,2,288,512]{3,2,1,0:T(8,128)(2,1)} %bitcast.150, bf16[2,8,576,576]{3,2,1,0:T(8,128)(2,1)} %get-tuple-element.162.refs_2_, bf16[512,2048]{1,0:T(8,128)(2,1)} %get-tuple-element.165.refs_3_), custom_call_target="tpu_custom_call" | custom-call | flops 6522981376 | bytes 6370099 | tf_op jit(solution)/shard_map/pallas_call | solution.py:305
  346.3 10.5 %shard_map.275 = (bf16[2,256,2048]{2,1,0:T(8,128)(2,1)}, bf16[2,256,2048]{2,1,0:T(8,128)(2,1)}) custom-call(bf16[1152,1024]{1,0:T(8,128)(2,1)} %get-tuple-element.119.refs_0_, bf16[1152,1024]{1,0:T(8,128)(2,1)} %get-tuple-element.164.refs_2_.refs_1_, bf16[3,1152,512]{2,1,0:T(8,128)(2,1)} %bitcast.88, bf16[1152,512]{1,0:T(8,128)(2,1)} %bitcast.115, ...), custom_call_target="tpu_custom_call" | custom-call | flops 2899102976 | bytes 8178892 | tf_op jit(solution)/shard_map/pallas_call | solution.py:305
  358.2 14.4 %shard_map.276.refs_2_ = bf16[2,288,1024]{2,1,0:T(8,128)(2,1)} custom-call(s32[6]{0:T(128)} %pad_add_fusion.refs_0_, bf16[1152,2048]{1,0:T(8,128)(2,1)} %get-tuple-element.142.refs_5_.refs_1_, bf16[1152,2048]{1,0:T(8,128)(2,1)} %get-tuple-element.148.refs_2_, f32[1152,1024]{1,0:T(8,128)} %get-tuple-element.149.refs_2_.refs_3_, f32[1,1024]{1,0:T(1,128)} %bitcast.132, ...), custom_call_target="tpu_custom_call" | custom-call | flops 3623878656 | bytes 9987686 | tf_op jit(solution)/shard_map/pallas_call | solution.py:305
  378.9 21.1 %shard_map.278 = (bf16[3,2,2,288,512]{4,3,2,1,0:T(8,128)(2,1)}, f32[2,2,512]{2,1,0:T(2,128)}) custom-call(bf16[3,2,2,288,512]{4,3,2,1,0:T(8,128)(2,1)} %bitcast.107, bf16[2,2,288,512]{3,2,1,0:T(8,128)(2,1)} %bitcast.149, bf16[2,8,576,576]{3,2,1,0:T(8,128)(2,1)} %get-tuple-element.175.refs_2_, bf16[256,2048]{1,0:T(8,128)(2,1)} %get-tuple-element.171.refs_3_), custom_call_target="tpu_custom_call" | custom-call | flops 6522981376 | bytes 6370099 | tf_op jit(solution)/shard_map/pallas_call | solution.py:305
  412.2 12.4 %collective-permute-done.21 = bf16[256,2048]{1,0:T(8,128)(2,1)S(1)} collective-permute-done((bf16[256,2048]{1,0:T(8,128)(2,1)}, bf16[256,2048]{1,0:T(8,128)(2,1)S(1)}, u32[]{:S(2)}, u32[]{:S(2)}) %collective-permute-start.21) | collective-permute-done | bytes 1048608 | tf_op jit(solution)/shard_map/ppermute | solution.py:246
  428.0 10.5 %shard_map.282 = (bf16[2,256,2048]{2,1,0:T(8,128)(2,1)}, bf16[2,256,2048]{2,1,0:T(8,128)(2,1)}) custom-call(bf16[1152,1024]{1,0:T(8,128)(2,1)} %get-tuple-element.119.refs_0_, bf16[1152,1024]{1,0:T(8,128)(2,1)} %get-tuple-element.164.refs_2_.refs_1_, bf16[3,1152,512]{2,1,0:T(8,128)(2,1)} %bitcast.92, bf16[1152,512]{1,0:T(8,128)(2,1)} %bitcast.98, ...), custom_call_target="tpu_custom_call" | custom-call | flops 2899102976 | bytes 8178892 | tf_op jit(solution)/shard_map/pallas_call | solution.py:305
  449.4 12.2 %shard_map.284 = (bf16[2,288,1024]{2,1,0:T(8,128)(2,1)}, f32[8,1024]{1,0:T(8,128)}) custom-call(s32[6]{0:T(128)} %pad_add_fusion.refs_0_, bf16[3,1152,512]{2,1,0:T(8,128)(2,1)} %bitcast.93, bf16[3,1152,512]{2,1,0:T(8,128)(2,1)} %bitcast.89, bf16[1152,1024]{1,0:T(8,128)(2,1)} %get-tuple-element.134.refs_2_.refs_3_, f32[1152,1024]{1,0:T(8,128)} %get-tuple-element.185.refs_4_, ...), custom_call_target="tpu_custom_call" | custom-call | flops 2899102976 | bytes 9437184 | tf_op jit(solution)/shard_map/pallas_call | solution.py:305
  463.1 12.6 %shard_map.285 = (bf16[4,288,1024]{2,1,0:T(8,128)(2,1)}, f32[8,1024]{1,0:T(8,128)}) custom-call(s32[6]{0:T(128)} %pad_add_fusion.refs_0_, bf16[3,1152,512]{2,1,0:T(8,128)(2,1)} %bitcast.94, bf16[3,1152,512]{2,1,0:T(8,128)(2,1)} %bitcast.90, bf16[1152,1024]{1,0:T(8,128)(2,1)} %get-tuple-element.134.refs_2_.refs_3_, f32[1152,1024]{1,0:T(8,128)} %get-tuple-element.185.refs_4_, ...), custom_call_target="tpu_custom_call" | custom-call | flops 2899102976 | bytes 9437184 | tf_op jit(solution)/shard_map/pallas_call | solution.py:305
  493.3 10.6 %shard_map.289.refs_2_.refs_8_ = bf16[4,288,1024]{2,1,0:T(8,128)(2,1)} custom-call(s32[6]{0:T(128)} %pad_add_fusion.refs_0_, bf16[1152,2048]{1,0:T(8,128)(2,1)} %get-tuple-element.142.refs_5_.refs_1_, bf16[1152,2048]{1,0:T(8,128)(2,1)} %get-tuple-element.148.refs_2_, f32[1152,1024]{1,0:T(8,128)} %get-tuple-element.149.refs_2_.refs_3_, f32[1,1024]{1,0:T(1,128)} %bitcast.133, ...), custom_call_target="tpu_custom_call" | custom-call | flops 3623878656 | bytes 9987686 | tf_op jit(solution)/shard_map/pallas_call | solution.py:305
  512.4 10.4 %shard_map.291.refs_2_ = bf16[4,288,1024]{2,1,0:T(8,128)(2,1)} custom-call(s32[6]{0:T(128)} %pad_add_fusion.refs_0_, bf16[1152,2048]{1,0:T(8,128)(2,1)} %get-tuple-element.142.refs_5_.refs_1_, bf16[1152,2048]{1,0:T(8,128)(2,1)} %get-tuple-element.148.refs_2_, f32[1152,1024]{1,0:T(8,128)} %get-tuple-element.149.refs_2_.refs_3_, ...), custom_call_target="tpu_custom_call", output_to_operand_aliasing={{}: (8, {})} | custom-call | flops 3623878656 | bytes 9987686 | tf_op jit(solution)/shard_map/pallas_call | solution.py:305
  541.1 12.2 %collective-permute-done.41 = bf16[64,2048]{1,0:T(8,128)(2,1)S(1)} collective-permute-done((bf16[64,2048]{1,0:T(8,128)(2,1)}, bf16[64,2048]{1,0:T(8,128)(2,1)S(1)}, u32[]{:S(2)}, u32[]{:S(2)}) %collective-permute-start.41) | collective-permute-done | bytes 262176 | tf_op jit(solution)/shard_map/ppermute | solution.py:246
  (267 shorter events, 209.6 us)
Async XLA Ops:
  7.3 246.5 %all-gather.3.cloned.1.call-start = ((), (), s32[]{:S(2)}) async-start(), calls=%async_computation | async-start | bytes 8650752 | tf_op jit(solution)/shard_map/all_gather | solution.py:953
  8.8 29.1 %collective-permute-start = (bf16[2,288,1024]{2,1,0:T(8,128)(2,1)S(1)}, bf16[2,288,1024]{2,1,0:T(8,128)(2,1)}, u32[]{:S(2)}, u32[]{:S(2)}) collective-permute-start(bf16[2,288,1024]{2,1,0:T(8,128)(2,1)S(1)} %constant_dynamic-slice_fusion.1), channel_id=1, source_target_pairs={{0,1},{1,0},{2,3},{3,2},{4,5},{5,4},{6,7},{7,6},{8,9},{9,8},{10,11... | collective-permute-start | bytes 3538952 | tf_op jit(solution)/shard_map/ppermute | solution.py:246
  39.1 41.6 %collective-permute-start.5 = (bf16[272,2048]{1,0:T(8,128)(2,1)}, bf16[272,2048]{1,0:T(8,128)(2,1)S(1)}, u32[]{:S(2)}, u32[]{:S(2)}) collective-permute-start(bf16[272,2048]{1,0:T(8,128)(2,1)} %pad_maximum_fusion.4), channel_id=1, source_target_pairs={{0,1},{1,0},{2,3},{3,2},{4,5},{5,4},{6,7},{7,6},{8,9},{9,8},{10,11... | collective-permute-start | bytes 3342344 | tf_op jit(solution)/shard_map/ppermute | solution.py:246
  46.4 34.3 %collective-permute-start.4 = (bf16[256,2048]{1,0:T(8,128)(2,1)}, bf16[256,2048]{1,0:T(8,128)(2,1)}, u32[]{:S(2)}, u32[]{:S(2)}) collective-permute-start(bf16[256,2048]{1,0:T(8,128)(2,1)} %copy-done.1), channel_id=1, source_target_pairs={{0,4},{2,6},{4,0},{6,2},{8,12},{10,14},{12,8},{14,10},{16,20},{18,... | collective-permute-start | bytes 3145736 | tf_op jit(solution)/shard_map/ppermute | solution.py:246
  49.5 30.5 %collective-permute-start.8 = (bf16[64,2048]{1,0:T(8,128)(2,1)S(1)}, bf16[64,2048]{1,0:T(8,128)(2,1)S(1)}, u32[]{:S(2)}, u32[]{:S(2)}) collective-permute-start(bf16[64,2048]{1,0:T(8,128)(2,1)S(1)} %copy-done.25), channel_id=1, source_target_pairs={{0,24},{2,26},{4,28},{6,30},{8,16},{10,18},{12,20},{14,22},{16,8},... | collective-permute-start | bytes 786440 | tf_op jit(solution)/shard_map/ppermute | solution.py:246
  51.9 27.2 %collective-permute-start.7 = (bf16[64,2048]{1,0:T(8,128)(2,1)S(1)}, bf16[64,2048]{1,0:T(8,128)(2,1)S(1)}, u32[]{:S(2)}, u32[]{:S(2)}) collective-permute-start(bf16[64,2048]{1,0:T(8,128)(2,1)S(1)} %copy-done.25), channel_id=1, source_target_pairs={{0,16},{2,18},{4,20},{6,22},{8,24},{10,26},{12,28},{14,30},{16,0},... | collective-permute-start | bytes 786440 | tf_op jit(solution)/shard_map/ppermute | solution.py:246
  82.7 35.4 %collective-permute-start.10 = (bf16[272,2048]{1,0:T(8,128)(2,1)S(1)}, bf16[272,2048]{1,0:T(8,128)(2,1)S(1)}, u32[]{:S(2)}, u32[]{:S(2)}) collective-permute-start(bf16[272,2048]{1,0:T(8,128)(2,1)S(1)} %collective-permute-done.5.refs_2_.refs_7_.refs_12_.refs_8_), channel_id=1, source_target_pairs={{0,4},{2,6},{4,0},{6,2},{8,12},{10,14},{12,8},{14,10},{16,20},{18,... | collective-permute-start | bytes 3342344 | tf_op jit(solution)/shard_map/ppermute | solution.py:246
  120.1 34.8 %collective-permute-start.13 = (bf16[256,2048]{1,0:T(8,128)(2,1)}, bf16[256,2048]{1,0:T(8,128)(2,1)}, u32[]{:S(2)}, u32[]{:S(2)}) collective-permute-start(bf16[256,2048]{1,0:T(8,128)(2,1)} %constant_dynamic-update-slice_fusion.3.refs_2_.refs_5_), channel_id=1, source_target_pairs={{0,4},{2,6},{4,0},{6,2},{8,12},{10,14},{12,8},{14,10},{16,20},{18,... | collective-permute-start | bytes 3145736 | tf_op jit(solution)/shard_map/ppermute | solution.py:246
  175.4 29.7 %collective-permute-start.14 = (bf16[2,256,2048]{2,1,0:T(8,128)(2,1)}, bf16[2,256,2048]{2,1,0:T(8,128)(2,1)}, u32[]{:S(2)}, u32[]{:S(2)}) collective-permute-start(bf16[2,256,2048]{2,1,0:T(8,128)(2,1)} %pad_maximum_fusion.2), channel_id=1, source_target_pairs={{0,2},{2,0},{4,6},{6,4},{8,10},{10,8},{12,14},{14,12},{16,18},{18,... | collective-permute-start | bytes 6291464 | tf_op jit(solution)/shard_map/ppermute | solution.py:246
  176.5 28.6 %collective-permute-start.15 = (bf16[2,288,1024]{2,1,0:T(8,128)(2,1)}, bf16[2,288,1024]{2,1,0:T(8,128)(2,1)S(1)}, u32[]{:S(2)}, u32[]{:S(2)}) collective-permute-start(bf16[2,288,1024]{2,1,0:T(8,128)(2,1)} %constant_dynamic-slice_fusion), channel_id=1, source_target_pairs={{0,1},{1,0},{2,3},{3,2},{4,5},{5,4},{6,7},{7,6},{8,9},{9,8},{10,11... | collective-permute-start | bytes 3538952 | tf_op jit(solution)/shard_map/ppermute | solution.py:246
  177.0 41.4 %collective-permute-start.16 = (bf16[256,2048]{1,0:T(8,128)(2,1)S(1)}, bf16[256,2048]{1,0:T(8,128)(2,1)S(1)}, u32[]{:S(2)}, u32[]{:S(2)}) collective-permute-start(bf16[256,2048]{1,0:T(8,128)(2,1)S(1)} %copy-done.11), channel_id=1, source_target_pairs={{0,4},{2,6},{4,0},{6,2},{8,12},{10,14},{12,8},{14,10},{16,20},{18,... | collective-permute-start | bytes 3145736 | tf_op jit(solution)/shard_map/ppermute | solution.py:246
  291.6 50.0 %collective-permute-start.19 = (bf16[512,2048]{1,0:T(8,128)(2,1)}, bf16[512,2048]{1,0:T(8,128)(2,1)S(1)}, u32[]{:S(2)}, u32[]{:S(2)}) collective-permute-start(bf16[512,2048]{1,0:T(8,128)(2,1)} %get-tuple-element.158), channel_id=1, source_target_pairs={{0,4},{2,6},{4,0},{6,2},{8,12},{10,14},{12,8},{14,10},{16,20},{18,... | collective-permute-start | bytes 6291464 | tf_op jit(solution)/shard_map/ppermute | solution.py:246
  357.0 48.1 %collective-permute-start.24 = (bf16[512,2048]{1,0:T(8,128)(2,1)}, bf16[512,2048]{1,0:T(8,128)(2,1)S(1)}, u32[]{:S(2)}, u32[]{:S(2)}) collective-permute-start(bf16[512,2048]{1,0:T(8,128)(2,1)} %get-tuple-element.173), channel_id=1, source_target_pairs={{0,1},{1,0},{2,3},{3,2},{4,5},{5,4},{6,7},{7,6},{8,9},{9,8},{10,11... | collective-permute-start | bytes 6291464 | tf_op jit(solution)/shard_map/ppermute | solution.py:246
  375.9 33.8 %collective-permute-start.23 = (bf16[256,2048]{1,0:T(8,128)(2,1)}, bf16[256,2048]{1,0:T(8,128)(2,1)}, u32[]{:S(2)}, u32[]{:S(2)}) collective-permute-start(bf16[256,2048]{1,0:T(8,128)(2,1)} %get-tuple-element.172), channel_id=1, source_target_pairs={{0,4},{2,6},{4,0},{6,2},{8,12},{10,14},{12,8},{14,10},{16,20},{18,... | collective-permute-start | bytes 3145736 | tf_op jit(solution)/shard_map/ppermute | solution.py:246
  376.2 48.4 %collective-permute-start.21 = (bf16[256,2048]{1,0:T(8,128)(2,1)}, bf16[256,2048]{1,0:T(8,128)(2,1)S(1)}, u32[]{:S(2)}, u32[]{:S(2)}) collective-permute-start(bf16[256,2048]{1,0:T(8,128)(2,1)} %get-tuple-element.168), channel_id=1, source_target_pairs={{0,16},{2,18},{4,20},{6,22},{8,24},{10,26},{12,28},{14,30},{16,0},... | collective-permute-start | bytes 3145736 | tf_op jit(solution)/shard_map/ppermute | solution.py:246
  440.2 38.1 %collective-permute-start.29 = (bf16[256,2048]{1,0:T(8,128)(2,1)}, bf16[256,2048]{1,0:T(8,128)(2,1)}, u32[]{:S(2)}, u32[]{:S(2)}) collective-permute-start(bf16[256,2048]{1,0:T(8,128)(2,1)} %get-tuple-element.184), channel_id=1, source_target_pairs={{0,4},{2,6},{4,0},{6,2},{8,12},{10,14},{12,8},{14,10},{16,20},{18,... | collective-permute-start | bytes 3145736 | tf_op jit(solution)/shard_map/ppermute | solution.py:246
  442.0 41.4 %collective-permute-start.28 = (bf16[256,2048]{1,0:T(8,128)(2,1)S(1)}, bf16[256,2048]{1,0:T(8,128)(2,1)}, u32[]{:S(2)}, u32[]{:S(2)}) collective-permute-start(bf16[256,2048]{1,0:T(8,128)(2,1)S(1)} %copy-done.14), channel_id=1, source_target_pairs={{0,1},{1,0},{2,3},{3,2},{4,5},{5,4},{6,7},{7,6},{8,9},{9,8},{10,11... | collective-permute-start | bytes 3145736 | tf_op jit(solution)/shard_map/ppermute | solution.py:246
  443.5 47.8 %collective-permute-start.25 = (bf16[128,2048]{1,0:T(8,128)(2,1)}, bf16[128,2048]{1,0:T(8,128)(2,1)}, u32[]{:S(2)}, u32[]{:S(2)}) collective-permute-start(bf16[128,2048]{1,0:T(8,128)(2,1)} %get-tuple-element.179), channel_id=1, source_target_pairs={{0,8},{2,10},{4,12},{6,14},{8,0},{10,2},{12,4},{14,6},{16,24},{18,... | collective-permute-start | bytes 1572872 | tf_op jit(solution)/shard_map/ppermute | solution.py:246
  448.8 39.8 %collective-permute-start.27 = (bf16[256,2048]{1,0:T(8,128)(2,1)}, bf16[256,2048]{1,0:T(8,128)(2,1)}, u32[]{:S(2)}, u32[]{:S(2)}) collective-permute-start(bf16[256,2048]{1,0:T(8,128)(2,1)} %get-tuple-element.183), channel_id=1, source_target_pairs={{0,4},{2,6},{4,0},{6,2},{8,12},{10,14},{12,8},{14,10},{16,20},{18,... | collective-permute-start | bytes 3145736 | tf_op jit(solution)/shard_map/ppermute | solution.py:246
  461.6 47.9 %collective-permute-start.30 = (bf16[2,288,1024]{2,1,0:T(8,128)(2,1)}, bf16[2,288,1024]{2,1,0:T(8,128)(2,1)}, u32[]{:S(2)}, u32[]{:S(2)}) collective-permute-start(bf16[2,288,1024]{2,1,0:T(8,128)(2,1)} %get-tuple-element.186.refs_13_), channel_id=1, source_target_pairs={{0,1},{1,0},{2,3},{3,2},{4,5},{5,4},{6,7},{7,6},{8,9},{9,8},{10,11... | collective-permute-start | bytes 3538952 | tf_op jit(solution)/shard_map/ppermute | solution.py:246
  480.8 26.8 %collective-permute-start.31 = (bf16[128,2048]{1,0:T(8,128)(2,1)}, bf16[128,2048]{1,0:T(8,128)(2,1)}, u32[]{:S(2)}, u32[]{:S(2)}) collective-permute-start(bf16[128,2048]{1,0:T(8,128)(2,1)} %get-tuple-element.191), channel_id=1, source_target_pairs={{0,16},{2,18},{4,20},{6,22},{8,24},{10,26},{12,28},{14,30},{16,0},... | collective-permute-start | bytes 1572872 | tf_op jit(solution)/shard_map/ppermute | solution.py:246
  505.6 55.0 %collective-permute-start.32 = (bf16[2,288,1024]{2,1,0:T(8,128)(2,1)S(1)}, bf16[2,288,1024]{2,1,0:T(8,128)(2,1)}, u32[]{:S(2)}, u32[]{:S(2)}) collective-permute-start(bf16[2,288,1024]{2,1,0:T(8,128)(2,1)S(1)} %copy-done.13), channel_id=1, source_target_pairs={{0,1},{1,0},{2,3},{3,2},{4,5},{5,4},{6,7},{7,6},{8,9},{9,8},{10,11... | collective-permute-start | bytes 3538952 | tf_op jit(solution)/shard_map/ppermute | solution.py:246
  507.0 31.4 %collective-permute-start.42 = (bf16[64,2048]{1,0:T(8,128)(2,1)}, bf16[64,2048]{1,0:T(8,128)(2,1)S(1)}, u32[]{:S(2)}, u32[]{:S(2)}) collective-permute-start(bf16[64,2048]{1,0:T(8,128)(2,1)} %get-tuple-element.208), channel_id=1, source_target_pairs={{0,1},{1,0},{2,3},{3,2},{4,5},{5,4},{6,7},{7,6},{8,9},{9,8},{10,11... | collective-permute-start | bytes 786440 | tf_op jit(solution)/shard_map/ppermute | solution.py:246
  528.7 27.1 %collective-permute-start.38 = (bf16[64,2048]{1,0:T(8,128)(2,1)}, bf16[64,2048]{1,0:T(8,128)(2,1)S(1)}, u32[]{:S(2)}, u32[]{:S(2)}) collective-permute-start(bf16[64,2048]{1,0:T(8,128)(2,1)} %get-tuple-element.204), channel_id=1, source_target_pairs={{0,8},{2,10},{4,12},{6,14},{8,0},{10,2},{12,4},{14,6},{16,24},{18,... | collective-permute-start | bytes 786440 | tf_op jit(solution)/shard_map/ppermute | solution.py:246
  (67 other events, 624.2 us)
Sparse Core Ops, SparseCore 0:
  52.9 92.9 all-gather.2

commit v4 on v3

--- a/solution.py
+++ b/solution.py
@@ -324,6 +324,26 @@
     ] * far
 
 
+def gathered_specs(columns, halves=(0, 1), at=None):
+    def spec(block, x_at):
+        core, y_at, z_at = block // 8, (block // 4) % 2, block % 4
+        slab = z_at * 4 + y_at * 2 + core
+
+        def place(j, *refs):
+            where = refs[-1]
+            row = jnp.bitwise_xor(where[1], slab), jnp.bitwise_xor(where[0], x_at)
+            return (*row, 0, j if at is None else at)
+
+        mode = {} if at is None else {"pipeline_mode": pl.Buffered(1)}
+        return pl.BlockSpec((1, 1, ROWS, columns), place, **mode)
+
+    return [spec(block, x_at) for block in range(16) for x_at in halves]
+
+
+def joined(refs, first, last, step=1, offset=0):
+    return jnp.concatenate([refs[step * block + offset][0, 0] for block in range(first, last)], axis=0)
+
+
 def struct(shape, dtype=BF16):
     return jax.ShapeDtypeStruct(shape, dtype)
 
@@ -445,11 +465,9 @@
     mine = 2
 
     def kernel(side_ref, raw_ref, order_ref, *refs):
-        final_ref, plain_ref, sum_ref = refs[-3:]
+        final_ref, sum_ref = refs[-2:]
         keep = side_ref[2 + side_ref[0] * mine + pl.program_id(0)].astype(F32)
-        plain = (raw_ref[0].astype(F32) * keep).astype(BF16)
-        plain_ref[...] = plain
-        final = dot_nn(plain, order_ref[...])
+        final = dot_nn(raw_ref[0], order_ref[...]) * keep
         final_ref[...] = final.astype(BF16)
 
         @pl.when(first_step())
@@ -459,18 +477,18 @@
         sum_ref[...] += column_sum(final)
 
     offset = (lambda side_ref: side_ref[0] * mine) if half_at == 0 else (lambda side_ref: 0)
-    old = () if before is None else before
+    old = () if before is None else (before,)
     out = pl.BlockSpec((height, width), lambda i, _: (half_at * mine + i, 0))
     return call(
         kernel,
         (mine,),
         [image_block(height, width, offset), fixed(width, width)] + [ANYWHERE] * len(old),
-        [out, out, fixed(1, width)],
-        [struct((2 * mine * height, width))] * 2 + [struct((1, width), F32)],
+        [out, fixed(1, width)],
+        [struct((2 * mine * height, width)), struct((1, width), F32)],
         2 * mine * height * width * width,
         6 * mine * height * width,
         after,
-        {3: 0, 4: 1} if old else None,
+        {3: 0} if old else None,
         1,
         part=FORWARD_PART,
     )(side, images, order, *old)
@@ -610,59 +628,48 @@
     )(*contexts, rows, bias, gain, shift, *pieces)
 
 
-def feed_up(second, parts, bias, tile=512, after=()):
+def feed_up(places, x_at, second, gathered, bias, tile=512, after=()):
     count, width = second.shape
-    columns = parts[0].shape[1]
-
-    def kernel(second_ref, bias_ref, *refs):
-        weight = jnp.concatenate([refs[0][...], refs[1][...], refs[2][0], refs[2][1]], axis=0)
-        hidden = dot_nn(second_ref[...], weight) + bias_ref[...]
+    columns = gathered.shape[-1]
+
+    def kernel(place_ref, second_ref, bias_ref, *refs):
+        hidden = dot_nn(second_ref[...], joined(refs, 0, 16)) + bias_ref[...]
         gate = 0.5 + 0.5 * jnp.tanh(0.851 * hidden)
-        refs[3][...] = (hidden * gate).astype(BF16)
-        refs[4][...] = (gate * (1.0 + 1.702 * hidden * (1.0 - gate))).astype(BF16)
-
-    block = pl.BlockSpec((count, tile), lambda j: (0, j))
+        refs[16][...] = (hidden * gate).astype(BF16)
+        refs[17][...] = (gate * (1.0 + 1.702 * hidden * (1.0 - gate))).astype(BF16)
+
+    block = pl.BlockSpec((count, tile), lambda j, _: (0, j))
     return call(
         kernel,
         (columns // tile,),
-        [fixed(count, width), pl.BlockSpec((1, tile), lambda j: (0, j))] + piece_tiles(tile, 2, 1),
+        [fixed(count, width), pl.BlockSpec((1, tile), lambda j, _: (0, j))] + gathered_specs(tile, (x_at,)),
         [block, block],
         [struct((count, columns))] * 2,
         2 * count * width * columns,
         2 * count * (width + 2 * columns) + 2 * width * columns,
         after,
+        None,
+        1,
         part=FORWARD_PART,
-    )(second, bias, *parts)
+    )(places, second, bias, *[gathered] * 16)
 
 
 def feed_down(side, first_tile, last_tile, actives, middle, gathered, bias, order, before=None, tile=288, after=()):
     count, columns = actives[0].shape
     width = middle.shape[1]
     mine = count // tile // 2
-    slices = gathered.shape[0]
     half_at = first_tile // mine
     old = () if before is None else (before,)
 
     def kernel(side_ref, low_ref, high_ref, middle_ref, bias_ref, order_ref, *refs):
         keep = side_ref[2 + side_ref[0] * mine + first_tile % mine + pl.program_id(0)].astype(F32)
-        parts, out_ref = refs[:2], refs[-1]
-        feed = dot_nt(low_ref[...], parts[0][...].reshape(width, columns))
-        feed = feed + dot_nt(high_ref[...], parts[1][...].reshape(width, columns))
-        middle = middle_ref[...]
-        top = middle.astype(BF16)
-        rest = (middle - top.astype(F32)).astype(BF16)
-        middle = dot_nt(top, order_ref[...]) + dot_nt(rest, order_ref[...])
-        out_ref[0] = ((middle + (feed + bias_ref[...])) * keep).astype(BF16)
+        out_ref = refs[-1]
+        feed = dot_nt(low_ref[...], joined(refs, 0, 16, 2, 0)) + dot_nt(high_ref[...], joined(refs, 0, 16, 2, 1))
+        out = ((middle_ref[...] + (feed + bias_ref[...])) * keep).astype(BF16)
+        out_ref[0] = dot_nt(out, order_ref[...]).astype(BF16)
 
     hidden = pl.BlockSpec((tile, columns), lambda i, _: (first_tile + i, 0))
     offset = (lambda ref: ref[0] * mine + first_tile) if half_at == 0 else (lambda ref: first_tile - mine)
-
-    def weight(x_at):
-        return pl.BlockSpec(
-            (slices, 1, ROWS, columns),
-            lambda i, ref: (0, jnp.bitwise_xor(ref[0], x_at), 0, 0),
-            pipeline_mode=pl.Buffered(1),
-        )
 
     return call(
         kernel,
@@ -673,42 +680,37 @@
             pl.BlockSpec((tile, width), lambda i, _: (first_tile + i, 0)),
             fixed(1, width),
             fixed(width, width),
-            weight(0),
-            weight(1),
         ]
+        + gathered_specs(columns, at=0)
         + [ANYWHERE] * len(old),
         image_block(tile, width, offset),
         struct(((2 - half_at) * mine, tile, width)),
         2 * count * width * columns + count * width * width,
         2 * count * columns + 3 * count * width + 4 * width * columns,
         after,
-        {8: 0} if old else None,
+        {38: 0} if old else None,
         1,
-    )(side, *actives, middle, bias, order, gathered, gathered, *old)
-
-
-def gate_back(side, plain, slopes, gathered, tile=512, after=()):
-    count, width = plain.shape
-    slices, _, _, columns = gathered.shape
-
-    def kernel(side_ref, plain_ref, low_ref, high_ref, *refs):
-        parts, outs, sums = refs[:2], refs[2:4], refs[4:6]
+    )(side, *actives, middle, bias, order, *[gathered] * 32, *old)
+
+
+def gate_back(side, final, slopes, gathered, tile=512, after=()):
+    count, width = final.shape
+    columns = gathered.shape[-1]
+
+    def kernel(side_ref, final_ref, low_ref, high_ref, *refs):
+        outs, sums = refs[32:34], refs[34:36]
         for x_at, slope_ref in enumerate((low_ref, high_ref)):
-            weight = parts[x_at][...].reshape(width, tile)
-            grad = (dot_nn(plain_ref[...], weight) * slope_ref[...].astype(F32)).astype(BF16)
+            weight = joined(refs, 0, 16, 2, x_at)
+            grad = (dot_nn(final_ref[...], weight) * slope_ref[...].astype(F32)).astype(BF16)
             outs[x_at][...] = grad
             sums[x_at][...] = column_sum(grad.astype(F32))
 
     block = pl.BlockSpec((count, tile), lambda j, _: (0, j))
     sum_block = pl.BlockSpec((1, tile), lambda j, _: (0, j))
-
-    def weight(x_at):
-        return pl.BlockSpec((slices, 1, ROWS, tile), lambda j, ref: (0, jnp.bitwise_xor(ref[0], x_at), 0, j))
-
     return call(
         kernel,
         (columns // tile,),
-        [fixed(count, width), block, block, weight(0), weight(1)],
+        [fixed(count, width), block, block] + gathered_specs(tile),
         [block, block, sum_block, sum_block],
         [struct((count, columns))] * 2 + [struct((1, columns), F32)] * 2,
         4 * count * width * columns,
@@ -716,7 +718,7 @@
         after,
         None,
         1,
-    )(side, plain, *slopes, gathered, gathered)
+    )(side, final, *slopes, *[gathered] * 32)
 
 
 def sums_down(final, actives, tile=512, after=()):
@@ -728,18 +730,16 @@
             for core in range(2):
                 for y_at in range(2):
                     start = (2 * core + y_at) * PART
-                    part = dot_tn(final_ref[:, start : start + PART], right_ref[...]).astype(BF16)
-                    for z_at in range(4):
-                        row = (2 * (z_at % 2) + x_at) * ROWS
-                        outs[core][y_at, z_at // 2, row : row + ROWS, :] = part[z_at * ROWS : (z_at + 1) * ROWS]
+                    part = dot_tn(final_ref[:, start : start + PART], right_ref[...])
+                    outs[2 * core + y_at][x_at] = part.astype(BF16)
 
     right = pl.BlockSpec((count, tile), lambda j: (0, j))
     return call(
         kernel,
         (columns // tile,),
         [fixed(count, width), right, right],
-        [pl.BlockSpec((2, 2, PART, tile), lambda j: (0, 0, 0, j))] * 2,
-        [struct((2, 2, PART, columns))] * 2,
+        [pl.BlockSpec((2, PART, tile), lambda j: (0, 0, j))] * 4,
+        [struct((2, PART, columns))] * 4,
         4 * count * width * columns,
         4 * count * columns + 2 * count * width + 4 * width * columns,
         after,
@@ -756,15 +756,15 @@
                 for y_at in range(2):
                     start = (2 * core + y_at) * PART
                     part = dot_tn(second_ref[:, start : start + PART], right_ref[...])
-                    outs[core][x_at, y_at] = part.astype(BF16)
+                    outs[2 * core + x_at][y_at] = part.astype(BF16)
 
     right = pl.BlockSpec((count, tile), lambda j: (0, j))
     return call(
         kernel,
         (columns // tile,),
         [fixed(count, width), right, right],
-        [pl.BlockSpec((2, 2, PART, tile), lambda j: (0, 0, 0, j))] * 2,
-        [struct((2, 2, PART, columns))] * 2,
+        [pl.BlockSpec((2, PART, tile), lambda j: (0, 0, j))] * 4,
+        [struct((2, PART, columns))] * 4,
         4 * count * width * columns,
         4 * count * columns + 2 * count * width + 4 * width * columns,
         after,
@@ -780,7 +780,7 @@
             for core in range(2):
                 for y_at in range(2):
                     start = (2 * core + y_at) * PART
-                    outs[core][y_at] = dot_tn(left_ref[:, start : start + PART], right).astype(BF16)
+                    outs[2 * core + y_at][...] = dot_tn(left_ref[:, start : start + PART], right).astype(BF16)
 
         @pl.when(pl.program_id(0) < 3)
         def _():
@@ -795,26 +795,23 @@
         kernel,
         (4,),
         [left, left, pl.BlockSpec((1, count, half), lambda j: (jnp.minimum(j, 2), 0, 0)), fixed(count, half)],
-        [pl.BlockSpec((2, PART, half), lambda j: (0, 0, j))] * 2,
-        [struct((2, PART, 4 * half))] * 2,
+        [pl.BlockSpec((PART, half), lambda j: (0, j))] * 4,
+        [struct((PART, 4 * half))] * 4,
         8 * count * width * half,
         2 * count * (2 * width + 4 * half) + 8 * width * half,
         after,
     )(normed, branch, grad_projected, context)
 
 
-def second_back(grads, up_pieces, first_pieces, middle, final, gain, tile=288, after=()):
+def second_back(places, grads, gathered, first_pieces, middle, final, gain, tile=288, after=()):
     count, columns = grads[0].shape
     width = middle.shape[1]
     half = width // 2
 
-    def kernel(low_ref, high_ref, middle_ref, final_ref, gain_ref, *refs):
-        ups, outs = far_list(refs[:4], refs[4:6]), far_list(refs[6:10], refs[10:12])
-        grad_ref, branch_ref, context_low_ref, context_high_ref, sum_ref = refs[12:]
-        found = []
-        for at in range(4):
-            found.append(dot_nt(low_ref[...], ups[2 * at][...]) + dot_nt(high_ref[...], ups[2 * at + 1][...]))
-        grad_second = jnp.concatenate(found, axis=1)
+    def kernel(place_ref, low_ref, high_ref, middle_ref, final_ref, gain_ref, *refs):
+        ups, outs = refs[:32], far_list(refs[32:36], refs[36:38])
+        grad_ref, branch_ref, context_low_ref, context_high_ref, sum_ref = refs[38:]
+        grad_second = dot_nt(low_ref[...], joined(ups, 0, 16, 2, 0)) + dot_nt(high_ref[...], joined(ups, 0, 16, 2, 1))
         unit, inv_std = normal_parts(middle_ref[...])
         grad_middle = final_ref[...].astype(F32) + normalize_back(
             grad_second, unit, inv_std, gain_ref[...]
@@ -834,14 +831,14 @@
         sum_ref[1:2] += column_sum(grad_second)
         sum_ref[2:3] += column_sum(branch.astype(F32))
 
-    block = pl.BlockSpec((tile, width), lambda i: (i, 0))
-    half_block = pl.BlockSpec((tile, half), lambda i: (i, 0))
-    hidden = pl.BlockSpec((tile, columns), lambda i: (i, 0))
+    block = pl.BlockSpec((tile, width), lambda i, _: (i, 0))
+    half_block = pl.BlockSpec((tile, half), lambda i, _: (i, 0))
+    hidden = pl.BlockSpec((tile, columns), lambda i, _: (i, 0))
     return call(
         kernel,
         (count // tile,),
         [hidden, hidden, block, block, fixed(1, width)]
-        + piece_specs(columns)
+        + gathered_specs(columns, at=0)
         + piece_specs(half, 3),
         [block, block, half_block, half_block, fixed(8, width)],
         [struct((count, width), F32), struct((count, width))]
@@ -850,7 +847,9 @@
         4 * count * width * columns + 2 * count * width * width,
         4 * count * columns + 14 * count * width + 4 * width * columns,
         after,
-    )(*grads, middle, final, gain, *up_pieces, *first_pieces)
+        None,
+        1,
+    )(places, *grads, middle, final, gain, *[gathered] * 32, *first_pieces)
 
 
 def first_back(side, half_at, grads, pieces, rows, grad_middle, gain, order, tile=288, after=()):
@@ -894,6 +893,7 @@
         after,
         None,
         1,
+        part=0.3,
     )(side, *grads, rows, grad_middle, gain, order, *pieces)
 
 
@@ -922,6 +922,23 @@
     me = lax.axis_index("dp")
     side = lax.axis_index("tensor")
     side_array = jnp.concatenate([jnp.stack([side, me]).astype(jnp.int32), image_mask])
+    vectors = (norm1_gain, norm1_shift, norm2_gain, norm2_shift, out_bias, down_bias)
+    order, gain_one, shift_one, gain_two, shift_two, bias_out, bias_down = setup(
+        side_array, [vector.reshape(1, width) for vector in vectors]
+    )
+
+    def for_partner(values):
+        return over_x(lax.dynamic_slice_in_dim(values, (1 - side) * mine, mine, 0))
+
+    def z_all(values):
+        return jnp.concatenate([values] + [over_z(values, step) for step in (1, 2, 3)], axis=0)
+
+    up_all = lax.all_gather(up_weight, ("dp", "tensor")).reshape(-1, 2, ROWS, half_hidden)
+    own = prepare(side_array, tokens, order, gain_one, shift_one, 0)
+    final, sum_own = mask_grad(side_array, out_grad, order, 0, after=own[:1])
+    tokens_partner = for_partner(tokens)
+    first = jnp.concatenate([qkv_weight.reshape(ROWS, 3 * half), out_weight], axis=1)
+    first_base = late(z_all(first), final)
     biases = jnp.concatenate([qv_bias.reshape(-1), up_bias])
     bias_rows = jnp.pad(biases, (0, 16 * half_hidden - biases.size)).reshape(16, half_hidden)
 
@@ -930,82 +947,47 @@
         parts = jnp.stack([bias[:half], jnp.zeros((half,), F32), bias[half : 2 * half]])
         return parts[:, None], bias[None, 2 * half :]
 
-    vectors = (norm1_gain, norm1_shift, norm2_gain, norm2_shift, out_bias)
-    bias_down = down_bias.astype(F32).reshape(1, width)
-    order, gain_one, shift_one, gain_two, shift_two, bias_out = setup(
-        side_array, [vector.reshape(1, width) for vector in vectors]
-    )
-
-    def for_partner(values):
-        return over_x(lax.dynamic_slice_in_dim(values, (1 - side) * mine, mine, 0))
-
-    def from_partner(values, send):
-        return lax.dynamic_update_slice_in_dim(values, over_x(send), (1 - side) * mine, 0)
-
-    def z_all(values):
-        return jnp.concatenate([values] + [over_z(values, step) for step in (1, 2, 3)], axis=0)
-
-    own = prepare(side_array, tokens, order, gain_one, shift_one, 0)
-    *final, sum_own = mask_grad(side_array, out_grad, order, 0, after=own[:1])
-    tokens_partner = for_partner(tokens)
-    first = jnp.concatenate([qkv_weight.reshape(ROWS, 3 * half), out_weight], axis=1)
-    first_base = late(z_all(first), final[0])
-    down_all = lax.all_gather(late(down_weight, first_base), ("dp", "tensor"))
-    down_all = down_all.reshape(-1, 2, ROWS, half_hidden)
-    first_x = over_x(jnp.concatenate([late(first_base, tokens_partner), bias_rows], axis=0))
     rows, normed = prepare(
         side_array, tokens_partner, order, gain_one, shift_one, 1, own, after=[first_base]
     )
+    first_x = over_x(jnp.concatenate([late(first_base, normed), bias_rows], axis=0))
     first_y = over_y(late(first_base, normed))
-    up_base = z_all(late(up_weight, first_base))
     first_xy = over_y(late(first_x, first_y))
-    first_far = [over_core(jnp.stack(late([first_base, first_y], first_x, up_base)))]
-    up_x = over_x(late(up_base, first_x))
-    grad_partner = for_partner(late(out_grad, up_x))
-
+    first_far = [over_core(jnp.stack(late([first_base, first_y], first_x)))]
     biases = [split_bias(biases), split_bias(first_x[4 * ROWS :].reshape(-1)[: biases.size])]
     heads_shape = (3, 2, mine, half_len, half)
     projected, contexts, probs = [None, None], [None, None], [None, None]
-    projected[0] = project(
-        normed, [first_base, first_y] + first_far, biases[0][0]
-    ).reshape(heads_shape)
+    projected[0] = project(normed, [first_base, first_y] + first_far, biases[0][0]).reshape(heads_shape)
     begun = attend(projected[0], 0, 1, lanes=128)
     first_far += [over_core(jnp.stack(late([first_x, first_xy], begun[0])))]
     first_pieces = [first_base, first_x, first_y, first_xy] + first_far
-    up_y = over_y(late(up_base, first_xy))
     contexts[0], probs[0] = attend(projected[0], 1, 2, begun, lanes=128)
+    grad_partner = for_partner(late(out_grad, first_x))
     projected[1] = project(
-        normed, [first_x, first_xy] + first_far[1:], biases[1][0], after=[contexts[0], up_x]
+        normed, [first_x, first_xy] + first_far[1:], biases[1][0], after=[contexts[0]]
     ).reshape(heads_shape)
-    contexts[1], probs[1] = attend(projected[1], 0, 2, after=[up_y])
+    down_all = lax.all_gather(late(down_weight, up_all, contexts[0]), ("dp", "tensor"))
+    down_all = down_all.reshape(-1, 2, ROWS, half_hidden)
+    contexts[1], probs[1] = attend(projected[1], 0, 2)
     contexts = [values.reshape(count, half) for values in contexts]
-
-    up_xy = over_y(late(up_x, up_y, contexts[1]))
-    up_far = [over_core(jnp.stack(late([up_base, up_y], contexts[1])))]
-    middle, second = add_branch(
-        contexts, rows, first_pieces, bias_out, gain_two, shift_two
-    )
+    middle, second = add_branch(contexts, rows, first_pieces, bias_out, gain_two, shift_two)
     actives, slopes = [None, None], [None, None]
-    actives[0], slopes[0] = feed_up(second, [up_base, up_y] + up_far, biases[0][1], after=[grad_partner])
-    *final, sum_partner = mask_grad(side_array, grad_partner, order, 1, final, after=[actives[0]])
-    up_far += [over_core(jnp.stack(late([up_x, up_xy], actives[0])))]
-    up_pieces = [up_base, up_x, up_y, up_xy] + up_far
-    actives[1], slopes[1] = feed_up(second, [up_x, up_xy] + up_far[1:], biases[1][1], after=final[:1])
-
-    final, plain = final
-    down_sums, down_sent = sums_down(final, actives)
-    down_sent = over_core(down_sent)
-    grads_sums = gate_back(side_array, plain, slopes, down_all, after=[down_sums])
+    actives[0], slopes[0] = feed_up(side_array, 0, second, up_all, biases[0][1])
+    final, sum_partner = mask_grad(side_array, grad_partner, order, 1, final, after=[actives[0]])
+    actives[1], slopes[1] = feed_up(side_array, 1, second, up_all, biases[1][1], after=[final])
+
+    down_near, down_next, down_far, down_last = sums_down(final, actives)
+    grads_sums = gate_back(side_array, final, slopes, down_all, after=[down_near])
     grads, sum_hidden = grads_sums[:2], grads_sums[2:]
-    down_sums = combine([down_sums, down_sent], 2, after=grads[:1])
-    down_sent = over_y(down_sums[1])
-    up_sums, up_sent = sums_up(second, grads, after=down_sums[:1])
-    up_sent = over_core(up_sent)
+    (down_sent,) = combine([down_next, over_core(down_last)], 1, after=grads[:1])
+    down_sent_y = over_y(down_sent)
+    up_near, up_next, up_far_sums, up_last = sums_up(second, grads, after=[down_sent])
     grad_middle, branch, *grad_contexts, sums_two = second_back(
-        grads, up_pieces, first_pieces, middle, final, gain_two, after=[up_sums]
-    )
-    up_sums = combine([up_sums, up_sent], 2, after=[branch])
-    up_sent = over_x(up_sums[1])
+        side_array, grads, up_all, first_pieces, middle, final, gain_two, after=[up_near]
+    )
+    (up_sent,) = combine([up_next, over_core(up_last)], 1, after=[branch])
+    up_sent_x = over_x(up_sent)
+    down_far = over_core(late(down_far, up_sent))
 
     def heads_back(x_at, after):
         grad_context = grad_contexts[x_at].reshape(2, mine, half_len, half)
@@ -1013,49 +995,44 @@
         return grad.reshape(3, count, half), jnp.sum(sums, axis=0)
 
     grads_qkv, sums_qkv = [None, None], [None, None]
-    grads_qkv[1], sums_qkv[1] = heads_back(1, up_sums[:1])
-    down_sums = combine([down_sums[0], down_sent], 2, after=[grads_qkv[1]])
-    down_sent = over_z(down_sums[1], 2)
-    high, high_sent = sums_first(normed, branch, grads_qkv[1], contexts[1], after=down_sums[:1])
-    high_sent = over_core(high_sent)
-    out_send = feed_down(side_array, 2, 4, actives, middle, down_all, bias_down, order, after=[high])
-    high = combine([high, high_sent], 2, after=[out_send])
-    high_sent = over_y(high[1])
-    grads_qkv[0], sums_qkv[0] = heads_back(0, high[:1])
-    up_sums = combine([up_sums[0], up_sent], 2, after=[grads_qkv[0]])
-    up_sent = over_y(up_sums[1])
-    (high,) = combine([high[0], high_sent], 1, after=up_sums[:1])
-    high_sent = over_x(high)
-    down_sums = combine([down_sums[0], down_sent], 2, after=[high])
-    down_sent = over_z(down_sums[1], 1)
-    low, low_sent = sums_first(normed, branch, grads_qkv[0], contexts[0], after=down_sums[:1])
-    low = combine([low, over_core(low_sent)], 2)
-    low_sent = over_y(low[1])
+    grads_qkv[1], sums_qkv[1] = heads_back(1, [up_sent])
+    down_sums = combine([down_near, down_far, down_sent_y], 2, after=[grads_qkv[1]])
+    down_sent_x = over_x(down_sums[1])
+    high_near, high_next, high_far, high_last = sums_first(
+        normed, branch, grads_qkv[1], contexts[1], after=down_sums[:1]
+    )
+    up_far_sums = over_core(late(up_far_sums, high_near))
+    out_send = feed_down(side_array, 2, 4, actives, middle, down_all, bias_down, order, after=[high_near])
+    (high_sent,) = combine([high_next, over_core(high_last)], 1, after=[out_send])
+    high_sent_y = over_y(high_sent)
+    up_sums = combine([up_near, up_far_sums, up_sent_x], 2, after=[high_sent])
+    up_sent_y = over_y(up_sums[1])
+    high_far = over_core(late(high_far, up_sums[0]))
+    out_partner = over_x(late(out_send, up_sums[0]))
+    grads_qkv[0], sums_qkv[0] = heads_back(0, up_sums[:1])
+    low_near, low_next, low_far, low_last = sums_first(
+        normed, branch, grads_qkv[0], contexts[0], after=[high_far]
+    )
+    (high,) = combine([high_near, high_far, high_sent_y], 1, after=[low_near])
+    high_x = over_x(high)
+    down_sums = combine([down_sums[0], down_sent_x], 2, after=[high])
+    down_sent_z = over_z(down_sums[1], 2)
+    (low_sent,) = combine([low_next, over_core(low_last)], 1, after=down_sums[:1])
+    low_sent_y = over_y(low_sent)
     send, sums_partner = first_back(
-        side_array, 1, grads_qkv, first_pieces, rows, grad_middle, gain_one, order, after=low[:1]
-    )
+        side_array, 1, grads_qkv, first_pieces, rows, grad_middle, gain_one, order, after=[low_sent]
+    )
+    up_sums = combine([up_sums[0], up_sent_y], 2, after=[send])
+    up_sent_z = over_z(up_sums[1], 2)
+    down_sums = combine([down_sums[0], down_sent_z], 2, after=[up_sums[0], out_partner])
+    down_sent_z = over_z(down_sums[1], 1)
+    low_far = over_core(late(low_far, up_sums[0]))
     full, sums_own = first_back(
-        side_array, 0, grads_qkv, first_pieces, rows, grad_middle, gain_one, order, after=[send]
-    )
-    up_sums = combine([up_sums[0], up_sent], 2, after=[full])
-    up_sent = over_z(up_sums[1], 2)
-    low = combine([low[0], low_sent, high_sent], 4, after=up_sums[:1])
-    low_sent = [over_z(low[step], step) for step in (1, 2, 3)]
-    down_sums = combine([down_sums[0], down_sent], 2, after=low[:1])
-    down_sent = over_x(down_sums[1])
-    out_begun = feed_down(
-        side_array, 0, 1, actives, middle, down_all, bias_down, order, after=down_sums[:1]
-    )
-    tokens_grad = from_partner(full, send)
-    up_sums = combine([up_sums[0], up_sent], 2, after=[out_begun])
-    up_sent = over_z(up_sums[1], 1)
-    out_full = feed_down(
-        side_array, 1, 2, actives, middle, down_all, bias_down, order, out_begun, after=[tokens_grad, up_sums[0]]
-    )
-    (grad_down,) = combine([down_sums[0], down_sent], 1, F32, after=[out_full])
-    block_out = from_partner(out_full, out_send)
-    (grad_up,) = combine([up_sums[0], up_sent], 1, F32, after=[grad_down])
-    (grad_first,) = combine([low[0]] + low_sent, 1, F32, after=[grad_up, tokens_grad])
+        side_array, 0, grads_qkv, first_pieces, rows, grad_middle, gain_one, order, after=down_sums[:1]
+    )
+    up_sums = combine([up_sums[0], up_sent_z], 2, after=[full])
+    up_sent_z = over_z(up_sums[1], 1)
+    (grad_down,) = combine([down_sums[0], down_sent_z], 1, F32, after=up_sums[:1])
 
     sums = jnp.concatenate(
         [(sums_own + sums_partner)[:2], sums_two[2:3], sums_two[:2], sum_own + sum_partner], axis=0
@@ -1064,17 +1041,25 @@
     halves = [
         jnp.concatenate([sums_qkv[x_at].reshape(-1), sum_hidden[x_at][0]]) for x_at in range(2)
     ]
-    small = jnp.concatenate([halves[0], sums.reshape(-1), halves[1]])
+    small = late(jnp.concatenate([halves[0], sums.reshape(-1), halves[1]]), up_sums[0])
     small = small + over_core(small)
-    small = late(small, out_begun)
     small = small + over_y(small)
-    small = late(small, out_full)
     small = (small + over_z(small, 1)) + (over_z(small, 2) + over_z(small, 3))
     halves_size = 2 * half + half_hidden
-    small = late(small, grad_first)
-    small = small[:-halves_size] + over_x(
-        jnp.concatenate([small[-halves_size:], small[halves_size:-halves_size]])
-    )
+    small_x = over_x(jnp.concatenate([small[-halves_size:], small[halves_size:-halves_size]]))
+
+    low = combine([low_near, low_far, low_sent_y, high_x], 4, after=[grad_down])
+    low_z = [over_z(low[step], step) for step in (1, 2, 3)]
+    send_x = over_x(late(send, low[0]))
+    out_full = feed_down(
+        side_array, 0, 2, actives, middle, down_all, bias_down, order, after=[low[0], small]
+    )
+    block_out = lax.dynamic_update_slice_in_dim(out_full, out_partner, (1 - side) * mine, 0)
+    (grad_up,) = combine([up_sums[0], up_sent_z], 1, F32, after=[out_full])
+    tokens_grad = lax.dynamic_update_slice_in_dim(full, send_x, (1 - side) * mine, 0)
+    (grad_first,) = combine([low[0]] + low_z, 1, F32, after=[grad_up, tokens_grad])
+
+    small = small[:-halves_size] + small_x
     halves = small[:halves_size]
     sums = small[halves_size:].reshape(6, width)
     return (

time: 582 us -> 520 us (0.89)
  waiting for transfers between devices: 123 us -> 86 us
  starting transfers between devices: 44.7 us -> 33.8 us
  other arithmetic: 11.8 us -> 4.13 us
    ppermute x44 -> x40, waiting for transfers between devices: 123 us -> 85.3 us  [swap(): lax.ppermute(values, axis_name, [(place, place ^ flip) for place in range...]
    ppermute x44 -> x40, starting transfers between devices: 44.7 us -> 33.7 us  [swap(): lax.ppermute(values, axis_name, [(place, place ^ flip) for place in range...]
    another operation x3 -> x1, other arithmetic: 6.63 us -> 0.19 us  [fast_shards(): first_far = [over_core(jnp.stack(late([first_base, first_y], first_x)))]]
    pallas_call x41 -> x40, Pallas kernels: 347 us -> 342 us  [call(): return lambda *arrays: function(*arrays, *after)]
    unnamed x104 -> x97, local copies, waits for them, and re-layouts: 13.4 us -> 11 us
  transfers between devices with their start and end apart: 45 -> 42, of which waited for: 15 -> 15; matrix products, arithmetic and copies ran while one was open for 5% -> 4% of each run, Pallas kernels for 52% -> 62%
where the time goes in v4:
time: 520 us; the launch traced here: 511 us
  Pallas kernels  342 us (66%)
  waiting for transfers between devices  86 us (17%)
  starting transfers between devices  33.8 us (6%)
  local copies, waits for them, and re-layouts  27.8 us (5%)
  between operations  15.2 us (3%)
    pallas_call x40, Pallas kernels, call(): return lambda *arrays: function(*arrays, *after)  342 us
    ppermute x40, waiting for transfers between devices, swap(): lax.ppermute(values, axis_name, [(place, place ^ flip) for place in range...  85.3 us
    ppermute x40, starting transfers between devices, swap(): lax.ppermute(values, axis_name, [(place, place ^ flip) for place in range...  33.7 us
    unnamed x97, local copies, waits for them, and re-layouts  11 us
  transfers between devices with their start and end apart: 42, of which 15 were waited for; matrix products, arithmetic and copies ran while one was open for 4% of the time, Pallas kernels for 62%

profile of v4, /device:TPU:0, one launch (start us, length us, event | category | flops | bytes accessed | tf_op | source)
XLA Modules:
  0.0 510.9 jit_solution(12984991945749810164)
XLA Ops:
  35.0 8.8 %collective-permute-done.2 = bf16[64,2048]{1,0:T(8,128)(2,1)S(1)} collective-permute-done((bf16[64,2048]{1,0:T(8,128)(2,1)S(1)}, bf16[64,2048]{1,0:T(8,128)(2,1)S(1)}, u32[]{:S(2)}, u32[]{:S(2)}) %collective-permute-start.2) | collective-permute-done | bytes 262176 | tf_op jit(solution)/shard_map/ppermute | solution.py:246
  46.9 5.6 %shard_map.257 = (bf16[1152,1024]{1,0:T(8,128)(2,1)}, bf16[1152,1024]{1,0:T(8,128)(2,1)}) custom-call(s32[6]{0:T(128)} %pad_add_fusion.refs_0_, bf16[2,288,1024]{2,1,0:T(8,128)(2,1)} %copy-done.17, bf16[1024,1024]{1,0:T(8,128)(2,1)} %get-tuple-element.106.refs_2_.refs_5_.refs_6_, ...), custom_call_target="tpu_custom_call", output_to_operand_aliasing={{0}: (5, {}), {1}: (6, {})} | custom-call | flops 966367616 | bytes 2831155 | tf_op jit(solution)/shard_map/pallas_call | solution.py:305
  54.8 34.1 %collective-permute-done.4.refs_3_.refs_8_.refs_40_.refs_9_ = bf16[256,2048]{1,0:T(8,128)(2,1)S(1)} collective-permute-done((bf16[256,2048]{1,0:T(8,128)(2,1)S(1)}, bf16[256,2048]{1,0:T(8,128)(2,1)S(1)}, u32[]{:S(2)}, u32[]{:S(2)}) %collective-permute-start.4) | collective-permute-done | bytes 1048608 | tf_op jit(solution)/shard_map/ppermute | solution.py:246
  95.2 7.6 %shard_map.258 = bf16[3,1152,512]{2,1,0:T(8,128)(2,1)} custom-call(bf16[1152,1024]{1,0:T(8,128)(2,1)} %get-tuple-element.113.refs_0_, f32[3,1,512]{2,1,0:T(1,128)} %copy.38.refs_1_, bf16[256,2048]{1,0:T(8,128)(2,1)} %pad_maximum_fusion.3.refs_7_.refs_2_.refs_6_.refs_38_, bf16[256,2048]{1,0:T(8,128)(2,1)} %copy-done.5, ...), custom_call_target="tpu_custom_call" | custom-call | flops 2899102976 | bytes 7235174 | tf_op jit(solution)/shard_map/pallas_call | solution.py:305
  102.8 10.1 %shard_map.259 = (bf16[2,2,288,512]{3,2,1,0:T(8,128)(2,1)}, bf16[2,8,576,576]{3,2,1,0:T(8,128)(2,1)}) custom-call(bf16[3,2,2,288,512]{4,3,2,1,0:T(8,128)(2,1)} %bitcast.253), custom_call_target="tpu_custom_call" | custom-call | flops 3261490688 | bytes 4246732 | tf_op jit(solution)/shard_map/pallas_call | solution.py:305
  118.1 10.4 %shard_map.260 = (bf16[2,2,288,512]{3,2,1,0:T(8,128)(2,1)}, bf16[2,8,576,576]{3,2,1,0:T(8,128)(2,1)}) custom-call(bf16[3,2,2,288,512]{4,3,2,1,0:T(8,128)(2,1)} %bitcast.254, bf16[2,2,288,512]{3,2,1,0:T(8,128)(2,1)} %get-tuple-element.117.refs_1_, bf16[2,8,576,576]{3,2,1,0:T(8,128)(2,1)} %get-tuple-element.118.refs_2_), custom_call_target="tpu_custom_call", output_to_operand_aliasing={{0}: (1, {}), {1}: (2, {})} | custom-call | flops 3261490688 | bytes 4246732 | tf_op jit(solution)/shard_map/pallas_call | solution.py:305
  134.5 7.7 %shard_map.261 = bf16[3,1152,512]{2,1,0:T(8,128)(2,1)} custom-call(bf16[1152,1024]{1,0:T(8,128)(2,1)} %get-tuple-element.113.refs_0_, f32[3,1,512]{2,1,0:T(1,128)} %broadcast_in_dim.13.refs_1_, bf16[272,2048]{1,0:T(8,128)(2,1)} %copy-done.3, bf16[272,2048]{1,0:T(8,128)(2,1)} %copy-done.4, bf16[2,272,2048]{2,1,0:T(8,128)(2,1)} %copy-done.2, ...), custom_call_target="tpu_custom_call" | custom-call | flops 2899102976 | bytes 7235174 | tf_op jit(solution)/shard_map/pallas_call | solution.py:305
  142.2 17.0 %shard_map.262 = (bf16[2,2,288,512]{3,2,1,0:T(8,128)(2,1)}, bf16[2,8,576,576]{3,2,1,0:T(8,128)(2,1)}) custom-call(bf16[3,2,2,288,512]{4,3,2,1,0:T(8,128)(2,1)} %bitcast.251), custom_call_target="tpu_custom_call" | custom-call | flops 6522981376 | bytes 8493465 | tf_op jit(solution)/shard_map/pallas_call | solution.py:305
  159.2 8.0 %shard_map.263 = (f32[1152,1024]{1,0:T(8,128)}, bf16[1152,1024]{1,0:T(8,128)(2,1)}) custom-call(bf16[1152,512]{1,0:T(8,128)(2,1)} %bitcast.247, bf16[1152,512]{1,0:T(8,128)(2,1)} %bitcast.264, bf16[1152,1024]{1,0:T(8,128)(2,1)} %get-tuple-element.124.refs_2_.refs_3_, f32[1,1024]{1,0:T(1,128)} %get-tuple-element.125.refs_3_, ...), custom_call_target="tpu_custom_call" | custom-call | flops 1932735232 | bytes 11114905 | tf_op jit(solution)/shard_map/pallas_call | solution.py:305
  167.1 13.9 %shard_map.264 = (bf16[1152,2048]{1,0:T(8,128)(2,1)}, bf16[1152,2048]{1,0:T(8,128)(2,1)}) custom-call(s32[6]{0:T(128)} %pad_add_fusion.refs_0_, bf16[1152,1024]{1,0:T(8,128)(2,1)} %get-tuple-element.128.refs_1_.refs_0_, f32[1,2048]{1,0:T(1,128)} %bitcast.284, bf16[16,2,64,2048]{3,2,1,0:T(8,128)(2,1)} %bitcast.172, bf16[16,2,64,2048]{3,2,1,0:T(8,128)(2,1)} %bitcast.173, ...), custom_call_target="tpu_custom_call" | custom-call | flops 3865470464 | bytes 12792627 | tf_op jit(solution)/shard_map/pallas_call | solution.py:305
  186.0 13.9 %shard_map.266 = (bf16[1152,2048]{1,0:T(8,128)(2,1)}, bf16[1152,2048]{1,0:T(8,128)(2,1)}) custom-call(s32[6]{0:T(128)} %pad_add_fusion.refs_0_, bf16[1152,1024]{1,0:T(8,128)(2,1)} %get-tuple-element.128.refs_1_.refs_0_, f32[1,2048]{1,0:T(1,128)} %bitcast.283, bf16[16,2,64,2048]{3,2,1,0:T(8,128)(2,1)} %bitcast.203, bf16[16,2,64,2048]{3,2,1,0:T(8,128)(2,1)} %bitcast.189, ...), custom_call_target="tpu_custom_call" | custom-call | flops 3865470464 | bytes 12792627 | tf_op jit(solution)/shard_map/pallas_call | solution.py:305
  199.9 15.1 %shard_map.267 = (bf16[2,256,2048]{2,1,0:T(8,128)(2,1)}, bf16[2,256,2048]{2,1,0:T(8,128)(2,1)}, bf16[2,256,2048]{2,1,0:T(8,128)(2,1)}, bf16[2,256,2048]{2,1,0:T(8,128)(2,1)}) custom-call(bf16[1152,1024]{1,0:T(8,128)(2,1)} %get-tuple-element.131.refs_19_.refs_0_.refs_1_.refs_4_, bf16[1152,2048]{1,0:T(8,128)(2,1)} %get-tuple-element.129.refs_4_.refs_1_, ...), custom_call_target="tpu_custom_call" | custom-call | flops 5798205952 | bytes 12111052 | tf_op jit(solution)/shard_map/pallas_call | solution.py:305
  215.2 19.2 %shard_map.268 = (bf16[1152,2048]{1,0:T(8,128)(2,1)}, bf16[1152,2048]{1,0:T(8,128)(2,1)}, f32[1,2048]{1,0:T(1,128)}, f32[1,2048]{1,0:T(1,128)}) custom-call(s32[6]{0:T(128)} %pad_add_fusion.refs_0_, bf16[1152,1024]{1,0:T(8,128)(2,1)} %get-tuple-element.131.refs_19_.refs_0_.refs_1_.refs_4_, bf16[1152,2048]{1,0:T(8,128)(2,1)} %get-tuple-element.136.refs_2_, ...), custom_call_target="tpu_custom_call" | custom-call | flops 5798205952 | bytes 19188940 | tf_op jit(solution)/shard_map/pallas_call | solution.py:305
  239.3 15.0 %shard_map.270 = (bf16[2,256,2048]{2,1,0:T(8,128)(2,1)}, bf16[2,256,2048]{2,1,0:T(8,128)(2,1)}, bf16[2,256,2048]{2,1,0:T(8,128)(2,1)}, bf16[2,256,2048]{2,1,0:T(8,128)(2,1)}) custom-call(bf16[1152,1024]{1,0:T(8,128)(2,1)} %get-tuple-element.128.refs_1_.refs_0_, bf16[1152,2048]{1,0:T(8,128)(2,1)} %get-tuple-element.139.refs_2_.refs_1_, ...), custom_call_target="tpu_custom_call" | custom-call | flops 5798205952 | bytes 12111052 | tf_op jit(solution)/shard_map/pallas_call | solution.py:305
  256.1 24.2 %shard_map.271 = (f32[1152,1024]{1,0:T(8,128)}, bf16[1152,1024]{1,0:T(8,128)(2,1)}, bf16[1152,512]{1,0:T(8,128)(2,1)}, bf16[1152,512]{1,0:T(8,128)(2,1)}, f32[8,1024]{1,0:T(8,128)}) custom-call(s32[6]{0:T(128)} %pad_add_fusion.refs_0_, bf16[1152,2048]{1,0:T(8,128)(2,1)} %get-tuple-element.139.refs_2_.refs_1_, bf16[1152,2048]{1,0:T(8,128)(2,1)} %get-tuple-element.140.refs_2_, ...), custom_call_target="tpu_custom_call" | custom-call | flops 7247757312 | bytes 20604518 | tf_op jit(solution)/shard_map/pallas_call | solution.py:305
  286.3 21.1 %shard_map.273 = (bf16[3,2,2,288,512]{4,3,2,1,0:T(8,128)(2,1)}, f32[2,2,512]{2,1,0:T(2,128)}) custom-call(bf16[3,2,2,288,512]{4,3,2,1,0:T(8,128)(2,1)} %bitcast.252, bf16[2,2,288,512]{3,2,1,0:T(8,128)(2,1)} %bitcast.298, bf16[2,8,576,576]{3,2,1,0:T(8,128)(2,1)} %get-tuple-element.149.refs_2_, bf16[512,2048]{1,0:T(8,128)(2,1)} %shard_map.272.refs_3_), custom_call_target="tpu_custom_call" | custom-call | flops 6522981376 | bytes 6370099 | tf_op jit(solution)/shard_map/pallas_call | solution.py:305
  311.6 10.5 %shard_map.275 = (bf16[256,2048]{1,0:T(8,128)(2,1)}, bf16[256,2048]{1,0:T(8,128)(2,1)}, bf16[256,2048]{1,0:T(8,128)(2,1)}, bf16[256,2048]{1,0:T(8,128)(2,1)}) custom-call(bf16[1152,1024]{1,0:T(8,128)(2,1)} %get-tuple-element.113.refs_0_, bf16[1152,1024]{1,0:T(8,128)(2,1)} %get-tuple-element.144.refs_2_.refs_1_, bf16[3,1152,512]{2,1,0:T(8,128)(2,1)} %bitcast.240, ...), custom_call_target="tpu_custom_call" | custom-call | flops 2899102976 | bytes 8178892 | tf_op jit(solution)/shard_map/pallas_call | solution.py:305
  322.5 13.5 %shard_map.276.refs_2_ = bf16[2,288,1024]{2,1,0:T(8,128)(2,1)} custom-call(s32[6]{0:T(128)} %pad_add_fusion.refs_0_, bf16[1152,2048]{1,0:T(8,128)(2,1)} %get-tuple-element.129.refs_4_.refs_1_, bf16[1152,2048]{1,0:T(8,128)(2,1)} %get-tuple-element.132.refs_2_, f32[1152,1024]{1,0:T(8,128)} %get-tuple-element.133.refs_3_, ...), custom_call_target="tpu_custom_call" | custom-call | flops 3623878656 | bytes 9987686 | tf_op jit(solution)/shard_map/pallas_call | solution.py:305
  346.6 21.1 %shard_map.279 = (bf16[3,2,2,288,512]{4,3,2,1,0:T(8,128)(2,1)}, f32[2,2,512]{2,1,0:T(2,128)}) custom-call(bf16[3,2,2,288,512]{4,3,2,1,0:T(8,128)(2,1)} %bitcast.255, bf16[2,2,288,512]{3,2,1,0:T(8,128)(2,1)} %bitcast.297, bf16[2,8,576,576]{3,2,1,0:T(8,128)(2,1)} %get-tuple-element.146.refs_2_, bf16[256,2048]{1,0:T(8,128)(2,1)} %get-tuple-element.160.refs_3_), custom_call_target="tpu_custom_call" | custom-call | flops 6522981376 | bytes 6370099 | tf_op jit(solution)/shard_map/pallas_call | solution.py:305
  368.7 10.6 %shard_map.280 = (bf16[256,2048]{1,0:T(8,128)(2,1)}, bf16[256,2048]{1,0:T(8,128)(2,1)}, bf16[256,2048]{1,0:T(8,128)(2,1)}, bf16[256,2048]{1,0:T(8,128)(2,1)}) custom-call(bf16[1152,1024]{1,0:T(8,128)(2,1)} %get-tuple-element.113.refs_0_, bf16[1152,1024]{1,0:T(8,128)(2,1)} %get-tuple-element.144.refs_2_.refs_1_, bf16[3,1152,512]{2,1,0:T(8,128)(2,1)} %bitcast.244, ...), custom_call_target="tpu_custom_call" | custom-call | flops 2899102976 | bytes 8178892 | tf_op jit(solution)/shard_map/pallas_call | solution.py:305
  393.0 12.2 %shard_map.284 = (bf16[2,288,1024]{2,1,0:T(8,128)(2,1)}, f32[8,1024]{1,0:T(8,128)}) custom-call(s32[6]{0:T(128)} %pad_add_fusion.refs_0_, bf16[3,1152,512]{2,1,0:T(8,128)(2,1)} %bitcast.245, bf16[3,1152,512]{2,1,0:T(8,128)(2,1)} %bitcast.241, bf16[1152,1024]{1,0:T(8,128)(2,1)} %get-tuple-element.124.refs_2_.refs_3_, ...), custom_call_target="tpu_custom_call" | custom-call | flops 1449551488 | bytes 4718592 | tf_op jit(solution)/shard_map/pallas_call | solution.py:305
  410.6 13.6 %collective-permute-done.25 = bf16[128,2048]{1,0:T(8,128)(2,1)} collective-permute-done((bf16[128,2048]{1,0:T(8,128)(2,1)}, bf16[128,2048]{1,0:T(8,128)(2,1)}, u32[]{:S(2)}, u32[]{:S(2)}) %collective-permute-start.25) | collective-permute-done | bytes 524320 | tf_op jit(solution)/shard_map/ppermute | solution.py:246
  426.0 12.6 %shard_map.287 = (bf16[4,288,1024]{2,1,0:T(8,128)(2,1)}, f32[8,1024]{1,0:T(8,128)}) custom-call(s32[6]{0:T(128)} %pad_add_fusion.refs_0_, bf16[3,1152,512]{2,1,0:T(8,128)(2,1)} %bitcast.246, bf16[3,1152,512]{2,1,0:T(8,128)(2,1)} %bitcast.242, bf16[1152,1024]{1,0:T(8,128)(2,1)} %get-tuple-element.124.refs_2_.refs_3_, ...), custom_call_target="tpu_custom_call" | custom-call | flops 1449551488 | bytes 4718592 | tf_op jit(solution)/shard_map/pallas_call | solution.py:305
  477.1 13.6 %shard_map.291.refs_2_ = bf16[4,288,1024]{2,1,0:T(8,128)(2,1)} custom-call(s32[6]{0:T(128)} %pad_add_fusion.refs_0_, bf16[1152,2048]{1,0:T(8,128)(2,1)} %get-tuple-element.129.refs_4_.refs_1_, bf16[1152,2048]{1,0:T(8,128)(2,1)} %get-tuple-element.132.refs_2_, f32[1152,1024]{1,0:T(8,128)} %get-tuple-element.133.refs_3_, ...), custom_call_target="tpu_custom_call" | custom-call | flops 3623878656 | bytes 9987686 | tf_op jit(solution)/shard_map/pallas_call | solution.py:305
  (250 shorter events, 156.4 us)
Async XLA Ops:
  7.3 121.2 %all-gather.5.cloned.1.call-start = ((), (), s32[]{:S(2)}) async-start(), calls=%async_computation | async-start | bytes 8650752 | tf_op jit(solution)/shard_map/all_gather | solution.py:936
  8.0 207.2 %all-gather.7.cloned.1.call-start = ((), (), s32[]{:S(2)}) async-start(), calls=%async_computation.1 | async-start | bytes 8650752 | tf_op jit(solution)/shard_map/all_gather | solution.py:969
  9.4 36.4 %collective-permute-start = (bf16[2,288,1024]{2,1,0:T(8,128)(2,1)S(1)}, bf16[2,288,1024]{2,1,0:T(8,128)(2,1)S(1)}, u32[]{:S(2)}, u32[]{:S(2)}) collective-permute-start(bf16[2,288,1024]{2,1,0:T(8,128)(2,1)S(1)} %constant_dynamic-slice_fusion.1), channel_id=1, source_target_pairs={{0,1},{1,0},{2,3},{3,2},{4,5},{5,4},{6,7},{7,6},{8,9},{9,8},{10,11... | collective-permute-start | bytes 3538952 | tf_op jit(solution)/shard_map/ppermute | solution.py:246
  16.2 27.6 %collective-permute-start.2 = (bf16[64,2048]{1,0:T(8,128)(2,1)S(1)}, bf16[64,2048]{1,0:T(8,128)(2,1)S(1)}, u32[]{:S(2)}, u32[]{:S(2)}) collective-permute-start(bf16[64,2048]{1,0:T(8,128)(2,1)S(1)} %constant_dynamic-update-slice_fusion), channel_id=1, source_target_pairs={{0,16},{2,18},{4,20},{6,22},{8,24},{10,26},{12,28},{14,30},{16,0},... | collective-permute-start | bytes 786440 | tf_op jit(solution)/shard_map/ppermute | solution.py:246
  16.2 27.6 %collective-permute-start.1 = (bf16[64,2048]{1,0:T(8,128)(2,1)S(1)}, bf16[64,2048]{1,0:T(8,128)(2,1)}, u32[]{:S(2)}, u32[]{:S(2)}) collective-permute-start(bf16[64,2048]{1,0:T(8,128)(2,1)S(1)} %constant_dynamic-update-slice_fusion), channel_id=1, source_target_pairs={{0,8},{2,10},{4,12},{6,14},{8,0},{10,2},{12,4},{14,6},{16,24},{18,... | collective-permute-start | bytes 786440 | tf_op jit(solution)/shard_map/ppermute | solution.py:246
  52.6 38.0 %collective-permute-start.5 = (bf16[272,2048]{1,0:T(8,128)(2,1)S(1)}, bf16[272,2048]{1,0:T(8,128)(2,1)S(1)}, u32[]{:S(2)}, u32[]{:S(2)}) collective-permute-start(bf16[272,2048]{1,0:T(8,128)(2,1)S(1)} %pad_maximum_fusion.2), channel_id=1, source_target_pairs={{0,1},{1,0},{2,3},{3,2},{4,5},{5,4},{6,7},{7,6},{8,9},{9,8},{10,11... | collective-permute-start | bytes 3342344 | tf_op jit(solution)/shard_map/ppermute | solution.py:246
  53.2 35.6 %collective-permute-start.4 = (bf16[256,2048]{1,0:T(8,128)(2,1)S(1)}, bf16[256,2048]{1,0:T(8,128)(2,1)S(1)}, u32[]{:S(2)}, u32[]{:S(2)}) collective-permute-start(bf16[256,2048]{1,0:T(8,128)(2,1)S(1)} %copy-done.1), channel_id=1, source_target_pairs={{0,4},{2,6},{4,0},{6,2},{8,12},{10,14},{12,8},{14,10},{16,20},{18,... | collective-permute-start | bytes 3145736 | tf_op jit(solution)/shard_map/ppermute | solution.py:246
  91.1 27.0 %collective-permute-start.7 = (bf16[272,2048]{1,0:T(8,128)(2,1)S(1)}, bf16[272,2048]{1,0:T(8,128)(2,1)S(1)}, u32[]{:S(2)}, u32[]{:S(2)}) collective-permute-start(bf16[272,2048]{1,0:T(8,128)(2,1)S(1)} %collective-permute-done.5.refs_2_.refs_7_.refs_39_.refs_8_), channel_id=1, source_target_pairs={{0,4},{2,6},{4,0},{6,2},{8,12},{10,14},{12,8},{14,10},{16,20},{18,... | collective-permute-start | bytes 3342344 | tf_op jit(solution)/shard_map/ppermute | solution.py:246
  130.8 50.3 %collective-permute-start.9 = (bf16[2,288,1024]{2,1,0:T(8,128)(2,1)S(1)}, bf16[2,288,1024]{2,1,0:T(8,128)(2,1)}, u32[]{:S(2)}, u32[]{:S(2)}) collective-permute-start(bf16[2,288,1024]{2,1,0:T(8,128)(2,1)S(1)} %constant_dynamic-slice_fusion), channel_id=1, source_target_pairs={{0,1},{1,0},{2,3},{3,2},{4,5},{5,4},{6,7},{7,6},{8,9},{9,8},{10,11... | collective-permute-start | bytes 3538952 | tf_op jit(solution)/shard_map/ppermute | solution.py:246
  254.3 26.1 %collective-permute-start.11 = (bf16[2,256,2048]{2,1,0:T(8,128)(2,1)}, bf16[2,256,2048]{2,1,0:T(8,128)(2,1)S(1)}, u32[]{:S(2)}, u32[]{:S(2)}) collective-permute-start(bf16[2,256,2048]{2,1,0:T(8,128)(2,1)} %get-tuple-element.151), channel_id=1, source_target_pairs={{0,2},{2,0},{4,6},{6,4},{8,10},{10,8},{12,14},{14,12},{16,18},{18,... | collective-permute-start | bytes 6291464 | tf_op jit(solution)/shard_map/ppermute | solution.py:246
  254.5 52.9 %collective-permute-start.13 = (bf16[512,2048]{1,0:T(8,128)(2,1)}, bf16[512,2048]{1,0:T(8,128)(2,1)}, u32[]{:S(2)}, u32[]{:S(2)}) collective-permute-start(bf16[512,2048]{1,0:T(8,128)(2,1)} %shard_map.269.refs_3_), channel_id=1, source_target_pairs={{0,4},{2,6},{4,0},{6,2},{8,12},{10,14},{12,8},{14,10},{16,20},{18,... | collective-permute-start | bytes 6291464 | tf_op jit(solution)/shard_map/ppermute | solution.py:246
  285.1 54.4 %collective-permute-start.15 = (bf16[512,2048]{1,0:T(8,128)(2,1)}, bf16[512,2048]{1,0:T(8,128)(2,1)S(1)}, u32[]{:S(2)}, u32[]{:S(2)}) collective-permute-start(bf16[512,2048]{1,0:T(8,128)(2,1)} %shard_map.272.refs_3_), channel_id=1, source_target_pairs={{0,1},{1,0},{2,3},{3,2},{4,5},{5,4},{6,7},{7,6},{8,9},{9,8},{10,11... | collective-permute-start | bytes 6291464 | tf_op jit(solution)/shard_map/ppermute | solution.py:246
  345.3 39.7 %collective-permute-start.20 = (bf16[256,2048]{1,0:T(8,128)(2,1)}, bf16[256,2048]{1,0:T(8,128)(2,1)}, u32[]{:S(2)}, u32[]{:S(2)}) collective-permute-start(bf16[256,2048]{1,0:T(8,128)(2,1)} %get-tuple-element.170), channel_id=1, source_target_pairs={{0,1},{1,0},{2,3},{3,2},{4,5},{5,4},{6,7},{7,6},{8,9},{9,8},{10,11... | collective-permute-start | bytes 3145736 | tf_op jit(solution)/shard_map/ppermute | solution.py:246
  346.2 36.0 %collective-permute-start.21 = (bf16[256,2048]{1,0:T(8,128)(2,1)S(1)}, bf16[256,2048]{1,0:T(8,128)(2,1)}, u32[]{:S(2)}, u32[]{:S(2)}) collective-permute-start(bf16[256,2048]{1,0:T(8,128)(2,1)S(1)} %copy-done.13), channel_id=1, source_target_pairs={{0,4},{2,6},{4,0},{6,2},{8,12},{10,14},{12,8},{14,10},{16,20},{18,... | collective-permute-start | bytes 3145736 | tf_op jit(solution)/shard_map/ppermute | solution.py:246
  379.3 31.2 %collective-permute-start.26 = (bf16[2,288,1024]{2,1,0:T(8,128)(2,1)S(1)}, bf16[2,288,1024]{2,1,0:T(8,128)(2,1)S(1)}, u32[]{:S(2)}, u32[]{:S(2)}) collective-permute-start(bf16[2,288,1024]{2,1,0:T(8,128)(2,1)S(1)} %copy-done.9), channel_id=1, source_target_pairs={{0,1},{1,0},{2,3},{3,2},{4,5},{5,4},{6,7},{7,6},{8,9},{9,8},{10,11... | collective-permute-start | bytes 3538952 | tf_op jit(solution)/shard_map/ppermute | solution.py:246
  380.3 26.3 %collective-permute-start.18 = (bf16[256,2048]{1,0:T(8,128)(2,1)}, bf16[256,2048]{1,0:T(8,128)(2,1)}, u32[]{:S(2)}, u32[]{:S(2)}) collective-permute-start(bf16[256,2048]{1,0:T(8,128)(2,1)} %get-tuple-element.166), channel_id=1, source_target_pairs={{0,4},{2,6},{4,0},{6,2},{8,12},{10,14},{12,8},{14,10},{16,20},{18,... | collective-permute-start | bytes 3145736 | tf_op jit(solution)/shard_map/ppermute | solution.py:246
  387.5 36.6 %collective-permute-start.25 = (bf16[128,2048]{1,0:T(8,128)(2,1)}, bf16[128,2048]{1,0:T(8,128)(2,1)}, u32[]{:S(2)}, u32[]{:S(2)}) collective-permute-start(bf16[128,2048]{1,0:T(8,128)(2,1)} %get-tuple-element.175), channel_id=1, source_target_pairs={{0,16},{2,18},{4,20},{6,22},{8,24},{10,26},{12,28},{14,30},{16,0},... | collective-permute-start | bytes 1572872 | tf_op jit(solution)/shard_map/ppermute | solution.py:246
  389.2 76.0 %collective-permute-start.24 = (bf16[256,2048]{1,0:T(8,128)(2,1)S(1)}, bf16[256,2048]{1,0:T(8,128)(2,1)}, u32[]{:S(2)}, u32[]{:S(2)}) collective-permute-start(bf16[256,2048]{1,0:T(8,128)(2,1)S(1)} %copy-done.12), channel_id=1, source_target_pairs={{0,1},{1,0},{2,3},{3,2},{4,5},{5,4},{6,7},{7,6},{8,9},{9,8},{10,11... | collective-permute-start | bytes 3145736 | tf_op jit(solution)/shard_map/ppermute | solution.py:246
  392.6 72.6 %collective-permute-start.23 = (bf16[256,2048]{1,0:T(8,128)(2,1)}, bf16[256,2048]{1,0:T(8,128)(2,1)}, u32[]{:S(2)}, u32[]{:S(2)}) collective-permute-start(bf16[256,2048]{1,0:T(8,128)(2,1)} %shard_map.283.refs_13_), channel_id=1, source_target_pairs={{0,4},{2,6},{4,0},{6,2},{8,12},{10,14},{12,8},{14,10},{16,20},{18,... | collective-permute-start | bytes 3145736 | tf_op jit(solution)/shard_map/ppermute | solution.py:246
  409.1 32.2 %collective-permute-start.28 = (bf16[128,2048]{1,0:T(8,128)(2,1)}, bf16[128,2048]{1,0:T(8,128)(2,1)}, u32[]{:S(2)}, u32[]{:S(2)}) collective-permute-start(bf16[128,2048]{1,0:T(8,128)(2,1)} %get-tuple-element.179), channel_id=1, source_target_pairs={{0,16},{2,18},{4,20},{6,22},{8,24},{10,26},{12,28},{14,30},{16,0},... | collective-permute-start | bytes 1572872 | tf_op jit(solution)/shard_map/ppermute | solution.py:246
  441.2 24.0 %collective-permute-start.22 = (bf16[256,2048]{1,0:T(8,128)(2,1)}, bf16[256,2048]{1,0:T(8,128)(2,1)S(1)}, u32[]{:S(2)}, u32[]{:S(2)}) collective-permute-start(bf16[256,2048]{1,0:T(8,128)(2,1)} %get-tuple-element.174), channel_id=1, source_target_pairs={{0,2},{2,0},{4,6},{6,4},{8,10},{10,8},{12,14},{14,12},{16,18},{18,... | collective-permute-start | bytes 3145736 | tf_op jit(solution)/shard_map/ppermute | solution.py:246
  469.3 25.8 %collective-permute-start.34 = (bf16[2,288,1024]{2,1,0:T(8,128)(2,1)}, bf16[2,288,1024]{2,1,0:T(8,128)(2,1)}, u32[]{:S(2)}, u32[]{:S(2)}) collective-permute-start(bf16[2,288,1024]{2,1,0:T(8,128)(2,1)} %get-tuple-element.193.refs_2_), channel_id=1, source_target_pairs={{0,1},{1,0},{2,3},{3,2},{4,5},{5,4},{6,7},{7,6},{8,9},{9,8},{10,11... | collective-permute-start | bytes 3538952 | tf_op jit(solution)/shard_map/ppermute | solution.py:246
  472.7 24.7 %collective-permute-start.36 = (bf16[64,2048]{1,0:T(8,128)(2,1)}, bf16[64,2048]{1,0:T(8,128)(2,1)S(1)}, u32[]{:S(2)}, u32[]{:S(2)}) collective-permute-start(bf16[64,2048]{1,0:T(8,128)(2,1)} %get-tuple-element.194), channel_id=1, source_target_pairs={{0,8},{2,10},{4,12},{6,14},{8,0},{10,2},{12,4},{14,6},{16,24},{18,... | collective-permute-start | bytes 786440 | tf_op jit(solution)/shard_map/ppermute | solution.py:246
  474.0 23.4 %collective-permute-start.37 = (bf16[64,2048]{1,0:T(8,128)(2,1)}, bf16[64,2048]{1,0:T(8,128)(2,1)S(1)}, u32[]{:S(2)}, u32[]{:S(2)}) collective-permute-start(bf16[64,2048]{1,0:T(8,128)(2,1)} %get-tuple-element.195), channel_id=1, source_target_pairs={{0,16},{2,18},{4,20},{6,22},{8,24},{10,26},{12,28},{14,30},{16,0},... | collective-permute-start | bytes 786440 | tf_op jit(solution)/shard_map/ppermute | solution.py:246
  (61 other events, 522.2 us)
Sparse Core Ops, SparseCore 0:
  11.1 94.1 all-gather.4
  128.7 80.7 all-gather.6

commit v5 on v4

--- a/solution.py
+++ b/solution.py
@@ -233,7 +233,7 @@
 
 ROWS = 64
 PART = 256
-VMEM_BYTES = 60 * 1024 * 1024
+VMEM_BYTES = 24 * 1024 * 1024
 COST_PART = 0.6
 FORWARD_PART = 0.8
 LOG2_E = 1.4426950408889634
@@ -348,6 +348,16 @@
     return jax.ShapeDtypeStruct(shape, dtype)
 
 
+def outer(shape, dtype=BF16):
+    return pltpu.HBM(shape, dtype)
+
+
+def in_hbm(values):
+    if isinstance(values, (list, tuple)):
+        return [in_hbm(part) for part in values]
+    return pltpu.with_memory_space_constraint(values, pltpu.HBM)
+
+
 ANYWHERE = pl.BlockSpec(memory_space=pl.ANY)
 
 
@@ -380,11 +390,50 @@
         (columns // tile,),
         [pl.BlockSpec((pieces, rows, tile), lambda j: (0, 0, j))] * given,
         [pl.BlockSpec((rows, tile), lambda j: (0, j))] * pieces,
-        [struct((rows, columns), dtype)] * pieces,
+        [outer((rows, columns), dtype)] * pieces,
         0,
         2 * pieces * rows * columns * (given + 1),
         after,
     )(*arrays)
+
+
+def finish(low_near, up_near, small, near, middle, far, after=()):
+    rows, columns = low_near.shape
+    split = columns * 3 // 4
+    height = small.shape[0] // 2
+
+    def kernel(low_ref, up_ref, small_ref, near_ref, middle_ref, far_ref, qkv_ref, out_ref, up_out_ref, sum_ref):
+        def rows_of(ref, start):
+            return ref[start : start + rows, :].astype(F32)
+
+        def vectors_of(ref, start):
+            values = ref[start : start + 2 * height, :].astype(F32)
+            return values[:height] + values[height:]
+
+        low = (rows_of(low_ref, 0) + rows_of(near_ref, 0)) + (rows_of(middle_ref, 0) + rows_of(far_ref, 0))
+        qkv_ref[...] = low[:, :split]
+        out_ref[...] = low[:, split:]
+        up_out_ref[...] = rows_of(up_ref, 0) + rows_of(near_ref, rows)
+        sum_ref[...] = (vectors_of(small_ref, 0) + vectors_of(near_ref, 2 * rows)) + (
+            vectors_of(middle_ref, rows) + vectors_of(far_ref, rows)
+        )
+
+    given = [low_near, up_near, small, near, middle, far]
+    return call(
+        kernel,
+        (1,),
+        [fixed(*values.shape) for values in given],
+        [fixed(rows, split), fixed(rows, columns - split), fixed(rows, columns), fixed(height, columns)],
+        [
+            struct((rows, split), F32),
+            struct((rows, columns - split), F32),
+            struct((rows, columns), F32),
+            struct((height, columns), F32),
+        ],
+        0,
+        20 * rows * columns,
+        after,
+    )(*given)
 
 
 def first_step():
@@ -450,7 +499,7 @@
         [image_block(height, width, offset), fixed(width, width), fixed(1, width), fixed(1, width)]
         + [ANYWHERE] * len(old),
         [out, out],
-        [struct((2 * mine * height, width))] * 2,
+        [outer((2 * mine * height, width))] * 2,
         2 * mine * height * width * width,
         6 * mine * height * width,
         after,
@@ -508,7 +557,7 @@
         [fixed(count, width), pl.BlockSpec((1, 1, half), lambda j: (j, 0, 0))]
         + piece_tiles(half, 2, 1),
         pl.BlockSpec((1, count, half), lambda j: (j, 0, 0)),
-        struct((3, count, half)),
+        outer((3, count, half)),
         6 * count * width * half,
         2 * count * (width + 3 * half) + 6 * width * half,
         after,
@@ -546,13 +595,13 @@
             pl.BlockSpec((2, 1, half_len, lanes), lambda i, j: (0, first_image + i, 0, j)),
             pl.BlockSpec((1, per_step, length, length), lambda i, j: (first_image + i, j, 0, 0)),
         ],
-        [struct((2, images, half_len, half)), struct((images, heads, length, length))],
+        [struct((2, images, half_len, half)), outer((images, heads, length, length))],
         24 * (last_image - first_image) * heads * length * length * HDIM,
         (last_image - first_image) * heads * length * length * 2,
         after,
         {1: 0, 2: 1} if old else None,
         part=FORWARD_PART,
-    )(projected, *old)
+    )(in_hbm(projected), *old)
 
 
 def attend_back(projected, grad_context, probs, lanes=256, after=()):
@@ -596,41 +645,41 @@
         32 * images * heads * length * length * HDIM,
         images * heads * length * length * 2,
         after,
-    )(projected, grad_context, probs)
-
-
-def add_branch(contexts, rows, pieces, bias, gain, shift, tile=288, after=()):
+    )(in_hbm(projected), grad_context, in_hbm(probs))
+
+
+def add_branch(places, contexts, rows, gathered, bias, gain, shift, tile=288, after=()):
     count, width = rows.shape
     half = width // 2
 
-    def kernel(low_ref, high_ref, rows_ref, bias_ref, gain_ref, shift_ref, *refs):
-        parts, (middle_ref, norm_ref) = far_list(refs[:4], refs[4:6]), refs[6:]
-        found = []
-        for at in range(4):
-            found.append(dot_nt(low_ref[...], parts[2 * at][...]) + dot_nt(high_ref[...], parts[2 * at + 1][...]))
-        middle = rows_ref[...].astype(F32) + (jnp.concatenate(found, axis=1) + bias_ref[...])
+    def kernel(place_ref, low_ref, high_ref, rows_ref, bias_ref, gain_ref, shift_ref, *refs):
+        middle_ref, norm_ref = refs[32:]
+        branch = dot_nt(low_ref[...], joined(refs, 0, 16, 2, 0)) + dot_nt(high_ref[...], joined(refs, 0, 16, 2, 1))
+        middle = rows_ref[...].astype(F32) + (branch + bias_ref[...])
         middle_ref[...] = middle
         unit, _ = normal_parts(middle)
         norm_ref[...] = (unit * gain_ref[...] + shift_ref[...]).astype(BF16)
 
-    block = pl.BlockSpec((tile, width), lambda i: (i, 0))
-    half_block = pl.BlockSpec((tile, half), lambda i: (i, 0))
+    block = pl.BlockSpec((tile, width), lambda i, _: (i, 0))
+    half_block = pl.BlockSpec((tile, half), lambda i, _: (i, 0))
     return call(
         kernel,
         (count // tile,),
-        [half_block, half_block, block] + [fixed(1, width)] * 3 + piece_specs(half, 3),
+        [half_block, half_block, block] + [fixed(1, width)] * 3 + gathered_specs(half, at=4),
         [block, block],
-        [struct((count, width), F32), struct((count, width))],
+        [outer((count, width), F32), struct((count, width))],
         2 * count * width * width,
         10 * count * width + 2 * width * width,
         after,
+        None,
+        1,
         part=FORWARD_PART,
-    )(*contexts, rows, bias, gain, shift, *pieces)
+    )(places, *contexts, rows, bias, gain, shift, *[gathered] * 32)
 
 
 def feed_up(places, x_at, second, gathered, bias, tile=512, after=()):
     count, width = second.shape
-    columns = gathered.shape[-1]
+    columns = bias.shape[-1]
 
     def kernel(place_ref, second_ref, bias_ref, *refs):
         hidden = dot_nn(second_ref[...], joined(refs, 0, 16)) + bias_ref[...]
@@ -644,7 +693,7 @@
         (columns // tile,),
         [fixed(count, width), pl.BlockSpec((1, tile), lambda j, _: (0, j))] + gathered_specs(tile, (x_at,)),
         [block, block],
-        [struct((count, columns))] * 2,
+        [outer((count, columns))] * 2,
         2 * count * width * columns,
         2 * count * (width + 2 * columns) + 2 * width * columns,
         after,
@@ -690,7 +739,7 @@
         after,
         {38: 0} if old else None,
         1,
-    )(side, *actives, middle, bias, order, *[gathered] * 32, *old)
+    )(side, *[in_hbm(values) for values in actives], in_hbm(middle), bias, order, *[gathered] * 32, *old)
 
 
 def gate_back(side, final, slopes, gathered, tile=512, after=()):
@@ -718,7 +767,7 @@
         after,
         None,
         1,
-    )(side, final, *slopes, *[gathered] * 32)
+    )(side, in_hbm(final), *in_hbm(slopes), *[gathered] * 32)
 
 
 def sums_down(final, actives, tile=512, after=()):
@@ -739,11 +788,11 @@
         (columns // tile,),
         [fixed(count, width), right, right],
         [pl.BlockSpec((2, PART, tile), lambda j: (0, 0, j))] * 4,
-        [struct((2, PART, columns))] * 4,
+        [outer((2, PART, columns))] * 4,
         4 * count * width * columns,
         4 * count * columns + 2 * count * width + 4 * width * columns,
         after,
-    )(final, *actives)
+    )(final, *[in_hbm(values) for values in actives])
 
 
 def sums_up(second, grads, tile=512, after=()):
@@ -764,7 +813,7 @@
         (columns // tile,),
         [fixed(count, width), right, right],
         [pl.BlockSpec((2, PART, tile), lambda j: (0, 0, j))] * 4,
-        [struct((2, PART, columns))] * 4,
+        [outer((2, PART, columns))] * 4,
         4 * count * width * columns,
         4 * count * columns + 2 * count * width + 4 * width * columns,
         after,
@@ -796,21 +845,21 @@
         (4,),
         [left, left, pl.BlockSpec((1, count, half), lambda j: (jnp.minimum(j, 2), 0, 0)), fixed(count, half)],
         [pl.BlockSpec((PART, half), lambda j: (0, j))] * 4,
-        [struct((PART, 4 * half))] * 4,
+        [outer((PART, 4 * half))] * 4,
         8 * count * width * half,
         2 * count * (2 * width + 4 * half) + 8 * width * half,
         after,
     )(normed, branch, grad_projected, context)
 
 
-def second_back(places, grads, gathered, first_pieces, middle, final, gain, tile=288, after=()):
+def second_back(places, grads, gathered, middle, final, gain, tile=288, after=()):
     count, columns = grads[0].shape
     width = middle.shape[1]
     half = width // 2
 
     def kernel(place_ref, low_ref, high_ref, middle_ref, final_ref, gain_ref, *refs):
-        ups, outs = refs[:32], far_list(refs[32:36], refs[36:38])
-        grad_ref, branch_ref, context_low_ref, context_high_ref, sum_ref = refs[38:]
+        ups, outs = refs[:32], refs[32:64]
+        grad_ref, branch_ref, context_low_ref, context_high_ref, sum_ref = refs[64:]
         grad_second = dot_nt(low_ref[...], joined(ups, 0, 16, 2, 0)) + dot_nt(high_ref[...], joined(ups, 0, 16, 2, 1))
         unit, inv_std = normal_parts(middle_ref[...])
         grad_middle = final_ref[...].astype(F32) + normalize_back(
@@ -820,8 +869,7 @@
         grad_ref[...] = grad_middle
         branch_ref[...] = branch
         for x_at, context_ref in enumerate((context_low_ref, context_high_ref)):
-            weight = jnp.concatenate([outs[2 * at + x_at][...] for at in range(4)], axis=0)
-            context_ref[...] = dot_nn(branch, weight).astype(BF16)
+            context_ref[...] = dot_nn(branch, joined(outs, 0, 16, 2, x_at)).astype(BF16)
 
         @pl.when(first_step())
         def _():
@@ -839,9 +887,9 @@
         (count // tile,),
         [hidden, hidden, block, block, fixed(1, width)]
         + gathered_specs(columns, at=0)
-        + piece_specs(half, 3),
+        + gathered_specs(half, at=4),
         [block, block, half_block, half_block, fixed(8, width)],
-        [struct((count, width), F32), struct((count, width))]
+        [outer((count, width), F32), struct((count, width))]
         + [struct((count, half))] * 2
         + [struct((8, width), F32)],
         4 * count * width * columns + 2 * count * width * width,
@@ -849,7 +897,7 @@
         after,
         None,
         1,
-    )(places, *grads, middle, final, gain, *[gathered] * 32, *first_pieces)
+    )(places, *grads, middle, final, gain, *[gathered] * 64)
 
 
 def first_back(side, half_at, grads, pieces, rows, grad_middle, gain, order, tile=288, after=()):
@@ -894,7 +942,7 @@
         None,
         1,
         part=0.3,
-    )(side, *grads, rows, grad_middle, gain, order, *pieces)
+    )(side, *in_hbm(grads), in_hbm(rows), in_hbm(grad_middle), gain, order, *in_hbm(pieces))
 
 
 def fast_shards(
@@ -933,14 +981,15 @@
     def z_all(values):
         return jnp.concatenate([values] + [over_z(values, step) for step in (1, 2, 3)], axis=0)
 
-    up_all = lax.all_gather(up_weight, ("dp", "tensor")).reshape(-1, 2, ROWS, half_hidden)
+    second_group = jnp.concatenate([up_weight, out_weight], axis=1)
+    up_all = lax.all_gather(second_group, ("dp", "tensor")).reshape(-1, 2, ROWS, half_hidden + half)
     own = prepare(side_array, tokens, order, gain_one, shift_one, 0)
     final, sum_own = mask_grad(side_array, out_grad, order, 0, after=own[:1])
     tokens_partner = for_partner(tokens)
-    first = jnp.concatenate([qkv_weight.reshape(ROWS, 3 * half), out_weight], axis=1)
+    first = qkv_weight.reshape(ROWS, 3 * half)
     first_base = late(z_all(first), final)
     biases = jnp.concatenate([qv_bias.reshape(-1), up_bias])
-    bias_rows = jnp.pad(biases, (0, 16 * half_hidden - biases.size)).reshape(16, half_hidden)
+    bias_rows = jnp.pad(biases, (0, 16 * 3 * half - biases.size)).reshape(16, 3 * half)
 
     def split_bias(bias):
         bias = bias.astype(F32)
@@ -950,10 +999,10 @@
     rows, normed = prepare(
         side_array, tokens_partner, order, gain_one, shift_one, 1, own, after=[first_base]
     )
-    first_x = over_x(jnp.concatenate([late(first_base, normed), bias_rows], axis=0))
-    first_y = over_y(late(first_base, normed))
+    first_x = over_x(jnp.concatenate([first_base, bias_rows], axis=0))
+    first_y = over_y(first_base)
     first_xy = over_y(late(first_x, first_y))
-    first_far = [over_core(jnp.stack(late([first_base, first_y], first_x)))]
+    first_far = [over_core(jnp.stack(late([first_base, first_y], first_x, normed)))]
     biases = [split_bias(biases), split_bias(first_x[4 * ROWS :].reshape(-1)[: biases.size])]
     heads_shape = (3, 2, mine, half_len, half)
     projected, contexts, probs = [None, None], [None, None], [None, None]
@@ -970,7 +1019,7 @@
     down_all = down_all.reshape(-1, 2, ROWS, half_hidden)
     contexts[1], probs[1] = attend(projected[1], 0, 2)
     contexts = [values.reshape(count, half) for values in contexts]
-    middle, second = add_branch(contexts, rows, first_pieces, bias_out, gain_two, shift_two)
+    middle, second = add_branch(side_array, contexts, rows, up_all, bias_out, gain_two, shift_two)
     actives, slopes = [None, None], [None, None]
     actives[0], slopes[0] = feed_up(side_array, 0, second, up_all, biases[0][1])
     final, sum_partner = mask_grad(side_array, grad_partner, order, 1, final, after=[actives[0]])
@@ -983,7 +1032,7 @@
     down_sent_y = over_y(down_sent)
     up_near, up_next, up_far_sums, up_last = sums_up(second, grads, after=[down_sent])
     grad_middle, branch, *grad_contexts, sums_two = second_back(
-        side_array, grads, up_all, first_pieces, middle, final, gain_two, after=[up_near]
+        side_array, grads, up_all, middle, final, gain_two, after=[up_near]
     )
     (up_sent,) = combine([up_next, over_core(up_last)], 1, after=[branch])
     up_sent_x = over_x(up_sent)
@@ -1010,14 +1059,14 @@
     high_far = over_core(late(high_far, up_sums[0]))
     out_partner = over_x(late(out_send, up_sums[0]))
     grads_qkv[0], sums_qkv[0] = heads_back(0, up_sums[:1])
+    down_sums = combine([down_sums[0], down_sent_x], 2, after=[high_far, grads_qkv[0]])
+    down_sent_z = over_z(down_sums[1], 2)
     low_near, low_next, low_far, low_last = sums_first(
-        normed, branch, grads_qkv[0], contexts[0], after=[high_far]
+        normed, branch, grads_qkv[0], contexts[0], after=down_sums[:1]
     )
     (high,) = combine([high_near, high_far, high_sent_y], 1, after=[low_near])
     high_x = over_x(high)
-    down_sums = combine([down_sums[0], down_sent_x], 2, after=[high])
-    down_sent_z = over_z(down_sums[1], 2)
-    (low_sent,) = combine([low_next, over_core(low_last)], 1, after=down_sums[:1])
+    (low_sent,) = combine([low_next, over_core(low_last)], 1, after=[high])
     low_sent_y = over_y(low_sent)
     send, sums_partner = first_back(
         side_array, 1, grads_qkv, first_pieces, rows, grad_middle, gain_one, order, after=[low_sent]
@@ -1031,9 +1080,6 @@
         side_array, 0, grads_qkv, first_pieces, rows, grad_middle, gain_one, order, after=down_sums[:1]
     )
     up_sums = combine([up_sums[0], up_sent_z], 2, after=[full])
-    up_sent_z = over_z(up_sums[1], 1)
-    (grad_down,) = combine([down_sums[0], down_sent_z], 1, F32, after=up_sums[:1])
-
     sums = jnp.concatenate(
         [(sums_own + sums_partner)[:2], sums_two[2:3], sums_two[:2], sum_own + sum_partner], axis=0
     )
@@ -1041,35 +1087,42 @@
     halves = [
         jnp.concatenate([sums_qkv[x_at].reshape(-1), sum_hidden[x_at][0]]) for x_at in range(2)
     ]
-    small = late(jnp.concatenate([halves[0], sums.reshape(-1), halves[1]]), up_sums[0])
-    small = small + over_core(small)
+    small = jnp.concatenate([halves[0], sums.reshape(-1), halves[1]])
+    small = late(small + over_core(small), up_sums[0])
     small = small + over_y(small)
-    small = (small + over_z(small, 1)) + (over_z(small, 2) + over_z(small, 3))
     halves_size = 2 * half + half_hidden
     small_x = over_x(jnp.concatenate([small[-halves_size:], small[halves_size:-halves_size]]))
-
-    low = combine([low_near, low_far, low_sent_y, high_x], 4, after=[grad_down])
-    low_z = [over_z(low[step], step) for step in (1, 2, 3)]
+    small = small[:-halves_size] + small_x
+    height = 8
+    small_rows = jnp.pad(small, (0, height * half_hidden - small.size)).reshape(height, half_hidden)
+    small_top = small_rows.astype(BF16)
+    small_rows = jnp.concatenate([small_top, (small_rows - small_top.astype(F32)).astype(BF16)], axis=0)
+
+    low = combine([low_near, low_far, low_sent_y, high_x], 4, after=up_sums[:1])
+    near_z = over_z(jnp.concatenate([low[1], up_sums[1], small_rows], axis=0), 1)
+    middle_z = over_z(jnp.concatenate([low[2], small_rows], axis=0), 2)
+    far_z = over_z(jnp.concatenate([low[3], small_rows], axis=0), 3)
     send_x = over_x(late(send, low[0]))
     out_full = feed_down(
-        side_array, 0, 2, actives, middle, down_all, bias_down, order, after=[low[0], small]
-    )
+        side_array, 0, 2, actives, middle, down_all, bias_down, order, after=[low[0], small_rows]
+    )
+    (grad_down,) = combine([down_sums[0], down_sent_z], 1, F32, after=[out_full])
     block_out = lax.dynamic_update_slice_in_dim(out_full, out_partner, (1 - side) * mine, 0)
-    (grad_up,) = combine([up_sums[0], up_sent_z], 1, F32, after=[out_full])
     tokens_grad = lax.dynamic_update_slice_in_dim(full, send_x, (1 - side) * mine, 0)
-    (grad_first,) = combine([low[0]] + low_z, 1, F32, after=[grad_up, tokens_grad])
-
-    small = small[:-halves_size] + small_x
-    halves = small[:halves_size]
-    sums = small[halves_size:].reshape(6, width)
+    grad_qkv, grad_out, grad_up, sums = finish(
+        low[0], up_sums[0], small_rows, near_z, middle_z, far_z, after=[out_full, tokens_grad]
+    )
+    sums = sums.reshape(-1)
+    halves = sums[:halves_size]
+    sums = sums[halves_size : halves_size + 6 * width].reshape(6, width)
     return (
         block_out,
         tokens_grad,
         sums[0],
         sums[1],
-        grad_first[:, : 3 * half].reshape(ROWS, 3, half),
+        grad_qkv.reshape(ROWS, 3, half),
         halves[: 2 * half].reshape(2, half),
-        grad_first[:, 3 * half :],
+        grad_out,
         sums[2],
         sums[3],
         sums[4],

time: 520 us -> 495 us (0.952)
  Pallas kernels: 342 us -> 292 us
  local copies, waits for them, and re-layouts: 27.8 us -> 54.8 us
  waiting for transfers between devices: 86 us -> 77.5 us
    pallas_call x40 -> x39, Pallas kernels: 342 us -> 292 us  [call(): return lambda *arrays: function(*arrays, *after)]
    unnamed x97 -> x203, local copies, waits for them, and re-layouts: 11 us -> 46 us
    ppermute x40 -> x36, waiting for transfers between devices: 85.3 us -> 75.7 us  [swap(): lax.ppermute(values, axis_name, [(place, place ^ flip) for place in range...]
    ppermute x40 -> x36, starting transfers between devices: 33.7 us -> 35.5 us  [swap(): lax.ppermute(values, axis_name, [(place, place ^ flip) for place in range...]
  transfers between devices with their start and end apart: 42 -> 38, of which waited for: 15 -> 14; matrix products, arithmetic and copies ran while one was open for 4% -> 3% of each run, Pallas kernels for 62% -> 57%
where the time goes in v5:
time: 495 us; the launch traced here: 486 us
  Pallas kernels  292 us (59%)
  waiting for transfers between devices  77.5 us (16%)
  local copies, waits for them, and re-layouts  54.8 us (11%)
  starting transfers between devices  35.6 us (7%)
  between operations  15.6 us (3%)
  other arithmetic  8.32 us (2%)
    pallas_call x39, Pallas kernels, call(): return lambda *arrays: function(*arrays, *after)  292 us
    ppermute x36, waiting for transfers between devices, swap(): lax.ppermute(values, axis_name, [(place, place ^ flip) for place in range...  75.7 us
    unnamed x203, local copies, waits for them, and re-layouts  46 us
    ppermute x36, starting transfers between devices, swap(): lax.ppermute(values, axis_name, [(place, place ^ flip) for place in range...  35.5 us
  transfers between devices with their start and end apart: 38, of which 14 were waited for; matrix products, arithmetic and copies ran while one was open for 3% of the time, Pallas kernels for 57%

profile of v5, /device:TPU:0, one launch (start us, length us, event | category | flops | bytes accessed | tf_op | source)
XLA Modules:
  0.0 485.5 jit_solution(11014618682149559300)
XLA Ops:
  29.0 10.0 %collective-permute-done.2 = bf16[64,1536]{1,0:T(8,128)(2,1)S(1)} collective-permute-done((bf16[64,1536]{1,0:T(8,128)(2,1)S(1)}, bf16[64,1536]{1,0:T(8,128)(2,1)S(1)}, u32[]{:S(2)}, u32[]{:S(2)}) %collective-permute-start.2) | collective-permute-done | bytes 196640 | tf_op jit(solution)/shard_map/ppermute | solution.py:246
  44.0 10.0 %collective-permute-done.refs_1_ = bf16[2,288,1024]{2,1,0:T(8,128)(2,1)} collective-permute-done((bf16[2,288,1024]{2,1,0:T(8,128)(2,1)}, bf16[2,288,1024]{2,1,0:T(8,128)(2,1)}, u32[]{:S(2)}, u32[]{:S(2)}) %collective-permute-start) | collective-permute-done | bytes 1179680 | tf_op jit(solution)/shard_map/ppermute | solution.py:246
  58.7 6.8 %collective-permute-done.4.refs_3_.refs_9_ = bf16[256,1536]{1,0:T(8,128)(2,1)S(1)} collective-permute-done((bf16[256,1536]{1,0:T(8,128)(2,1)S(1)}, bf16[256,1536]{1,0:T(8,128)(2,1)S(1)}, u32[]{:S(2)}, u32[]{:S(2)}) %collective-permute-start.4) | collective-permute-done | bytes 786464 | tf_op jit(solution)/shard_map/ppermute | solution.py:246
  65.5 9.8 %collective-permute-done.5.refs_2_.refs_8_ = bf16[272,1536]{1,0:T(8,128)(2,1)S(1)} collective-permute-done((bf16[272,1536]{1,0:T(8,128)(2,1)S(1)}, bf16[272,1536]{1,0:T(8,128)(2,1)S(1)}, u32[]{:S(2)}, u32[]{:S(2)}) %collective-permute-start.5) | collective-permute-done | bytes 835616 | tf_op jit(solution)/shard_map/ppermute | solution.py:246
  92.6 10.0 %shard_map.259 = (bf16[2,2,288,512]{3,2,1,0:T(8,128)(2,1)S(1)}, bf16[2,8,576,576]{3,2,1,0:T(8,128)(2,1)}) custom-call(bf16[3,2,2,288,512]{4,3,2,1,0:T(8,128)(2,1)} %bitcast.340), custom_call_target="tpu_custom_call" | custom-call | flops 3261490688 | bytes 4246732 | tf_op jit(solution)/shard_map/pallas_call | solution.py:305
  102.6 13.3 %collective-permute-done.7.refs_3_.refs_10_ = bf16[272,1536]{1,0:T(8,128)(2,1)S(1)} collective-permute-done((bf16[272,1536]{1,0:T(8,128)(2,1)}, bf16[272,1536]{1,0:T(8,128)(2,1)S(1)}, u32[]{:S(2)}, u32[]{:S(2)}) %collective-permute-start.7) | collective-permute-done | bytes 835616 | tf_op jit(solution)/shard_map/ppermute | solution.py:246
  116.9 10.1 %shard_map.260 = (bf16[2,2,288,512]{3,2,1,0:T(8,128)(2,1)S(1)}, bf16[2,8,576,576]{3,2,1,0:T(8,128)(2,1)}) custom-call(bf16[3,2,2,288,512]{4,3,2,1,0:T(8,128)(2,1)} %bitcast.341, bf16[2,2,288,512]{3,2,1,0:T(8,128)(2,1)S(1)} %get-tuple-element.119.refs_1_, ...), custom_call_target="tpu_custom_call", output_to_operand_aliasing={{0}: (1, {}), {1}: (2, {})} | custom-call | flops 3261490688 | bytes 4246732 | tf_op jit(solution)/shard_map/pallas_call | solution.py:305
  142.1 17.1 %shard_map.262 = (bf16[2,2,288,512]{3,2,1,0:T(8,128)(2,1)S(1)}, bf16[2,8,576,576]{3,2,1,0:T(8,128)(2,1)}) custom-call(bf16[3,2,2,288,512]{4,3,2,1,0:T(8,128)(2,1)} %bitcast.361), custom_call_target="tpu_custom_call" | custom-call | flops 6522981376 | bytes 8493465 | tf_op jit(solution)/shard_map/pallas_call | solution.py:305
  159.3 7.5 %shard_map.263 = (f32[1152,1024]{1,0:T(8,128)}, bf16[1152,1024]{1,0:T(8,128)(2,1)S(1)}) custom-call(s32[6]{0:T(128)S(1)} %pad_add_fusion.refs_0_, bf16[1152,512]{1,0:T(8,128)(2,1)S(1)} %bitcast.311, bf16[1152,512]{1,0:T(8,128)(2,1)S(1)} %bitcast.321, bf16[1152,1024]{1,0:T(8,128)(2,1)S(1)} %copy-done.6, f32[1,1024]{1,0:T(1,128)S(1)} %get-tuple-element.127.refs_4_, ...), custom_call_target="tpu_custom_call" | custom-call | flops 1932735232 | bytes 11114905 | tf_op jit(solution)/shard_map/pallas_call | solution.py:305
  166.9 11.9 %shard_map.264 = (bf16[1152,2048]{1,0:T(8,128)(2,1)}, bf16[1152,2048]{1,0:T(8,128)(2,1)}) custom-call(s32[6]{0:T(128)S(1)} %pad_add_fusion.refs_0_, bf16[1152,1024]{1,0:T(8,128)(2,1)S(1)} %get-tuple-element.130.refs_1_.refs_0_, f32[1,2048]{1,0:T(1,128)S(1)} %bitcast.335, bf16[16,2,64,2560]{3,2,1,0:T(8,128)(2,1)S(1)} %bitcast.167, ...), custom_call_target="tpu_custom_call" | custom-call | flops 3865470464 | bytes 12792627 | tf_op jit(solution)/shard_map/pallas_call | solution.py:305
  184.6 12.0 %shard_map.266 = (bf16[1152,2048]{1,0:T(8,128)(2,1)}, bf16[1152,2048]{1,0:T(8,128)(2,1)}) custom-call(s32[6]{0:T(128)S(1)} %pad_add_fusion.refs_0_, bf16[1152,1024]{1,0:T(8,128)(2,1)S(1)} %get-tuple-element.130.refs_1_.refs_0_, f32[1,2048]{1,0:T(1,128)S(1)} %bitcast.334, bf16[16,2,64,2560]{3,2,1,0:T(8,128)(2,1)S(1)} %bitcast.198, ...), custom_call_target="tpu_custom_call" | custom-call | flops 3865470464 | bytes 12792627 | tf_op jit(solution)/shard_map/pallas_call | solution.py:305
  196.6 14.5 %shard_map.267 = (bf16[2,256,2048]{2,1,0:T(8,128)(2,1)}, bf16[2,256,2048]{2,1,0:T(8,128)(2,1)}, bf16[2,256,2048]{2,1,0:T(8,128)(2,1)}, bf16[2,256,2048]{2,1,0:T(8,128)(2,1)}) custom-call(bf16[1152,1024]{1,0:T(8,128)(2,1)S(1)} %get-tuple-element.133.refs_19_.refs_0_.refs_1_.refs_4_, bf16[1152,2048]{1,0:T(8,128)(2,1)} %get-tuple-element.131.refs_4_.refs_1_, ...), custom_call_target="tpu_custom_call" | custom-call | flops 5798205952 | bytes 12111052 | tf_op jit(solution)/shard_map/pallas_call | solution.py:305
  216.3 17.9 %shard_map.268 = (bf16[1152,2048]{1,0:T(8,128)(2,1)S(1)}, bf16[1152,2048]{1,0:T(8,128)(2,1)S(1)}, f32[1,2048]{1,0:T(1,128)S(1)}, f32[1,2048]{1,0:T(1,128)S(1)}) custom-call(s32[6]{0:T(128)S(1)} %pad_add_fusion.refs_0_, bf16[1152,1024]{1,0:T(8,128)(2,1)} %copy-done.8, bf16[1152,2048]{1,0:T(8,128)(2,1)} %get-tuple-element.138.refs_2_, ...), custom_call_target="tpu_custom_call" | custom-call | flops 5798205952 | bytes 19188940 | tf_op jit(solution)/shard_map/pallas_call | solution.py:305
  236.2 13.6 %shard_map.270 = (bf16[2,256,2048]{2,1,0:T(8,128)(2,1)}, bf16[2,256,2048]{2,1,0:T(8,128)(2,1)}, bf16[2,256,2048]{2,1,0:T(8,128)(2,1)}, bf16[2,256,2048]{2,1,0:T(8,128)(2,1)}) custom-call(bf16[1152,1024]{1,0:T(8,128)(2,1)S(1)} %copy-done.20, bf16[1152,2048]{1,0:T(8,128)(2,1)S(1)} %get-tuple-element.141.refs_2_.refs_1_, ...), custom_call_target="tpu_custom_call" | custom-call | flops 5798205952 | bytes 12111052 | tf_op jit(solution)/shard_map/pallas_call | solution.py:305
  254.0 23.5 %shard_map.271 = (f32[1152,1024]{1,0:T(8,128)}, bf16[1152,1024]{1,0:T(8,128)(2,1)S(1)}, bf16[1152,512]{1,0:T(8,128)(2,1)S(1)}, bf16[1152,512]{1,0:T(8,128)(2,1)S(1)}, f32[8,1024]{1,0:T(8,128)S(1)}) custom-call(s32[6]{0:T(128)S(1)} %pad_add_fusion.refs_0_, bf16[1152,2048]{1,0:T(8,128)(2,1)S(1)} %get-tuple-element.141.refs_2_.refs_1_, ...), custom_call_target="tpu_custom_call" | custom-call | flops 7247757312 | bytes 20604518 | tf_op jit(solution)/shard_map/pallas_call | solution.py:305
  282.2 20.3 %shard_map.273 = (bf16[3,2,2,288,512]{4,3,2,1,0:T(8,128)(2,1)S(1)}, f32[2,2,512]{2,1,0:T(2,128)S(1)}) custom-call(bf16[3,2,2,288,512]{4,3,2,1,0:T(8,128)(2,1)} %bitcast.362, bf16[2,2,288,512]{3,2,1,0:T(8,128)(2,1)S(1)} %bitcast.339, bf16[2,8,576,576]{3,2,1,0:T(8,128)(2,1)} %get-tuple-element.151.refs_2_, bf16[512,2048]{1,0:T(8,128)(2,1)S(1)} %copy-done.49), custom_call_target="tpu_custom_call" | custom-call | flops 6522981376 | bytes 6370099 | tf_op jit(solution)/shard_map/pallas_call | solution.py:305
  308.7 7.4 %shard_map.275 = (bf16[256,2048]{1,0:T(8,128)(2,1)}, bf16[256,2048]{1,0:T(8,128)(2,1)}, bf16[256,2048]{1,0:T(8,128)(2,1)}, bf16[256,2048]{1,0:T(8,128)(2,1)}) custom-call(bf16[1152,1024]{1,0:T(8,128)(2,1)S(1)} %copy-done.48, bf16[1152,1024]{1,0:T(8,128)(2,1)S(1)} %get-tuple-element.146.refs_2_.refs_1_, bf16[3,1152,512]{2,1,0:T(8,128)(2,1)S(1)} %bitcast.300, ...), custom_call_target="tpu_custom_call" | custom-call | flops 2899102976 | bytes 8178892 | tf_op jit(solution)/shard_map/pallas_call | solution.py:305
  319.9 9.1 %shard_map.276.refs_2_ = bf16[2,288,1024]{2,1,0:T(8,128)(2,1)S(1)} custom-call(s32[6]{0:T(128)S(1)} %pad_add_fusion.refs_0_, bf16[1152,2048]{1,0:T(8,128)(2,1)} %get-tuple-element.131.refs_4_.refs_1_, bf16[1152,2048]{1,0:T(8,128)(2,1)} %get-tuple-element.134.refs_2_, f32[1152,1024]{1,0:T(8,128)} %get-tuple-element.135.refs_3_, ...), custom_call_target="tpu_custom_call" | custom-call | flops 3623878656 | bytes 9987686 | tf_op jit(solution)/shard_map/pallas_call | solution.py:305
  334.6 20.3 %shard_map.279 = (bf16[3,2,2,288,512]{4,3,2,1,0:T(8,128)(2,1)S(1)}, f32[2,2,512]{2,1,0:T(2,128)S(1)}) custom-call(bf16[3,2,2,288,512]{4,3,2,1,0:T(8,128)(2,1)} %bitcast.342, bf16[2,2,288,512]{3,2,1,0:T(8,128)(2,1)S(1)} %bitcast.338, bf16[2,8,576,576]{3,2,1,0:T(8,128)(2,1)} %get-tuple-element.148.refs_2_, bf16[256,2048]{1,0:T(8,128)(2,1)S(1)} %copy-done.60), custom_call_target="tpu_custom_call" | custom-call | flops 6522981376 | bytes 6370099 | tf_op jit(solution)/shard_map/pallas_call | solution.py:305
  358.4 7.4 %shard_map.281 = (bf16[256,2048]{1,0:T(8,128)(2,1)}, bf16[256,2048]{1,0:T(8,128)(2,1)}, bf16[256,2048]{1,0:T(8,128)(2,1)}, bf16[256,2048]{1,0:T(8,128)(2,1)}) custom-call(bf16[1152,1024]{1,0:T(8,128)(2,1)S(1)} %copy-done.48, bf16[1152,1024]{1,0:T(8,128)(2,1)S(1)} %get-tuple-element.146.refs_2_.refs_1_, bf16[3,1152,512]{2,1,0:T(8,128)(2,1)S(1)} %bitcast.304, ...), custom_call_target="tpu_custom_call" | custom-call | flops 2899102976 | bytes 8178892 | tf_op jit(solution)/shard_map/pallas_call | solution.py:305
  384.6 10.8 %shard_map.284 = (bf16[2,288,1024]{2,1,0:T(8,128)(2,1)S(1)}, f32[8,1024]{1,0:T(8,128)S(1)}) custom-call(s32[6]{0:T(128)S(1)} %pad_add_fusion.refs_0_, bf16[3,1152,512]{2,1,0:T(8,128)(2,1)} %bitcast.305, bf16[3,1152,512]{2,1,0:T(8,128)(2,1)} %bitcast.301, bf16[1152,1024]{1,0:T(8,128)(2,1)} %get-tuple-element.126.refs_3_, ...), custom_call_target="tpu_custom_call" | custom-call | flops 1449551488 | bytes 4718592 | tf_op jit(solution)/shard_map/pallas_call | solution.py:305
  402.0 11.7 %shard_map.287 = (bf16[4,288,1024]{2,1,0:T(8,128)(2,1)}, f32[8,1024]{1,0:T(8,128)S(1)}) custom-call(s32[6]{0:T(128)S(1)} %pad_add_fusion.refs_0_, bf16[3,1152,512]{2,1,0:T(8,128)(2,1)} %bitcast.306, bf16[3,1152,512]{2,1,0:T(8,128)(2,1)} %bitcast.302, bf16[1152,1024]{1,0:T(8,128)(2,1)} %get-tuple-element.126.refs_3_, ...), custom_call_target="tpu_custom_call" | custom-call | flops 1449551488 | bytes 4718592 | tf_op jit(solution)/shard_map/pallas_call | solution.py:305
  449.4 10.1 %shard_map.290.refs_6_.refs_2_ = bf16[4,288,1024]{2,1,0:T(8,128)(2,1)} custom-call(s32[6]{0:T(128)S(1)} %pad_add_fusion.refs_0_, bf16[1152,2048]{1,0:T(8,128)(2,1)} %get-tuple-element.131.refs_4_.refs_1_, bf16[1152,2048]{1,0:T(8,128)(2,1)} %get-tuple-element.134.refs_2_, f32[1152,1024]{1,0:T(8,128)} %get-tuple-element.135.refs_3_, ...), custom_call_target="tpu_custom_call" | custom-call | flops 3623878656 | bytes 9987686 | tf_op jit(solution)/shard_map/pallas_call | solution.py:305
  465.0 6.8 %collective-permute-done.33.refs_4_ = bf16[80,2048]{1,0:T(8,128)(2,1)S(1)} collective-permute-done((bf16[80,2048]{1,0:T(8,128)(2,1)S(1)}, bf16[80,2048]{1,0:T(8,128)(2,1)S(1)}, u32[]{:S(2)}, u32[]{:S(2)}) %collective-permute-start.33) | collective-permute-done | bytes 327712 | tf_op jit(solution)/shard_map/ppermute | solution.py:246
  (355 shorter events, 178.0 us)
Async XLA Ops:
  7.3 122.5 %all-gather.5.cloned.1.call-start = ((), (), s32[]{:S(2)}) async-start(), calls=%async_computation | async-start | bytes 10813440 | tf_op jit(solution)/shard_map/all_gather | solution.py:985
  9.2 202.1 %all-gather.7.cloned.1.call-start = ((), (), s32[]{:S(2)}) async-start(), calls=%async_computation.1 | async-start | bytes 8650752 | tf_op jit(solution)/shard_map/all_gather | solution.py:1018
  15.3 23.7 %collective-permute-start.2 = (bf16[64,1536]{1,0:T(8,128)(2,1)S(1)}, bf16[64,1536]{1,0:T(8,128)(2,1)S(1)}, u32[]{:S(2)}, u32[]{:S(2)}) collective-permute-start(bf16[64,1536]{1,0:T(8,128)(2,1)S(1)} %bitcast.344), channel_id=1, source_target_pairs={{0,16},{2,18},{4,20},{6,22},{8,24},{10,26},{12,28},{14,30},{16,0},... | collective-permute-start | bytes 589832 | tf_op jit(solution)/shard_map/ppermute | solution.py:246
  15.3 24.4 %collective-permute-start.1 = (bf16[64,1536]{1,0:T(8,128)(2,1)S(1)}, bf16[64,1536]{1,0:T(8,128)(2,1)}, u32[]{:S(2)}, u32[]{:S(2)}) collective-permute-start(bf16[64,1536]{1,0:T(8,128)(2,1)S(1)} %bitcast.345), channel_id=1, source_target_pairs={{0,8},{2,10},{4,12},{6,14},{8,0},{10,2},{12,4},{14,6},{16,24},{18,... | collective-permute-start | bytes 589832 | tf_op jit(solution)/shard_map/ppermute | solution.py:246
  18.3 35.7 %collective-permute-start = (bf16[2,288,1024]{2,1,0:T(8,128)(2,1)}, bf16[2,288,1024]{2,1,0:T(8,128)(2,1)}, u32[]{:S(2)}, u32[]{:S(2)}) collective-permute-start(bf16[2,288,1024]{2,1,0:T(8,128)(2,1)} %constant_dynamic-slice_fusion.1), channel_id=1, source_target_pairs={{0,1},{1,0},{2,3},{3,2},{4,5},{5,4},{6,7},{7,6},{8,9},{9,8},{10,11... | collective-permute-start | bytes 3538952 | tf_op jit(solution)/shard_map/ppermute | solution.py:246
  40.9 34.3 %collective-permute-start.5 = (bf16[272,1536]{1,0:T(8,128)(2,1)S(1)}, bf16[272,1536]{1,0:T(8,128)(2,1)S(1)}, u32[]{:S(2)}, u32[]{:S(2)}) collective-permute-start(bf16[272,1536]{1,0:T(8,128)(2,1)S(1)} %pad_maximum_fusion.2), channel_id=1, source_target_pairs={{0,1},{1,0},{2,3},{3,2},{4,5},{5,4},{6,7},{7,6},{8,9},{9,8},{10,11... | collective-permute-start | bytes 2506760 | tf_op jit(solution)/shard_map/ppermute | solution.py:246
  77.7 38.2 %collective-permute-start.7 = (bf16[272,1536]{1,0:T(8,128)(2,1)}, bf16[272,1536]{1,0:T(8,128)(2,1)S(1)}, u32[]{:S(2)}, u32[]{:S(2)}) collective-permute-start(bf16[272,1536]{1,0:T(8,128)(2,1)} %copy-done.25), channel_id=1, source_target_pairs={{0,4},{2,6},{4,0},{6,2},{8,12},{10,14},{12,8},{14,10},{16,20},{18,... | collective-permute-start | bytes 2506760 | tf_op jit(solution)/shard_map/ppermute | solution.py:246
  132.9 45.9 %collective-permute-start.9 = (bf16[2,288,1024]{2,1,0:T(8,128)(2,1)}, bf16[2,288,1024]{2,1,0:T(8,128)(2,1)}, u32[]{:S(2)}, u32[]{:S(2)}) collective-permute-start(bf16[2,288,1024]{2,1,0:T(8,128)(2,1)} %constant_dynamic-slice_fusion), channel_id=1, source_target_pairs={{0,1},{1,0},{2,3},{3,2},{4,5},{5,4},{6,7},{7,6},{8,9},{9,8},{10,11... | collective-permute-start | bytes 3538952 | tf_op jit(solution)/shard_map/ppermute | solution.py:246
  211.1 23.2 %collective-permute-start.10 = (bf16[2,256,2048]{2,1,0:T(8,128)(2,1)}, bf16[2,256,2048]{2,1,0:T(8,128)(2,1)S(1)}, u32[]{:S(2)}, u32[]{:S(2)}) collective-permute-start(bf16[2,256,2048]{2,1,0:T(8,128)(2,1)} %get-tuple-element.144), channel_id=1, source_target_pairs={{0,2},{2,0},{4,6},{6,4},{8,10},{10,8},{12,14},{14,12},{16,18},{18,... | collective-permute-start | bytes 6291464 | tf_op jit(solution)/shard_map/ppermute | solution.py:246
  249.9 27.6 %collective-permute-start.11 = (bf16[2,256,2048]{2,1,0:T(8,128)(2,1)}, bf16[2,256,2048]{2,1,0:T(8,128)(2,1)}, u32[]{:S(2)}, u32[]{:S(2)}) collective-permute-start(bf16[2,256,2048]{2,1,0:T(8,128)(2,1)} %get-tuple-element.153), channel_id=1, source_target_pairs={{0,2},{2,0},{4,6},{6,4},{8,10},{10,8},{12,14},{14,12},{16,18},{18,... | collective-permute-start | bytes 6291464 | tf_op jit(solution)/shard_map/ppermute | solution.py:246
  250.2 52.4 %collective-permute-start.13 = (bf16[512,2048]{1,0:T(8,128)(2,1)}, bf16[512,2048]{1,0:T(8,128)(2,1)}, u32[]{:S(2)}, u32[]{:S(2)}) collective-permute-start(bf16[512,2048]{1,0:T(8,128)(2,1)} %shard_map.269.refs_3_), channel_id=1, source_target_pairs={{0,4},{2,6},{4,0},{6,2},{8,12},{10,14},{12,8},{14,10},{16,20},{18,... | collective-permute-start | bytes 6291464 | tf_op jit(solution)/shard_map/ppermute | solution.py:246
  280.6 49.7 %collective-permute-start.15 = (bf16[512,2048]{1,0:T(8,128)(2,1)}, bf16[512,2048]{1,0:T(8,128)(2,1)S(1)}, u32[]{:S(2)}, u32[]{:S(2)}) collective-permute-start(bf16[512,2048]{1,0:T(8,128)(2,1)} %shard_map.272.refs_3_), channel_id=1, source_target_pairs={{0,1},{1,0},{2,3},{3,2},{4,5},{5,4},{6,7},{7,6},{8,9},{9,8},{10,11... | collective-permute-start | bytes 6291464 | tf_op jit(solution)/shard_map/ppermute | solution.py:246
  316.7 38.2 %collective-permute-start.17 = (bf16[256,2048]{1,0:T(8,128)(2,1)S(1)}, bf16[256,2048]{1,0:T(8,128)(2,1)S(1)}, u32[]{:S(2)}, u32[]{:S(2)}) collective-permute-start(bf16[256,2048]{1,0:T(8,128)(2,1)S(1)} %copy-done.88), channel_id=1, source_target_pairs={{0,1},{1,0},{2,3},{3,2},{4,5},{5,4},{6,7},{7,6},{8,9},{9,8},{10,11... | collective-permute-start | bytes 3145736 | tf_op jit(solution)/shard_map/ppermute | solution.py:246
  333.1 38.4 %collective-permute-start.21 = (bf16[256,2048]{1,0:T(8,128)(2,1)}, bf16[256,2048]{1,0:T(8,128)(2,1)}, u32[]{:S(2)}, u32[]{:S(2)}) collective-permute-start(bf16[256,2048]{1,0:T(8,128)(2,1)} %shard_map.277.refs_3_), channel_id=1, source_target_pairs={{0,4},{2,6},{4,0},{6,2},{8,12},{10,14},{12,8},{14,10},{16,20},{18,... | collective-permute-start | bytes 3145736 | tf_op jit(solution)/shard_map/ppermute | solution.py:246
  366.1 32.1 %collective-permute-start.27 = (bf16[2,288,1024]{2,1,0:T(8,128)(2,1)S(1)}, bf16[2,288,1024]{2,1,0:T(8,128)(2,1)}, u32[]{:S(2)}, u32[]{:S(2)}) collective-permute-start(bf16[2,288,1024]{2,1,0:T(8,128)(2,1)S(1)} %shard_map.276.refs_2_), channel_id=1, source_target_pairs={{0,1},{1,0},{2,3},{3,2},{4,5},{5,4},{6,7},{7,6},{8,9},{9,8},{10,11... | collective-permute-start | bytes 3538952 | tf_op jit(solution)/shard_map/ppermute | solution.py:246
  367.0 28.5 %collective-permute-start.19 = (bf16[256,2048]{1,0:T(8,128)(2,1)}, bf16[256,2048]{1,0:T(8,128)(2,1)}, u32[]{:S(2)}, u32[]{:S(2)}) collective-permute-start(bf16[256,2048]{1,0:T(8,128)(2,1)} %get-tuple-element.170), channel_id=1, source_target_pairs={{0,4},{2,6},{4,0},{6,2},{8,12},{10,14},{12,8},{14,10},{16,20},{18,... | collective-permute-start | bytes 3145736 | tf_op jit(solution)/shard_map/ppermute | solution.py:246
  367.9 30.3 %collective-permute-start.26 = (bf16[128,2048]{1,0:T(8,128)(2,1)}, bf16[128,2048]{1,0:T(8,128)(2,1)}, u32[]{:S(2)}, u32[]{:S(2)}) collective-permute-start(bf16[128,2048]{1,0:T(8,128)(2,1)} %get-tuple-element.178), channel_id=1, source_target_pairs={{0,16},{2,18},{4,20},{6,22},{8,24},{10,26},{12,28},{14,30},{16,0},... | collective-permute-start | bytes 1572872 | tf_op jit(solution)/shard_map/ppermute | solution.py:246
  377.6 57.6 %collective-permute-start.24 = (bf16[256,2048]{1,0:T(8,128)(2,1)}, bf16[256,2048]{1,0:T(8,128)(2,1)}, u32[]{:S(2)}, u32[]{:S(2)}) collective-permute-start(bf16[256,2048]{1,0:T(8,128)(2,1)} %shard_map.282.refs_2_), channel_id=1, source_target_pairs={{0,1},{1,0},{2,3},{3,2},{4,5},{5,4},{6,7},{7,6},{8,9},{9,8},{10,11... | collective-permute-start | bytes 3145736 | tf_op jit(solution)/shard_map/ppermute | solution.py:246
  383.1 52.2 %collective-permute-start.23 = (bf16[256,2048]{1,0:T(8,128)(2,1)}, bf16[256,2048]{1,0:T(8,128)(2,1)}, u32[]{:S(2)}, u32[]{:S(2)}) collective-permute-start(bf16[256,2048]{1,0:T(8,128)(2,1)} %shard_map.283.refs_13_), channel_id=1, source_target_pairs={{0,4},{2,6},{4,0},{6,2},{8,12},{10,14},{12,8},{14,10},{16,20},{18,... | collective-permute-start | bytes 3145736 | tf_op jit(solution)/shard_map/ppermute | solution.py:246
  398.1 24.3 %collective-permute-start.25 = (bf16[128,2048]{1,0:T(8,128)(2,1)}, bf16[128,2048]{1,0:T(8,128)(2,1)}, u32[]{:S(2)}, u32[]{:S(2)}) collective-permute-start(bf16[128,2048]{1,0:T(8,128)(2,1)} %get-tuple-element.177), channel_id=1, source_target_pairs={{0,16},{2,18},{4,20},{6,22},{8,24},{10,26},{12,28},{14,30},{16,0},... | collective-permute-start | bytes 1572872 | tf_op jit(solution)/shard_map/ppermute | solution.py:246
  432.2 27.3 %collective-permute-start.35 = (bf16[64,2048]{1,0:T(8,128)(2,1)}, bf16[64,2048]{1,0:T(8,128)(2,1)S(1)}, u32[]{:S(2)}, u32[]{:S(2)}) collective-permute-start(bf16[64,2048]{1,0:T(8,128)(2,1)} %get-tuple-element.203), channel_id=1, source_target_pairs={{0,8},{2,10},{4,12},{6,14},{8,0},{10,2},{12,4},{14,6},{16,24},{18,... | collective-permute-start | bytes 786440 | tf_op jit(solution)/shard_map/ppermute | solution.py:246
  439.2 25.7 %collective-permute-start.31 = (bf16[2,288,1024]{2,1,0:T(8,128)(2,1)S(1)}, bf16[2,288,1024]{2,1,0:T(8,128)(2,1)S(1)}, u32[]{:S(2)}, u32[]{:S(2)}) collective-permute-start(bf16[2,288,1024]{2,1,0:T(8,128)(2,1)S(1)} %copy-done.57), channel_id=1, source_target_pairs={{0,1},{1,0},{2,3},{3,2},{4,5},{5,4},{6,7},{7,6},{8,9},{9,8},{10,11... | collective-permute-start | bytes 3538952 | tf_op jit(solution)/shard_map/ppermute | solution.py:246
  441.3 30.5 %collective-permute-start.32 = (bf16[144,2048]{1,0:T(8,128)(2,1)S(1)}, bf16[144,2048]{1,0:T(8,128)(2,1)S(1)}, u32[]{:S(2)}, u32[]{:S(2)}) collective-permute-start(bf16[144,2048]{1,0:T(8,128)(2,1)S(1)} %pad_maximum_fusion.4), channel_id=1, source_target_pairs={{0,8},{2,10},{4,12},{6,14},{8,0},{10,2},{12,4},{14,6},{16,24},{18,... | collective-permute-start | bytes 1769480 | tf_op jit(solution)/shard_map/ppermute | solution.py:246
  444.4 27.4 %collective-permute-start.33 = (bf16[80,2048]{1,0:T(8,128)(2,1)S(1)}, bf16[80,2048]{1,0:T(8,128)(2,1)S(1)}, u32[]{:S(2)}, u32[]{:S(2)}) collective-permute-start(bf16[80,2048]{1,0:T(8,128)(2,1)S(1)} %get-tuple-element.241), channel_id=1, source_target_pairs={{0,16},{2,18},{4,20},{6,22},{8,24},{10,26},{12,28},{14,30},{16,0},... | collective-permute-start | bytes 983048 | tf_op jit(solution)/shard_map/ppermute | solution.py:246
  (111 other events, 963.0 us)
Sparse Core Ops, SparseCore 0:
  11.6 118.1 all-gather.4
  132.8 78.4 all-gather.6
